TPU v7x, 256 devices: a whole 4x4x8 slice. The times are simulated.
256 devices in a mesh: blk: 32 (over z, x), uly: 8 (over y, core).
Axes of the slice: x: 4, y: 4, z: 8, core: 2. Of those that a mesh axis runs over, the one named last changes fastest.
Arguments:
- q_raw: bfloat16 [4608, 24, 128], P('blk', 'uly'), may hold values from -120 to 120
- k_raw: bfloat16 [4608, 24, 128], P('blk', 'uly'), may hold values from -120 to 120
- values: bfloat16 [4608, 24, 128], P('blk', 'uly'), may hold values from -6 to 6
- out_grad: bfloat16 [4608, 24, 128], P('blk', 'uly'), may hold values from -16 to 16
- q_gain: float32 [2, 128], replicated, may hold values from 0.5 to 6.5
- k_gain: float32 [2, 128], replicated, may hold values from 0.5 to 6.5
Outputs:
- q_grad: bfloat16 [4608, 24, 128], P('blk', 'uly')
- k_grad: bfloat16 [4608, 24, 128], P('blk', 'uly')
- v_grad: bfloat16 [4608, 24, 128], P('blk', 'uly')
- q_gain_grad: float32 [2, 128], replicated
- k_gain_grad: float32 [2, 128], replicated
All inputs are finite; a program needn't handle non-finite values.
Results may differ from a plain program's by a relative error of at most 0.009.
The roundings to bfloat16 on the way count: a program that leaves them out, or rounds other values in their place, can miss the bound.
Values may be sent and summed in bfloat16 or wider, within the bound.
No kernel may reach another device: no remote copies, remote signals or barrier semaphores. Data moves between devices by JAX's collectives and lax.ppermute only.
A program may use at most 64 MiB of HBM per device.

v0:
```python
import functools
import math

import jax
import jax.numpy as jnp
from jax import lax
from jax.sharding import Mesh
from jax.sharding import PartitionSpec as P

TXT = 512
BLK = ("blk_0", "blk_1")
BLK_ULY = ("blk_0", "blk_1", "uly_0", "uly_1")
ULY = ("uly_0", "uly_1")


epsilon = 1e-06
row_block = 576


def sent_together(arrays, axis, dim, along):
    both = jnp.concatenate(arrays, axis=along)
    out, at, gathered = (lax.all_gather(both, axis, axis=dim, tiled=True), 0, [])
    for a in arrays:
        gathered.append(lax.slice_in_dim(out, at, at + a.shape[along], axis=along))
        at += a.shape[along]
    return tuple(gathered)


def by_axis(array, axes):
    return functools.reduce(lax.psum, axes, array)


def block_length(row_total):
    length = min(row_total, row_block)
    while row_total % length:
        length -= 1
    return length


def over_blocks(update, state_now, arrays):
    row_total = arrays[0].shape[0]
    length = block_length(row_total)
    stacked = tuple(
        (member.reshape((row_total // length, length) + member.shape[1:]) for member in arrays)
    )

    def advance(carried, sliced):
        return (update(carried, sliced), None)

    final_state, unused = lax.scan(advance, state_now, stacked)
    return final_state


def gain_rows(gain, position):
    return jnp.where((position < TXT)[:, None], gain[0][None, :], gain[1][None, :])


def normalize(raw, gains):
    widened = raw.astype(jnp.float32)
    root_mean = jnp.sqrt(jnp.mean(widened * widened, axis=-1, keepdims=True) + epsilon)
    unit = widened / root_mean
    return (unit, root_mean, (unit * gains[:, None, :]).astype(jnp.bfloat16))


def norm_back(grad_norm, unit, root_mean, gains):
    grad_unit = grad_norm * gains[:, None, :]
    return (grad_unit - unit * jnp.mean(grad_unit * unit, axis=-1, keepdims=True)) / root_mean


def gain_parts(grad_norm, unit, position):
    per_row = jnp.sum(grad_norm * unit, axis=1)
    text_rows = (position < TXT)[:, None]
    return jnp.stack(
        [
            jnp.sum(jnp.where(text_rows, per_row, 0.0), axis=0),
            jnp.sum(jnp.where(text_rows, 0.0, per_row), axis=0),
        ]
    )


def scores(query_block, key_block, factor):
    return (
        jnp.einsum("qhc,khc->qhk", query_block, key_block, preferred_element_type=jnp.float32)
        * factor
    )


def make_stat_fold(queries, factor):

    def stat_update(carried, sliced):
        running, totals, attn_sum = carried
        key_block, value_block = sliced
        block_scores = scores(queries, key_block, factor)
        new_max = jnp.maximum(running, jnp.max(block_scores, axis=-1))
        rescale = jnp.exp(running - new_max)
        weights = jnp.exp(block_scores - new_max[..., None])
        totals = totals * rescale + jnp.sum(weights, axis=-1)
        attn_sum = attn_sum * rescale[..., None] + jnp.einsum(
            "qhk,khc->qhc",
            weights,
            value_block.astype(jnp.float32),
            precision=lax.Precision.HIGHEST,
            preferred_element_type=jnp.float32,
        )
        return (new_max, totals, attn_sum)

    def stat_fold(carried, visiting, offset):
        return over_blocks(stat_update, carried, visiting)

    return stat_fold


def make_kv_fold(all_logs, all_dots, key_rows, value_rows, factor):

    def kv_update(carried, sliced):
        grad_keys, grad_values = carried
        query_block, grad_block, log_block, dot_block = sliced
        probs = jnp.exp(scores(query_block, key_rows, factor) - log_block[..., None])
        grad_probs = jnp.einsum(
            "qhc,khc->qhk", grad_block, value_rows, preferred_element_type=jnp.float32
        )
        grad_scores = (probs * (grad_probs - dot_block[..., None])).astype(jnp.bfloat16)
        grad_keys = grad_keys + factor * jnp.einsum(
            "qhk,qhc->khc", grad_scores, query_block, preferred_element_type=jnp.float32
        )
        grad_values = grad_values + jnp.einsum(
            "qhk,qhc->khc",
            probs.astype(jnp.bfloat16),
            grad_block,
            preferred_element_type=jnp.float32,
        )
        return (grad_keys, grad_values)

    def kv_fold(carried, visiting, offset):
        return over_blocks(kv_update, carried, (visiting[0], visiting[1], all_logs, all_dots))

    return kv_fold


def local(q_raw, k_raw, values, out_grad, q_gain, k_gain):
    tok_rows = q_raw.shape[0]
    factor = 1.0 / math.sqrt(q_raw.shape[2])
    position = lax.axis_index(BLK) * tok_rows + jnp.arange(tok_rows, dtype=jnp.int32)
    q_gains = gain_rows(q_gain, position)
    k_gains = gain_rows(k_gain, position)
    q_unit, q_root, queries = normalize(q_raw, q_gains)
    k_unit, k_root, key_rows = normalize(k_raw, k_gains)
    stat_shape = (tok_rows, queries.shape[1])
    zeros_rows = jnp.zeros(stat_shape, jnp.float32)
    zeros_full = jnp.zeros(queries.shape, jnp.float32)
    start_max = jnp.full(stat_shape, -jnp.inf, jnp.float32)
    running, totals, attn_sum = make_stat_fold(queries, factor)(
        (start_max, zeros_rows, zeros_full),
        sent_together((key_rows, values), BLK, 0, 1),
        jnp.int32(0),
    )
    log_total = running + jnp.log(totals)
    row_dot = jnp.sum(out_grad.astype(jnp.float32) * (attn_sum / totals[..., None]), axis=-1)

    def grad_update(carried, sliced):
        weighted_grad, weighted_keys = carried
        key_block, value_block = sliced
        probs = jnp.exp(scores(queries, key_block, factor) - log_total[..., None])
        grad_probs = jnp.einsum(
            "qhc,khc->qhk", out_grad, value_block, preferred_element_type=jnp.float32
        )
        weighted_grad = weighted_grad + jnp.einsum(
            "qhk,khc->qhc",
            (probs * grad_probs).astype(jnp.bfloat16),
            key_block,
            preferred_element_type=jnp.float32,
        )
        weighted_keys = weighted_keys + jnp.einsum(
            "qhk,khc->qhc",
            probs.astype(jnp.bfloat16),
            key_block,
            preferred_element_type=jnp.float32,
        )
        return (weighted_grad, weighted_keys)

    weighted_grad, weighted_keys = over_blocks(
        grad_update, (zeros_full, zeros_full), sent_together((key_rows, values), BLK, 0, 1)
    )
    grad_queries = factor * (weighted_grad - row_dot[..., None] * weighted_keys)
    all_logs, all_dots = sent_together((log_total, row_dot), BLK, 0, 1)
    grad_keys, grad_values = make_kv_fold(all_logs, all_dots, key_rows, values, factor)(
        (zeros_full, zeros_full), sent_together((queries, out_grad), BLK, 0, 1), jnp.int32(0)
    )
    q_result = norm_back(grad_queries, q_unit, q_root, q_gains).astype(jnp.bfloat16)
    k_result = norm_back(grad_keys, k_unit, k_root, k_gains).astype(jnp.bfloat16)
    v_result = grad_values.astype(jnp.bfloat16)
    q_part = gain_parts(grad_queries, q_unit, position)
    k_part = gain_parts(grad_keys, k_unit, position)
    q_total, k_total = (by_axis(q_part, BLK_ULY), by_axis(k_part, BLK_ULY))
    return (q_result, k_result, v_result, q_total, k_total)


def solution(mesh):
    torus = Mesh(mesh.devices.reshape(8, 4, 4, 2), ("blk_0", "blk_1", "uly_0", "uly_1"))
    placed = (P(BLK, ULY, None), P(BLK, ULY, None), P(BLK, ULY, None), P(BLK, ULY, None), P(), P())
    return jax.shard_map(
        local,
        mesh=torus,
        in_specs=placed,
        out_specs=(P(BLK, ULY, None), P(BLK, ULY, None), P(BLK, ULY, None), P(), P()),
        check_vma=False,
    )
```

profile of v0, /device:TPU:32, one launch (start us, length us, event | category | flops | bytes accessed | tf_op | source)
XLA Modules:
  0.0 319.3 jit_solution(9018746482859978979)
XLA Ops:
  13.1 92.6 %all-gather.4.cloned.1.call-done = bf16[4608,6,128]{2,0,1:T(8,128)(2,1)} async-done(((bf16[144,6,128]{2,0,1:T(8,128)(2,1)}), bf16[4608,6,128]{2,0,1:T(8,128)(2,1)}) %all-gather.4.cloned.1.call-update) | async-done | bytes 7077904 | tf_op jit(solution)/shard_map/all_gather | solution.py:22
  105.8 3.5 %fusion.66 = (bf16[4608,3,128]{2,0,1:T(8,128)(2,1)S(1)}, bf16[4608,3,128]{2,0,1:T(8,128)(2,1)S(1)}) fusion(bf16[4608,6,128]{2,0,1:T(8,128)(2,1)} %all-gather.4.cloned.1.call-done), kind=kLoop, calls=%fused_computation.113 | loop fusion | bytes 14155776 | tf_op jit(solution)/shard_map/slice | solution.py:24
  109.3 2.1 copy.28
  111.4 2.1 copy.27
  113.5 30.4 %while.41 = (s32[]{:T(128)}, f32[144,3]{0,1:T(4,128)S(1)}, f32[144,3]{0,1:T(4,128)S(1)}, f32[144,3,128]{2,0,1:T(8,128)S(1)}, bf16[8,576,3,128]{3,1,2,0:T(8,128)(...) while((s32[]{:T(128)}, f32[144,3]{0,1:T(4,128)S(1)}, ...), condition=%wide.region_5.6_spmd.clone, body=%wide.region_2.5_spmd.clone.sunk | while | flops 447319168 | bytes 4451449 | solution.py:50
  115.4 1.9 fusion.104
  119.2 1.9 fusion.104
  123.0 1.9 fusion.104
  126.8 1.9 fusion.104
  130.6 1.9 fusion.104
  134.4 1.9 fusion.104
  138.2 1.9 fusion.104
  142.0 1.9 fusion.104
  144.2 47.3 %all-gather = f32[32,144,6]{1,2,0:T(8,128)S(1)} all-gather(f32[1,144,6]{1,2,0:T(8,128)S(1)} %maximum_bitcast_fusion), channel_id=1, replica_groups=mesh['blk_0'=8,'blk_1'=4,'uly_0'=4,'uly_1'=2] {'blk_0','blk_1'}, dimensions={0}, use_global_device_ids=true | all-gather | bytes 114048 | tf_op jit(solution)/shard_map/all_gather | solution.py:22
  192.0 35.7 %while.42 = (s32[]{:T(128)}, f32[144,3,128]{2,0,1:T(8,128)S(1)}, f32[144,3,128]{2,0,1:T(8,128)S(1)}, bf16[8,576,3,128]{3,1,2,0:T(8,128)(2,1)}, bf16[144,3,128]{2...) while((s32[]{:T(128)}, f32[144,3,128]{2,0,1:T(8,128)S(1)}, ...), condition=%wide.region_7.8_spmd.clone, body=%wide.region_6.7_spmd.clone.sunk | while | flops 256269312 | bytes 5864767 | solution.py:50
  193.4 1.7 fusion.113
  202.3 1.7 fusion.113
  206.8 1.7 fusion.113
  228.1 6.5 %fusion.65 = (bf16[4608,3,128]{2,0,1:T(8,128)(2,1)}, bf16[4608,3,128]{2,0,1:T(8,128)(2,1)}) fusion(bf16[4608,6,128]{2,0,1:T(8,128)(2,1)} %all-gather.6.cloned.1.call-done), kind=kLoop, calls=%fused_computation.112 | loop fusion | bytes 14155776 | tf_op jit(solution)/shard_map/slice | solution.py:24
  234.7 36.3 %while.43 = (s32[]{:T(128)}, f32[144,3,128]{2,0,1:T(8,128)S(1)}, f32[144,3,128]{2,0,1:T(8,128)S(1)}, bf16[8,576,3,128]{3,1,0,2:T(8,128)(2,1)}, bf16[144,3,128]{2...) while((s32[]{:T(128)}, f32[144,3,128]{2,0,1:T(8,128)S(1)}, ...), condition=%wide.region_11.12_spmd.clone, body=%wide.region_10.11_spmd.clone.sunk | while | flops 256573440 | bytes 5932171 | solution.py:50
  236.1 1.7 fusion.123
  240.6 1.7 fusion.123
  245.2 1.7 fusion.123
  249.7 1.7 fusion.123
  254.3 1.7 fusion.123
  258.8 1.7 fusion.123
  263.3 1.7 fusion.123
  267.9 1.7 fusion.123
  273.8 15.5 %all-reduce = (f32[2,128]{1,0:T(2,128)S(1)}, f32[2,128]{1,0:T(2,128)S(1)}) all-reduce(f32[2,128]{1,0:T(2,128)S(1)} %pad_maximum_fusion.2, f32[2,128]{1,0:T(2,128)S(1)} %pad_maximum_fusion.3), channel_id=1, replica_groups=mesh['blk_0'=8,'blk_1'=4,'uly_0'=4,'uly_1'=2] {'blk_0'}, use_global_device_ids=true, to_apply=%region_16.17 | all-reduce | flops 512 | bytes 4096 | tf_op jit(solution)/shard_map/psum | solution.py:30
  289.3 9.7 %all-reduce.2 = (f32[2,128]{1,0:T(2,128)S(1)}, f32[2,128]{1,0:T(2,128)S(1)}) all-reduce(f32[2,128]{1,0:T(2,128)S(1)} %get-tuple-element.353, f32[2,128]{1,0:T(2,128)S(1)} %get-tuple-element.354), channel_id=1, replica_groups=mesh['blk_0'=8,'blk_1'=4,'uly_0'=4,'uly_1'=2] {'blk_1'}, use_global_device_ids=true, to_apply=%region_17.18 | all-reduce | flops 512 | bytes 4096 | tf_op jit(solution)/shard_map/psum | solution.py:30
  299.0 10.4 %all-reduce.1 = (f32[2,128]{1,0:T(2,128)S(1)}, f32[2,128]{1,0:T(2,128)S(1)}) all-reduce(f32[2,128]{1,0:T(2,128)S(1)} %get-tuple-element.357, f32[2,128]{1,0:T(2,128)S(1)} %get-tuple-element.358), channel_id=1, replica_groups=mesh['blk_0'=8,'blk_1'=4,'uly_0'=4,'uly_1'=2] {'uly_0'}, use_global_device_ids=true, to_apply=%region_18.19 | all-reduce | flops 512 | bytes 4096 | tf_op jit(solution)/shard_map/psum | solution.py:30
  309.4 3.0 all-reduce.3
  (150 shorter events, 77.5 us)
Async XLA Ops:
  7.2 4.8 %copy-start.3 = (bf16[144,3,128]{2,0,1:T(8,128)(2,1)S(1)}, bf16[144,3,128]{2,0,1:T(8,128)(2,1)}, u32[]{:S(2)}) copy-start(bf16[144,3,128]{2,0,1:T(8,128)(2,1)} %param.12) | copy-start | bytes 331780
  7.2 5.1 %copy-start = (bf16[144,3,128]{2,0,1:T(8,128)(2,1)S(1)}, bf16[144,3,128]{2,0,1:T(8,128)(2,1)}, u32[]{:S(2)}) copy-start(bf16[144,3,128]{2,0,1:T(8,128)(2,1)} %param.15) | copy-start | bytes 331780
  7.2 98.6 %all-gather.4.cloned.1.call-start = ((), (), s32[]{:S(2)}) async-start(), calls=%async_computation | async-start | bytes 7299072 | tf_op jit(solution)/shard_map/all_gather | solution.py:22
  11.9 216.2 %all-gather.6.cloned.1.call-start = ((), (), s32[]{:S(2)}) async-start(), calls=%async_computation.1 | async-start | bytes 7299072 | tf_op jit(solution)/shard_map/all_gather | solution.py:22
  228.1 6.5 %copy-start.1 = (bf16[144,3,128]{2,0,1:T(8,128)(2,1)S(1)}, bf16[144,3,128]{2,0,1:T(8,128)(2,1)}, u32[]{:S(2)}) copy-start(bf16[144,3,128]{2,0,1:T(8,128)(2,1)} %param.14) | copy-start | bytes 331780
  234.6 36.3 %copy-start.2 = (bf16[144,3,128]{2,0,1:T(8,128)(2,1)S(1)}, bf16[144,3,128]{2,0,1:T(8,128)(2,1)}, u32[]{:S(2)}) copy-start(bf16[144,3,128]{2,0,1:T(8,128)(2,1)} %param.13) | copy-start | bytes 331780
Sparse Core Ops, SparseCore 0:
  12.0 93.6 all-gather.3
  108.5 90.2 all-gather.5
where the time goes:
time: 324 us; the launch traced here: 319 us
  matrix products  97.6 us (30%)
  waiting for transfers between devices  92.7 us (29%)
  blocking collectives  86 us (27%)
  local copies, waits for them, and re-layouts  15.6 us (5%)
  between operations  14.3 us (4%)
  other arithmetic  11.9 us (4%)
    all_gather x2, waiting for transfers between devices, sent_together(): lax.all_gather(both, axis, axis=dim, tiled=True)  92.6 us
    all_gather x1, blocking collectives, sent_together(): lax.all_gather(both, axis, axis=dim, tiled=True)  47.3 us
    psum x4, blocking collectives, by_axis(): return functools.reduce(lax.psum, axes, array)  38.7 us
    dot_general x24, matrix products, scores(): jnp.einsum('qhc,khc->qhk', query_block, key_block, preferred_element_type...  33.6 us
    dot_general x8, matrix products, stat_update(): jnp.einsum('qhk,khc->qhc', weights, value_block.astype(jnp.float32), prec...  14.9 us
    dot_general x8, matrix products, kv_update(): jnp.einsum('qhk,qhc->khc', grad_scores, query_block, preferred_element_ty...  13.7 us
    dot_general x8, matrix products, grad_update(): jnp.einsum('qhk,khc->qhc', (probs * grad_probs).astype(jnp.bfloat16), key...  13.5 us
    dot_general x8, matrix products, kv_update(): jnp.einsum('qhk,qhc->khc', probs.astype(jnp.bfloat16), grad_block, prefer...  11 us
  transfers between devices with their start and end apart: 2, of which 1 were waited for; matrix products, arithmetic and copies ran while one was open for 24% of the time, Pallas kernels for 0%

commit v1 on v0

v1 whole, which is shorter than its diff:
```python
import functools
import math

import jax
import jax.numpy as jnp
from jax import lax
from jax.experimental import pallas as pl
from jax.experimental.pallas import tpu as pltpu
from jax.sharding import Mesh
from jax.sharding import PartitionSpec as P

TXT = 512
EPS = 1e-06
NH, HD, BR = 3, 128, 144
NQ, NX, NZ = 4, 4, 2
QR = NQ * BR
KC = NZ * BR
KR = NX * KC
FACTOR = 1.0 / math.sqrt(HD)
SCALE2 = FACTOR * math.log2(math.e)
F32, BF16 = jnp.float32, jnp.bfloat16
ALL_ROWS = ("zq", "zk", "x")


def nt_dot(a, b):
    return lax.dot_general(a, b, (((1,), (1,)), ((), ())), preferred_element_type=F32)


def nn_dot(a, b):
    return lax.dot_general(a, b, (((1,), (0,)), ((), ())), preferred_element_type=F32)


def tn_dot(a, b):
    return lax.dot_general(a, b, (((0,), (0,)), ((), ())), preferred_element_type=F32)


def text_mask(block):
    row = block * BR + lax.broadcasted_iota(jnp.int32, (BR, 1), 0)
    return row < TXT


def unit_and_root(raw):
    wide = raw.astype(F32)
    root = jnp.sqrt(jnp.mean(wide * wide, axis=-1, keepdims=True) + EPS)
    return wide / root, root


def gain_of(mask, gain_ref):
    return jnp.where(mask, gain_ref[0:1, :], gain_ref[1:2, :])


def here():
    return lax.axis_index("zq"), lax.axis_index("zk"), lax.axis_index("x")


def q_block(slot, place):
    zq, zk, x = place
    return (2 * lax.rem(zq + slot, NQ) + zk) * NX + x


def kv_block(xslot, j, place):
    zq, zk, x = place
    return (2 * zq + (zk + j - 2 * zk * j)) * NX + lax.rem(x + xslot, NX)


def q_offset(slot, place):
    return pl.multiple_of(lax.rem(place[0] + slot, NQ) * BR, 16)


def stat_kernel(*refs):
    q_refs, kv_refs = refs[:NQ], refs[NQ : NQ + NX * NZ]
    gq_ref, gk_ref, stat_ref, qn_ref, kn_ref, v_ref, do_ref = refs[NQ + NX * NZ :]
    place = here()
    for slot in range(NQ):
        gain = gain_of(text_mask(q_block(slot, place)), gq_ref)
        rows = pl.ds(q_offset(slot, place), BR)
        for h in range(NH):
            unit, _ = unit_and_root(q_refs[slot][0, h])
            qn_ref[h, rows, :] = (unit * gain).astype(BF16)
            do_ref[h, rows, :] = q_refs[slot][1, h]
    for k in range(NX):
        for j in range(NZ):
            ref = kv_refs[k * NZ + j]
            gain = gain_of(text_mask(kv_block(k, j, place)), gk_ref)
            rows = pl.ds(k * KC + j * BR, BR)
            for h in range(NH):
                unit, _ = unit_and_root(ref[0, h])
                kn_ref[h, rows, :] = (unit * gain).astype(BF16)
                v_ref[h, rows, :] = ref[1, h]
    stat_ref[...] = jnp.zeros_like(stat_ref)
    for h in range(NH):
        top = total = dot = None
        for k in range(NX):
            rows = pl.ds(k * KC, KC)
            s = nt_dot(kn_ref[h, rows, :], qn_ref[h]) * SCALE2
            g = nt_dot(v_ref[h, rows, :], do_ref[h])
            peak = jnp.max(s, axis=0, keepdims=True)
            new = peak if top is None else jnp.maximum(top, peak)
            w = jnp.exp2(s - new)
            part = jnp.sum(w, axis=0, keepdims=True)
            dpart = jnp.sum(w * g, axis=0, keepdims=True)
            if top is None:
                total, dot = part, dpart
            else:
                keep = jnp.exp2(top - new)
                total, dot = total * keep + part, dot * keep + dpart
            top = new
        stat_ref[3 * h : 3 * h + 1, :] = top
        stat_ref[3 * h + 1 : 3 * h + 2, :] = total
        stat_ref[3 * h + 2 : 3 * h + 3, :] = dot


def grad_kernel(*refs):
    s_refs, q_refs = refs[:NQ], refs[NQ : 2 * NQ]
    kv_refs = refs[2 * NQ : 2 * NQ + NX * NZ]
    (gq_ref, gk_ref, qn_ref, kn_ref, v_ref, do_ref,
     dq_own, dq1, dq2, dq3, kv_own, kv1, kv2, kv3, gain_ref, dq_all) = refs[2 * NQ + NX * NZ :]
    place = here()
    kv_outs, dq_outs = (kv_own, kv1, kv2, kv3), (dq_own, dq1, dq2, dq3)
    k_text = jnp.zeros((1, HD), F32)
    k_all = jnp.zeros((1, HD), F32)
    q_text = jnp.zeros((1, HD), F32)
    q_all = jnp.zeros((1, HD), F32)
    for h in range(NH):
        tops = [r[3 * h : 3 * h + 1, :] for r in s_refs]
        top = functools.reduce(jnp.maximum, tops)
        shares = [jnp.exp2(t - top) for t in tops]
        total = sum(r[3 * h + 1 : 3 * h + 2, :] * e for r, e in zip(s_refs, shares))
        row_dot = sum(r[3 * h + 2 : 3 * h + 3, :] * e for r, e in zip(s_refs, shares)) / total
        log_total = top + jnp.log2(total)
        wg = wk = None
        for k in range(NX):
            rows = pl.ds(k * KC, KC)
            kn = kn_ref[h, rows, :]
            s = nt_dot(kn, qn_ref[h]) * SCALE2
            g = nt_dot(v_ref[h, rows, :], do_ref[h])
            p = jnp.exp2(s - log_total)
            low = p.astype(BF16)
            mixed = (p * g).astype(BF16)
            gs = (p * (g - row_dot)).astype(BF16)
            dv = nn_dot(low, do_ref[h])
            dk = nn_dot(gs, qn_ref[h]) * FACTOR
            a, b = tn_dot(mixed, kn), tn_dot(low, kn)
            wg, wk = (a, b) if wg is None else (wg + a, wk + b)
            for j in range(NZ):
                part = dk[j * BR : (j + 1) * BR]
                kv_outs[k][j, 0, h] = part.astype(kv_outs[k].dtype)
                kv_outs[k][j, 1, h] = dv[j * BR : (j + 1) * BR].astype(kv_outs[k].dtype)
                unit, _ = unit_and_root(kv_refs[k * NZ + j][0, h])
                term = part * unit
                k_all += jnp.sum(term, axis=0, keepdims=True)
                k_text += jnp.sum(jnp.where(text_mask(kv_block(k, j, place)), term, 0.0), axis=0, keepdims=True)
        column = jnp.transpose(jnp.broadcast_to(row_dot, (HD, QR)), (1, 0))
        dq_all[...] = (wg - column * wk) * FACTOR
        for slot in range(NQ):
            part = dq_all[pl.ds(q_offset(slot, place), BR), :]
            dq_outs[slot][h] = part.astype(dq_outs[slot].dtype)
            unit, _ = unit_and_root(q_refs[slot][0, h])
            term = part * unit
            q_all += jnp.sum(term, axis=0, keepdims=True)
            q_text += jnp.sum(jnp.where(text_mask(q_block(slot, place)), term, 0.0), axis=0, keepdims=True)
    gain_ref[...] = jnp.concatenate(
        [q_text, q_all - q_text, k_text, k_all - k_text, jnp.zeros((4, HD), F32)], axis=0
    )


def pair_sum_kernel(own, r1, r2, r3, keep_ref, send_ref):
    def total(j):
        return own[j] + r1[j].astype(F32) + r2[j].astype(F32) + r3[j].astype(F32)

    send_ref[...] = total(1).astype(BF16)
    keep_ref[...] = total(0)


def back(grad, raw, gain):
    unit, root = unit_and_root(raw)
    grad = grad * gain
    return (grad - unit * jnp.mean(grad * unit, axis=-1, keepdims=True)) / root


def q_out_kernel(own, r1, r2, r3, raw, gain_ref, out):
    gain = gain_of(text_mask(q_block(0, here())), gain_ref)
    for h in range(NH):
        grad = own[h] + r1[h].astype(F32) + r2[h].astype(F32) + r3[h].astype(F32)
        out[h] = back(grad, raw[0, h], gain).astype(BF16)


def kv_out_kernel(keep, got, raw, gain_ref, k_out, v_out):
    gain = gain_of(text_mask(q_block(0, here())), gain_ref)
    for h in range(NH):
        k_out[h] = back(keep[0, h] + got[0, h].astype(F32), raw[0, h], gain).astype(BF16)
        v_out[h] = (keep[1, h] + got[1, h].astype(F32)).astype(BF16)


def kernel_call(kernel, outs, args, scratch=(), flops=0):
    whole = pl.BlockSpec(memory_space=pltpu.VMEM)
    size = sum(a.size * a.dtype.itemsize for a in args)
    return pl.pallas_call(
        kernel,
        out_shape=[jax.ShapeDtypeStruct(s, d) for s, d in outs],
        in_specs=[whole] * len(args),
        out_specs=[whole] * len(outs),
        scratch_shapes=list(scratch),
        compiler_params=pltpu.CompilerParams(vmem_limit_bytes=48 * 1024 * 1024),
        cost_estimate=pl.CostEstimate(flops=flops, bytes_accessed=size, transcendentals=0),
    )(*args)


def fetch(a, axis, n, k):
    return lax.ppermute(a, axis, [((i + k) % n, i) for i in range(n)])


def give(a, axis, n, k):
    return lax.ppermute(a, axis, [(i, (i + k) % n) for i in range(n)])


def summed(a, axis, n):
    terms = [a] + [lax.ppermute(a, axis, [(i, i ^ k) for i in range(n)]) for k in range(1, n)]
    while len(terms) > 1:
        terms = [terms[i] + terms[i + 1] for i in range(0, len(terms), 2)]
    return terms[0]


def local(q_raw, k_raw, values, out_grad, q_gain, k_gain):
    def heads_first(a):
        return jnp.transpose(a, (1, 0, 2))

    kv = jnp.stack([heads_first(k_raw), heads_first(values)])
    qd = jnp.stack([heads_first(q_raw), heads_first(out_grad)])
    kv_pair = fetch(kv, "zk", NZ, 1)
    kvs = [kv, kv_pair]
    for k in range(1, NX):
        kvs += [fetch(kv, "x", NX, k), fetch(kv_pair, "x", NX, k)]
    qds = [qd] + [fetch(qd, "zq", NQ, k) for k in range(1, NQ)]
    tile = NH * QR * KR * HD * 2
    stat, qn, kn, v, do = kernel_call(
        stat_kernel,
        [((16, QR), F32), ((NH, QR, HD), BF16), ((NH, KR, HD), BF16), ((NH, KR, HD), BF16), ((NH, QR, HD), BF16)],
        [*qds, *kvs, q_gain, k_gain],
        flops=2 * tile,
    )
    stats = [stat] + [fetch(stat, "zq", NQ, k) for k in range(1, NQ)]
    part = (NH, BR, HD)
    kv_part = (NZ, 2, NH, BR, HD)
    dq0, dq1, dq2, dq3, kv0, kv1, kv2, kv3, gains = kernel_call(
        grad_kernel,
        [(part, F32)] + [(part, BF16)] * 3 + [(kv_part, F32)] + [(kv_part, BF16)] * 3 + [((8, HD), F32)],
        [*stats, *qds, *kvs, q_gain, k_gain, qn, kn, v, do],
        scratch=[pltpu.VMEM((QR, HD), F32)],
        flops=6 * tile,
    )
    kv_got = [give(a, "x", NX, k) for k, a in ((1, kv1), (2, kv2), (3, kv3))]
    dq_got = [give(a, "zq", NQ, k) for k, a in ((1, dq1), (2, dq2), (3, dq3))]
    gains = summed(gains, "core", 2)
    gains = summed(gains, "y", 4)
    gains = summed(gains, "x", NX)
    gains = summed(gains, "zk", NZ)
    gains = summed(gains, "zq", NQ)
    keep, send = kernel_call(
        pair_sum_kernel, [((2, NH, BR, HD), F32), ((2, NH, BR, HD), BF16)], [kv0, *kv_got]
    )
    got = fetch(send, "zk", NZ, 1)
    (q_out,) = kernel_call(q_out_kernel, [(part, BF16)], [dq0, *dq_got, qd, q_gain])
    k_out, v_out = kernel_call(kv_out_kernel, [(part, BF16)] * 2, [keep, got, kv, k_gain])

    return (
        heads_first(q_out), heads_first(k_out), heads_first(v_out), gains[0:2], gains[2:4],
    )


def solution(mesh):
    torus = Mesh(mesh.devices.reshape(4, 2, 4, 4, 2), ("zq", "zk", "x", "y", "core"))
    placed = P(ALL_ROWS, ("y", "core"), None)
    return jax.shard_map(
        local,
        mesh=torus,
        in_specs=(placed,) * 4 + (P(), P()),
        out_specs=(placed,) * 3 + (P(), P()),
        check_vma=False,
    )
```

time: 324 us -> 126 us (0.39)
  matrix products: 97.6 us -> 0 us
  blocking collectives: 86 us -> 0 us
  starting transfers between devices: 0.08 us -> 57.7 us
  waiting for transfers between devices: 92.7 us -> 42.5 us
  Pallas kernels: 0 us -> 18.4 us
  between operations: 14.3 us -> 0.75 us
  local copies, waits for them, and re-layouts: 15.6 us -> 3.59 us
  other arithmetic: 11.9 us -> 1.06 us
    dot_general x64 -> x0, matrix products: 97.6 us -> none  [the longest x24 33.6 us: scores(): jnp.einsum('qhc,khc->qhk', query_block, key_block, preferred_element_type...]
    all_gather x2 -> x0, waiting for transfers between devices: 92.6 us -> none  [sent_together(): lax.all_gather(both, axis, axis=dim, tiled=True)]
    ppermute x0 -> x31, starting transfers between devices: none -> 57.7 us  [the longest x14 31.6 us: fetch(): return lax.ppermute(a, axis, [((i + k) % n, i) for i in range(n)])]
    all_gather x1 -> x0, blocking collectives: 47.3 us -> none  [sent_together(): lax.all_gather(both, axis, axis=dim, tiled=True)]
    ppermute x0 -> x31, waiting for transfers between devices: none -> 42.5 us  [the longest x14 24.7 us: fetch(): return lax.ppermute(a, axis, [((i + k) % n, i) for i in range(n)])]
    psum x4 -> x0, blocking collectives: 38.7 us -> none  [by_axis(): return functools.reduce(lax.psum, axes, array)]
    pallas_call x0 -> x5, Pallas kernels: none -> 18.4 us  [kernel_call(): pl.pallas_call(kernel, out_shape=[jax.ShapeDtypeStruct(s, d) for s, d in...]
    slice x3 -> x1, local copies, waits for them, and re-layouts: 10.1 us -> 0.57 us  [local(): gains[2:4]]
  transfers between devices with their start and end apart: 2 -> 31, of which waited for: 1 -> 15; matrix products, arithmetic and copies ran while one was open for 24% -> 0% of each run, Pallas kernels for 0% -> 1%
where the time goes in v1:
time: 126 us; the launch traced here: 124 us
  starting transfers between devices  57.7 us (46%)
  waiting for transfers between devices  42.5 us (34%)
  Pallas kernels  18.4 us (15%)
  local copies, waits for them, and re-layouts  3.59 us (3%)
    ppermute x14, starting transfers between devices, fetch(): return lax.ppermute(a, axis, [((i + k) % n, i) for i in range(n)])  31.6 us
    ppermute x14, waiting for transfers between devices, fetch(): return lax.ppermute(a, axis, [((i + k) % n, i) for i in range(n)])  24.7 us
    pallas_call x5, Pallas kernels, kernel_call(): pl.pallas_call(kernel, out_shape=[jax.ShapeDtypeStruct(s, d) for s, d in...  18.4 us
    ppermute x11, starting transfers between devices, summed(): lax.ppermute(a, axis, [(i, i ^ k) for i in range(n)])  15.2 us
    ppermute x11, waiting for transfers between devices, summed(): lax.ppermute(a, axis, [(i, i ^ k) for i in range(n)])  12.7 us
    ppermute x6, starting transfers between devices, give(): return lax.ppermute(a, axis, [(i, (i + k) % n) for i in range(n)])  10.9 us
    ppermute x6, waiting for transfers between devices, give(): return lax.ppermute(a, axis, [(i, (i + k) % n) for i in range(n)])  5.16 us
    unnamed x14, local copies, waits for them, and re-layouts  3.02 us
  transfers between devices with their start and end apart: 31, of which 15 were waited for; matrix products, arithmetic and copies ran while one was open for 0% of the time, Pallas kernels for 1%

profile of v1, /device:TPU:32, one launch (start us, length us, event | category | flops | bytes accessed | tf_op | source)
XLA Modules:
  0.0 124.0 jit_solution(18153905416812972526)
XLA Ops:
  1.7 3.3 %collective-permute-start.2 = (bf16[2,3,144,128]{3,2,1,0:T(8,128)(2,1)S(1)}, bf16[2,3,144,128]{3,2,1,0:T(8,128)(2,1)S(1)}, u32[]{:S(2)}, u32[]{:S(2)}) collective-permute-start(bf16[2,3,144,128]{3,2,1,0:T(8,128)(2,1)S(1)} %pad_maximum_fusion.refs_0_.refs_4_.raw), channel_id=1, source_target_pairs={{192,0},{0,64},{64,128},{128,192},{193,1},{1,65},{65,129},{129,193... | collective-permute-start | bytes 663560 | tf_op jit(solution)/shard_map/ppermute | solution.py:210
  5.0 4.5 %collective-permute-start.1 = (bf16[2,3,144,128]{3,2,1,0:T(8,128)(2,1)S(1)}, bf16[2,3,144,128]{3,2,1,0:T(8,128)(2,1)S(1)}, u32[]{:S(2)}, u32[]{:S(2)}) collective-permute-start(bf16[2,3,144,128]{3,2,1,0:T(8,128)(2,1)S(1)} %pad_maximum_fusion.refs_0_.refs_4_.raw), channel_id=1, source_target_pairs={{128,0},{192,64},{0,128},{64,192},{129,1},{193,65},{1,129},{65,193... | collective-permute-start | bytes 663560 | tf_op jit(solution)/shard_map/ppermute | solution.py:210
  10.6 2.7 %collective-permute-start = (bf16[2,3,144,128]{3,2,1,0:T(8,128)(2,1)S(1)}, bf16[2,3,144,128]{3,2,1,0:T(8,128)(2,1)S(1)}, u32[]{:S(2)}, u32[]{:S(2)}) collective-permute-start(bf16[2,3,144,128]{3,2,1,0:T(8,128)(2,1)S(1)} %pad_maximum_fusion.refs_0_.refs_4_.raw), channel_id=1, source_target_pairs={{64,0},{128,64},{192,128},{0,192},{65,1},{129,65},{193,129},{1,193... | collective-permute-start | bytes 663560 | tf_op jit(solution)/shard_map/ppermute | solution.py:210
  13.3 1.5 %collective-permute-start.8 = (bf16[2,3,144,128]{3,2,1,0:T(8,128)(2,1)S(1)}, bf16[2,3,144,128]{3,2,1,0:T(8,128)(2,1)S(1)}, u32[]{:S(2)}, u32[]{:S(2)}) collective-permute-start(bf16[2,3,144,128]{3,2,1,0:T(8,128)(2,1)S(1)} %pad_maximum_fusion.1.refs_4_.refs_8_.raw), channel_id=1, source_target_pairs={{24,0},{0,8},{8,16},{16,24},{25,1},{1,9},{9,17},{17,25},{26,2},{2,... | collective-permute-start | bytes 663560 | tf_op jit(solution)/shard_map/ppermute | solution.py:210
  14.8 7.9 %collective-permute-done.2.refs_3_.refs_7_ = bf16[2,3,144,128]{3,2,1,0:T(8,128)(2,1)S(1)} collective-permute-done((bf16[2,3,144,128]{3,2,1,0:T(8,128)(2,1)S(1)}, bf16[2,3,144,128]{3,2,1,0:T(8,128)(2,1)S(1)}, u32[]{:S(2)}, u32[]{:S(2)}) %collective-permute-start.2) | collective-permute-done | bytes 221216 | tf_op jit(solution)/shard_map/ppermute | solution.py:210
  22.7 3.0 %collective-permute-start.6 = (bf16[2,3,144,128]{3,2,1,0:T(8,128)(2,1)S(1)}, bf16[2,3,144,128]{3,2,1,0:T(8,128)(2,1)S(1)}, u32[]{:S(2)}, u32[]{:S(2)}) collective-permute-start(bf16[2,3,144,128]{3,2,1,0:T(8,128)(2,1)S(1)} %pad_maximum_fusion.1.refs_4_.refs_8_.raw), channel_id=1, source_target_pairs={{16,0},{24,8},{0,16},{8,24},{17,1},{25,9},{1,17},{9,25},{18,2},{26... | collective-permute-start | bytes 663560 | tf_op jit(solution)/shard_map/ppermute | solution.py:210
  26.9 2.4 %collective-permute-done.3.refs_5_.refs_9_ = bf16[2,3,144,128]{3,2,1,0:T(8,128)(2,1)S(1)} collective-permute-done((bf16[2,3,144,128]{3,2,1,0:T(8,128)(2,1)S(1)}, bf16[2,3,144,128]{3,2,1,0:T(8,128)(2,1)S(1)}, u32[]{:S(2)}, u32[]{:S(2)}) %collective-permute-start.3) | collective-permute-done | bytes 221216 | tf_op jit(solution)/shard_map/ppermute | solution.py:210
  29.3 1.5 %collective-permute-start.9 = (bf16[2,3,144,128]{3,2,1,0:T(8,128)(2,1)S(1)}, bf16[2,3,144,128]{3,2,1,0:T(8,128)(2,1)S(1)}, u32[]{:S(2)}, u32[]{:S(2)}) collective-permute-start(bf16[2,3,144,128]{3,2,1,0:T(8,128)(2,1)S(1)} %collective-permute-done.3.refs_5_.refs_9_), channel_id=1, source_target_pairs={{24,0},{0,8},{8,16},{16,24},{25,1},{1,9},{9,17},{17,25},{26,2},{2,... | collective-permute-start | bytes 663560 | tf_op jit(solution)/shard_map/ppermute | solution.py:210
  30.8 2.9 %collective-permute-done.refs_1_.refs_5_ = bf16[2,3,144,128]{3,2,1,0:T(8,128)(2,1)S(1)} collective-permute-done((bf16[2,3,144,128]{3,2,1,0:T(8,128)(2,1)S(1)}, bf16[2,3,144,128]{3,2,1,0:T(8,128)(2,1)S(1)}, u32[]{:S(2)}, u32[]{:S(2)}) %collective-permute-start) | collective-permute-done | bytes 221216 | tf_op jit(solution)/shard_map/ppermute | solution.py:210
  33.7 3.0 %collective-permute-start.7 = (bf16[2,3,144,128]{3,2,1,0:T(8,128)(2,1)S(1)}, bf16[2,3,144,128]{3,2,1,0:T(8,128)(2,1)S(1)}, u32[]{:S(2)}, u32[]{:S(2)}) collective-permute-start(bf16[2,3,144,128]{3,2,1,0:T(8,128)(2,1)S(1)} %collective-permute-done.3.refs_5_.refs_9_), channel_id=1, source_target_pairs={{16,0},{24,8},{0,16},{8,24},{17,1},{25,9},{1,17},{9,25},{18,2},{26... | collective-permute-start | bytes 663560 | tf_op jit(solution)/shard_map/ppermute | solution.py:210
  37.9 5.1 %collective-permute-done.7.refs_9_.refs_13_ = bf16[2,3,144,128]{3,2,1,0:T(8,128)(2,1)S(1)} collective-permute-done((bf16[2,3,144,128]{3,2,1,0:T(8,128)(2,1)S(1)}, bf16[2,3,144,128]{3,2,1,0:T(8,128)(2,1)S(1)}, u32[]{:S(2)}, u32[]{:S(2)}) %collective-permute-start.7) | collective-permute-done | bytes 221216 | tf_op jit(solution)/shard_map/ppermute | solution.py:210
  43.0 3.4 %collective-permute-done.5.refs_7_.refs_11_ = bf16[2,3,144,128]{3,2,1,0:T(8,128)(2,1)S(1)} collective-permute-done((bf16[2,3,144,128]{3,2,1,0:T(8,128)(2,1)S(1)}, bf16[2,3,144,128]{3,2,1,0:T(8,128)(2,1)S(1)}, u32[]{:S(2)}, u32[]{:S(2)}) %collective-permute-start.5) | collective-permute-done | bytes 221216 | tf_op jit(solution)/shard_map/ppermute | solution.py:210
  46.4 4.8 %shard_map.101 = (f32[16,576]{1,0:T(8,128)S(1)}, bf16[3,576,128]{2,1,0:T(8,128)(2,1)S(1)}, bf16[3,1152,128]{2,1,0:T(8,128)(2,1)S(1)}, bf16[3,1152,128]{2,1,0:T(8,128)(2,1)S(1)}, bf16[3,576,128]{2,1,0:T(8,128)(2,1)S(1)}) custom-call(bf16[2,3,144,128]{3,2,1,0:T(8,128)(2,1)S(1)} %pad_maximum_fusion.refs_0_.refs_4_.raw, ...), custom_call_target="tpu_custom_call" | custom-call | flops 1019215872 | bytes 2656256 | tf_op jit(solution)/shard_map/pallas_call | solution.py:198
  53.0 1.3 %collective-permute-start.12 = (f32[16,576]{1,0:T(8,128)S(1)}, f32[16,576]{1,0:T(8,128)S(1)}, u32[]{:S(2)}, u32[]{:S(2)}) collective-permute-start(f32[16,576]{1,0:T(8,128)S(1)} %get-tuple-element.23.refs_0_), channel_id=1, source_target_pairs={{192,0},{0,64},{64,128},{128,192},{193,1},{1,65},{65,129},{129,193... | collective-permute-start | bytes 110600 | tf_op jit(solution)/shard_map/ppermute | solution.py:210
  54.3 5.3 %collective-permute-start.11 = (f32[16,576]{1,0:T(8,128)S(1)}, f32[16,576]{1,0:T(8,128)S(1)}, u32[]{:S(2)}, u32[]{:S(2)}) collective-permute-start(f32[16,576]{1,0:T(8,128)S(1)} %get-tuple-element.23.refs_0_), channel_id=1, source_target_pairs={{128,0},{192,64},{0,128},{64,192},{129,1},{193,65},{1,129},{65,193... | collective-permute-start | bytes 110600 | tf_op jit(solution)/shard_map/ppermute | solution.py:210
  59.6 2.0 %collective-permute-start.10 = (f32[16,576]{1,0:T(8,128)S(1)}, f32[16,576]{1,0:T(8,128)S(1)}, u32[]{:S(2)}, u32[]{:S(2)}) collective-permute-start(f32[16,576]{1,0:T(8,128)S(1)} %get-tuple-element.23.refs_0_), channel_id=1, source_target_pairs={{64,0},{128,64},{192,128},{0,192},{65,1},{129,65},{193,129},{1,193... | collective-permute-start | bytes 110600 | tf_op jit(solution)/shard_map/ppermute | solution.py:210
  61.6 1.4 %collective-permute-done.11.refs_2_ = f32[16,576]{1,0:T(8,128)S(1)} collective-permute-done((f32[16,576]{1,0:T(8,128)S(1)}, f32[16,576]{1,0:T(8,128)S(1)}, u32[]{:S(2)}, u32[]{:S(2)}) %collective-permute-start.11) | collective-permute-done | bytes 36896 | tf_op jit(solution)/shard_map/ppermute | solution.py:210
  63.0 1.5 %collective-permute-done.10.refs_1_ = f32[16,576]{1,0:T(8,128)S(1)} collective-permute-done((f32[16,576]{1,0:T(8,128)S(1)}, f32[16,576]{1,0:T(8,128)S(1)}, u32[]{:S(2)}, u32[]{:S(2)}) %collective-permute-start.10) | collective-permute-done | bytes 36896 | tf_op jit(solution)/shard_map/ppermute | solution.py:210
  64.5 11.6 %shard_map.102 = (f32[3,144,128]{2,1,0:T(8,128)S(1)}, bf16[3,144,128]{2,1,0:T(8,128)(2,1)S(1)}, bf16[3,144,128]{2,1,0:T(8,128)(2,1)S(1)}, bf16[3,144,128]{2,1,0:...) custom-call(f32[16,576]{1,0:T(8,128)S(1)} %get-tuple-element.23.refs, ...), custom_call_target="tpu_custom_call" | custom-call | flops 3057647616 | bytes 5457920 | tf_op jit(solution)/shard_map/pallas_call | solution.py:198
  77.3 3.0 %collective-permute-start.23 = (f32[8,128]{1,0:T(8,128)S(1)}, f32[8,128]{1,0:T(8,128)S(1)}, u32[]{:S(2)}, u32[]{:S(2)}) collective-permute-start(f32[8,128]{1,0:T(8,128)S(1)} %add.33), channel_id=1, source_target_pairs={{0,6},{2,4},{4,2},{6,0},{1,7},{3,5},{5,3},{7,1},{8,14},{10,12},{12... | collective-permute-start | bytes 12296 | tf_op jit(solution)/shard_map/ppermute | solution.py:218
  82.1 3.3 %collective-permute-done.22 = f32[8,128]{1,0:T(8,128)S(1)} collective-permute-done((f32[8,128]{1,0:T(8,128)S(1)}, f32[8,128]{1,0:T(8,128)S(1)}, u32[]{:S(2)}, u32[]{:S(2)}) %collective-permute-start.22) | collective-permute-done | bytes 4128 | tf_op jit(solution)/shard_map/ppermute | solution.py:218
  85.4 2.7 %collective-permute-start.26 = (f32[8,128]{1,0:T(8,128)S(1)}, f32[8,128]{1,0:T(8,128)S(1)}, u32[]{:S(2)}, u32[]{:S(2)}) collective-permute-start(f32[8,128]{1,0:T(8,128)S(1)} %add_add_fusion.2), channel_id=1, source_target_pairs={{0,24},{8,16},{16,8},{24,0},{1,25},{9,17},{17,9},{25,1},{2,26},{10... | collective-permute-start | bytes 12296 | tf_op jit(solution)/shard_map/ppermute | solution.py:218
  89.6 1.4 %collective-permute-start.16 = (bf16[2,2,3,144,128]{4,3,2,1,0:T(8,128)(2,1)S(1)}, bf16[2,2,3,144,128]{4,3,2,1,0:T(8,128)(2,1)S(1)}, u32[]{:S(2)}, u32[]{:S(2)}) collective-permute-start(bf16[2,2,3,144,128]{4,3,2,1,0:T(8,128)(2,1)S(1)} %get-tuple-element.33), channel_id=1, source_target_pairs={{0,8},{8,16},{16,24},{24,0},{1,9},{9,17},{17,25},{25,1},{2,10},{10... | collective-permute-start | bytes 1327112 | tf_op jit(solution)/shard_map/ppermute | solution.py:214
  90.9 2.7 %collective-permute-start.17 = (bf16[2,2,3,144,128]{4,3,2,1,0:T(8,128)(2,1)S(1)}, bf16[2,2,3,144,128]{4,3,2,1,0:T(8,128)(2,1)S(1)}, u32[]{:S(2)}, u32[]{:S(2)}) collective-permute-start(bf16[2,2,3,144,128]{4,3,2,1,0:T(8,128)(2,1)S(1)} %get-tuple-element.34), channel_id=1, source_target_pairs={{0,16},{8,24},{16,0},{24,8},{1,17},{9,25},{17,1},{25,9},{2,18},{10... | collective-permute-start | bytes 1327112 | tf_op jit(solution)/shard_map/ppermute | solution.py:214
  94.4 3.6 %collective-permute-done.27 = f32[8,128]{1,0:T(8,128)S(1)} collective-permute-done((f32[8,128]{1,0:T(8,128)S(1)}, f32[8,128]{1,0:T(8,128)S(1)}, u32[]{:S(2)}, u32[]{:S(2)}) %collective-permute-start.27) | collective-permute-done | bytes 4128 | tf_op jit(solution)/shard_map/ppermute | solution.py:218
  98.0 3.2 %collective-permute-start.30 = (f32[8,128]{1,0:T(8,128)S(1)}, f32[8,128]{1,0:T(8,128)S(1)}, u32[]{:S(2)}, u32[]{:S(2)}) collective-permute-start(f32[8,128]{1,0:T(8,128)S(1)} %add.40), channel_id=1, source_target_pairs={{0,192},{64,128},{128,64},{192,0},{1,193},{65,129},{129,65},{193,1... | collective-permute-start | bytes 12296 | tf_op jit(solution)/shard_map/ppermute | solution.py:218
  101.2 2.0 %collective-permute-start.29 = (f32[8,128]{1,0:T(8,128)S(1)}, f32[8,128]{1,0:T(8,128)S(1)}, u32[]{:S(2)}, u32[]{:S(2)}) collective-permute-start(f32[8,128]{1,0:T(8,128)S(1)} %add.40), channel_id=1, source_target_pairs={{0,128},{64,192},{128,0},{192,64},{1,129},{65,193},{129,1},{193,65... | collective-permute-start | bytes 12296 | tf_op jit(solution)/shard_map/ppermute | solution.py:218
  103.7 1.6 %collective-permute-start.28 = (f32[8,128]{1,0:T(8,128)S(1)}, f32[8,128]{1,0:T(8,128)S(1)}, u32[]{:S(2)}, u32[]{:S(2)}) collective-permute-start(f32[8,128]{1,0:T(8,128)S(1)} %add.40), channel_id=1, source_target_pairs={{0,64},{64,0},{128,192},{192,128},{1,65},{65,1},{129,193},{193,129... | collective-permute-start | bytes 12296 | tf_op jit(solution)/shard_map/ppermute | solution.py:218
  105.4 3.4 %collective-permute-done.29 = f32[8,128]{1,0:T(8,128)S(1)} collective-permute-done((f32[8,128]{1,0:T(8,128)S(1)}, f32[8,128]{1,0:T(8,128)S(1)}, u32[]{:S(2)}, u32[]{:S(2)}) %collective-permute-start.29) | collective-permute-done | bytes 4128 | tf_op jit(solution)/shard_map/ppermute | solution.py:218
  110.0 2.1 %collective-permute-start.14 = (bf16[3,144,128]{2,1,0:T(8,128)(2,1)S(1)}, bf16[3,144,128]{2,1,0:T(8,128)(2,1)S(1)}, u32[]{:S(2)}, u32[]{:S(2)}) collective-permute-start(bf16[3,144,128]{2,1,0:T(8,128)(2,1)S(1)} %get-tuple-element.30), channel_id=1, source_target_pairs={{0,128},{64,192},{128,0},{192,64},{1,129},{65,193},{129,1},{193,65... | collective-permute-start | bytes 331784 | tf_op jit(solution)/shard_map/ppermute | solution.py:214
  112.2 2.8 %collective-permute-start.15 = (bf16[3,144,128]{2,1,0:T(8,128)(2,1)S(1)}, bf16[3,144,128]{2,1,0:T(8,128)(2,1)S(1)}, u32[]{:S(2)}, u32[]{:S(2)}) collective-permute-start(bf16[3,144,128]{2,1,0:T(8,128)(2,1)S(1)} %get-tuple-element.31), channel_id=1, source_target_pairs={{0,192},{64,0},{128,64},{192,128},{1,193},{65,1},{129,65},{193,129... | collective-permute-start | bytes 331784 | tf_op jit(solution)/shard_map/ppermute | solution.py:214
  117.0 4.8 %collective-permute-done.14.r2 = bf16[3,144,128]{2,1,0:T(8,128)(2,1)S(1)} collective-permute-done((bf16[3,144,128]{2,1,0:T(8,128)(2,1)S(1)}, bf16[3,144,128]{2,1,0:T(8,128)(2,1)S(1)}, u32[]{:S(2)}, u32[]{:S(2)}) %collective-permute-start.14) | collective-permute-done | bytes 110624 | tf_op jit(solution)/shard_map/ppermute | solution.py:214
  (57 shorter events, 17.4 us)
Async XLA Ops:
  1.7 21.1 %collective-permute-start.2 = (bf16[2,3,144,128]{3,2,1,0:T(8,128)(2,1)S(1)}, bf16[2,3,144,128]{3,2,1,0:T(8,128)(2,1)S(1)}, u32[]{:S(2)}, u32[]{:S(2)}) collective-permute-start(bf16[2,3,144,128]{3,2,1,0:T(8,128)(2,1)S(1)} %pad_maximum_fusion.refs_0_.refs_4_.raw), channel_id=1, source_target_pairs={{192,0},{0,64},{64,128},{128,192},{193,1},{1,65},{65,129},{129,193... | collective-permute-start | bytes 663560 | tf_op jit(solution)/shard_map/ppermute | solution.py:210
  5.0 20.7 %collective-permute-start.1 = (bf16[2,3,144,128]{3,2,1,0:T(8,128)(2,1)S(1)}, bf16[2,3,144,128]{3,2,1,0:T(8,128)(2,1)S(1)}, u32[]{:S(2)}, u32[]{:S(2)}) collective-permute-start(bf16[2,3,144,128]{3,2,1,0:T(8,128)(2,1)S(1)} %pad_maximum_fusion.refs_0_.refs_4_.raw), channel_id=1, source_target_pairs={{128,0},{192,64},{0,128},{64,192},{129,1},{193,65},{1,129},{65,193... | collective-permute-start | bytes 663560 | tf_op jit(solution)/shard_map/ppermute | solution.py:210
  9.5 36.9 %copy-start.2 = (f32[2,128]{1,0:T(2,128)S(1)}, f32[2,128]{1,0:T(2,128)}, u32[]{:S(2)}) copy-start(f32[2,128]{1,0:T(2,128)} %gain_ref.3) | copy-start | bytes 3076
  9.6 19.8 %collective-permute-start.3 = (bf16[2,3,144,128]{3,2,1,0:T(8,128)(2,1)S(1)}, bf16[2,3,144,128]{3,2,1,0:T(8,128)(2,1)S(1)}, u32[]{:S(2)}, u32[]{:S(2)}) collective-permute-start(bf16[2,3,144,128]{3,2,1,0:T(8,128)(2,1)S(1)} %pad_maximum_fusion.1.refs_4_.refs_8_.raw), channel_id=1, source_target_pairs={{32,0},{0,32},{33,1},{1,33},{34,2},{2,34},{35,3},{3,35},{36,4},{4,... | collective-permute-start | bytes 663560 | tf_op jit(solution)/shard_map/ppermute | solution.py:210
  10.6 23.1 %collective-permute-start = (bf16[2,3,144,128]{3,2,1,0:T(8,128)(2,1)S(1)}, bf16[2,3,144,128]{3,2,1,0:T(8,128)(2,1)S(1)}, u32[]{:S(2)}, u32[]{:S(2)}) collective-permute-start(bf16[2,3,144,128]{3,2,1,0:T(8,128)(2,1)S(1)} %pad_maximum_fusion.refs_0_.refs_4_.raw), channel_id=1, source_target_pairs={{64,0},{128,64},{192,128},{0,192},{65,1},{129,65},{193,129},{1,193... | collective-permute-start | bytes 663560 | tf_op jit(solution)/shard_map/ppermute | solution.py:210
  13.3 23.4 %collective-permute-start.8 = (bf16[2,3,144,128]{3,2,1,0:T(8,128)(2,1)S(1)}, bf16[2,3,144,128]{3,2,1,0:T(8,128)(2,1)S(1)}, u32[]{:S(2)}, u32[]{:S(2)}) collective-permute-start(bf16[2,3,144,128]{3,2,1,0:T(8,128)(2,1)S(1)} %pad_maximum_fusion.1.refs_4_.refs_8_.raw), channel_id=1, source_target_pairs={{24,0},{0,8},{8,16},{16,24},{25,1},{1,9},{9,17},{17,25},{26,2},{2,... | collective-permute-start | bytes 663560 | tf_op jit(solution)/shard_map/ppermute | solution.py:210
  22.7 15.1 %collective-permute-start.6 = (bf16[2,3,144,128]{3,2,1,0:T(8,128)(2,1)S(1)}, bf16[2,3,144,128]{3,2,1,0:T(8,128)(2,1)S(1)}, u32[]{:S(2)}, u32[]{:S(2)}) collective-permute-start(bf16[2,3,144,128]{3,2,1,0:T(8,128)(2,1)S(1)} %pad_maximum_fusion.1.refs_4_.refs_8_.raw), channel_id=1, source_target_pairs={{16,0},{24,8},{0,16},{8,24},{17,1},{25,9},{1,17},{9,25},{18,2},{26... | collective-permute-start | bytes 663560 | tf_op jit(solution)/shard_map/ppermute | solution.py:210
  25.8 12.1 %collective-permute-start.4 = (bf16[2,3,144,128]{3,2,1,0:T(8,128)(2,1)S(1)}, bf16[2,3,144,128]{3,2,1,0:T(8,128)(2,1)S(1)}, u32[]{:S(2)}, u32[]{:S(2)}) collective-permute-start(bf16[2,3,144,128]{3,2,1,0:T(8,128)(2,1)S(1)} %pad_maximum_fusion.1.refs_4_.refs_8_.raw), channel_id=1, source_target_pairs={{8,0},{16,8},{24,16},{0,24},{9,1},{17,9},{25,17},{1,25},{10,2},{18... | collective-permute-start | bytes 663560 | tf_op jit(solution)/shard_map/ppermute | solution.py:210
  29.3 8.6 %collective-permute-start.9 = (bf16[2,3,144,128]{3,2,1,0:T(8,128)(2,1)S(1)}, bf16[2,3,144,128]{3,2,1,0:T(8,128)(2,1)S(1)}, u32[]{:S(2)}, u32[]{:S(2)}) collective-permute-start(bf16[2,3,144,128]{3,2,1,0:T(8,128)(2,1)S(1)} %collective-permute-done.3.refs_5_.refs_9_), channel_id=1, source_target_pairs={{24,0},{0,8},{8,16},{16,24},{25,1},{1,9},{9,17},{17,25},{26,2},{2,... | collective-permute-start | bytes 663560 | tf_op jit(solution)/shard_map/ppermute | solution.py:210
  33.7 9.3 %collective-permute-start.7 = (bf16[2,3,144,128]{3,2,1,0:T(8,128)(2,1)S(1)}, bf16[2,3,144,128]{3,2,1,0:T(8,128)(2,1)S(1)}, u32[]{:S(2)}, u32[]{:S(2)}) collective-permute-start(bf16[2,3,144,128]{3,2,1,0:T(8,128)(2,1)S(1)} %collective-permute-done.3.refs_5_.refs_9_), channel_id=1, source_target_pairs={{16,0},{24,8},{0,16},{8,24},{17,1},{25,9},{1,17},{9,25},{18,2},{26... | collective-permute-start | bytes 663560 | tf_op jit(solution)/shard_map/ppermute | solution.py:210
  36.7 9.6 %collective-permute-start.5 = (bf16[2,3,144,128]{3,2,1,0:T(8,128)(2,1)S(1)}, bf16[2,3,144,128]{3,2,1,0:T(8,128)(2,1)S(1)}, u32[]{:S(2)}, u32[]{:S(2)}) collective-permute-start(bf16[2,3,144,128]{3,2,1,0:T(8,128)(2,1)S(1)} %collective-permute-done.3.refs_5_.refs_9_), channel_id=1, source_target_pairs={{8,0},{16,8},{24,16},{0,24},{9,1},{17,9},{25,17},{1,25},{10,2},{18... | collective-permute-start | bytes 663560 | tf_op jit(solution)/shard_map/ppermute | solution.py:210
  53.0 8.6 %collective-permute-start.12 = (f32[16,576]{1,0:T(8,128)S(1)}, f32[16,576]{1,0:T(8,128)S(1)}, u32[]{:S(2)}, u32[]{:S(2)}) collective-permute-start(f32[16,576]{1,0:T(8,128)S(1)} %get-tuple-element.23.refs_0_), channel_id=1, source_target_pairs={{192,0},{0,64},{64,128},{128,192},{193,1},{1,65},{65,129},{129,193... | collective-permute-start | bytes 110600 | tf_op jit(solution)/shard_map/ppermute | solution.py:210
  54.3 8.7 %collective-permute-start.11 = (f32[16,576]{1,0:T(8,128)S(1)}, f32[16,576]{1,0:T(8,128)S(1)}, u32[]{:S(2)}, u32[]{:S(2)}) collective-permute-start(f32[16,576]{1,0:T(8,128)S(1)} %get-tuple-element.23.refs_0_), channel_id=1, source_target_pairs={{128,0},{192,64},{0,128},{64,192},{129,1},{193,65},{1,129},{65,193... | collective-permute-start | bytes 110600 | tf_op jit(solution)/shard_map/ppermute | solution.py:210
  59.6 4.9 %collective-permute-start.10 = (f32[16,576]{1,0:T(8,128)S(1)}, f32[16,576]{1,0:T(8,128)S(1)}, u32[]{:S(2)}, u32[]{:S(2)}) collective-permute-start(f32[16,576]{1,0:T(8,128)S(1)} %get-tuple-element.23.refs_0_), channel_id=1, source_target_pairs={{64,0},{128,64},{192,128},{0,192},{65,1},{129,65},{193,129},{1,193... | collective-permute-start | bytes 110600 | tf_op jit(solution)/shard_map/ppermute | solution.py:210
  76.1 1.2 collective-permute-start.20
  77.3 4.8 %collective-permute-start.23 = (f32[8,128]{1,0:T(8,128)S(1)}, f32[8,128]{1,0:T(8,128)S(1)}, u32[]{:S(2)}, u32[]{:S(2)}) collective-permute-start(f32[8,128]{1,0:T(8,128)S(1)} %add.33), channel_id=1, source_target_pairs={{0,6},{2,4},{4,2},{6,0},{1,7},{3,5},{5,3},{7,1},{8,14},{10,12},{12... | collective-permute-start | bytes 12296 | tf_op jit(solution)/shard_map/ppermute | solution.py:218
  80.3 5.1 %collective-permute-start.22 = (f32[8,128]{1,0:T(8,128)S(1)}, f32[8,128]{1,0:T(8,128)S(1)}, u32[]{:S(2)}, u32[]{:S(2)}) collective-permute-start(f32[8,128]{1,0:T(8,128)S(1)} %add.33), channel_id=1, source_target_pairs={{0,4},{2,6},{4,0},{6,2},{1,5},{3,7},{5,1},{7,3},{8,12},{10,14},{12... | collective-permute-start | bytes 12296 | tf_op jit(solution)/shard_map/ppermute | solution.py:218
  80.9 4.5 %collective-permute-start.21 = (f32[8,128]{1,0:T(8,128)S(1)}, f32[8,128]{1,0:T(8,128)S(1)}, u32[]{:S(2)}, u32[]{:S(2)}) collective-permute-start(f32[8,128]{1,0:T(8,128)S(1)} %add.33), channel_id=1, source_target_pairs={{0,2},{2,0},{4,6},{6,4},{1,3},{3,1},{5,7},{7,5},{8,10},{10,8},{12,... | collective-permute-start | bytes 12296 | tf_op jit(solution)/shard_map/ppermute | solution.py:218
  85.4 8.3 %collective-permute-start.26 = (f32[8,128]{1,0:T(8,128)S(1)}, f32[8,128]{1,0:T(8,128)S(1)}, u32[]{:S(2)}, u32[]{:S(2)}) collective-permute-start(f32[8,128]{1,0:T(8,128)S(1)} %add_add_fusion.2), channel_id=1, source_target_pairs={{0,24},{8,16},{16,8},{24,0},{1,25},{9,17},{17,9},{25,1},{2,26},{10... | collective-permute-start | bytes 12296 | tf_op jit(solution)/shard_map/ppermute | solution.py:218
  88.1 6.2 %collective-permute-start.25 = (f32[8,128]{1,0:T(8,128)S(1)}, f32[8,128]{1,0:T(8,128)S(1)}, u32[]{:S(2)}, u32[]{:S(2)}) collective-permute-start(f32[8,128]{1,0:T(8,128)S(1)} %add_add_fusion.2), channel_id=1, source_target_pairs={{0,16},{8,24},{16,0},{24,8},{1,17},{9,25},{17,1},{25,9},{2,18},{10... | collective-permute-start | bytes 12296 | tf_op jit(solution)/shard_map/ppermute | solution.py:218
  88.9 5.4 %collective-permute-start.24 = (f32[8,128]{1,0:T(8,128)S(1)}, f32[8,128]{1,0:T(8,128)S(1)}, u32[]{:S(2)}, u32[]{:S(2)}) collective-permute-start(f32[8,128]{1,0:T(8,128)S(1)} %add_add_fusion.2), channel_id=1, source_target_pairs={{0,8},{8,0},{16,24},{24,16},{1,9},{9,1},{17,25},{25,17},{2,10},{10... | collective-permute-start | bytes 12296 | tf_op jit(solution)/shard_map/ppermute | solution.py:218
  89.6 22.6 %collective-permute-start.16 = (bf16[2,2,3,144,128]{4,3,2,1,0:T(8,128)(2,1)S(1)}, bf16[2,2,3,144,128]{4,3,2,1,0:T(8,128)(2,1)S(1)}, u32[]{:S(2)}, u32[]{:S(2)}) collective-permute-start(bf16[2,2,3,144,128]{4,3,2,1,0:T(8,128)(2,1)S(1)} %get-tuple-element.33), channel_id=1, source_target_pairs={{0,8},{8,16},{16,24},{24,0},{1,9},{9,17},{17,25},{25,1},{2,10},{10... | collective-permute-start | bytes 1327112 | tf_op jit(solution)/shard_map/ppermute | solution.py:214
  90.9 24.0 %collective-permute-start.17 = (bf16[2,2,3,144,128]{4,3,2,1,0:T(8,128)(2,1)S(1)}, bf16[2,2,3,144,128]{4,3,2,1,0:T(8,128)(2,1)S(1)}, u32[]{:S(2)}, u32[]{:S(2)}) collective-permute-start(bf16[2,2,3,144,128]{4,3,2,1,0:T(8,128)(2,1)S(1)} %get-tuple-element.34), channel_id=1, source_target_pairs={{0,16},{8,24},{16,0},{24,8},{1,17},{9,25},{17,1},{25,9},{2,18},{10... | collective-permute-start | bytes 1327112 | tf_op jit(solution)/shard_map/ppermute | solution.py:214
  93.7 21.3 %collective-permute-start.18 = (bf16[2,2,3,144,128]{4,3,2,1,0:T(8,128)(2,1)S(1)}, bf16[2,2,3,144,128]{4,3,2,1,0:T(8,128)(2,1)S(1)}, u32[]{:S(2)}, u32[]{:S(2)}) collective-permute-start(bf16[2,2,3,144,128]{4,3,2,1,0:T(8,128)(2,1)S(1)} %get-tuple-element.35), channel_id=1, source_target_pairs={{0,24},{8,0},{16,8},{24,16},{1,25},{9,1},{17,9},{25,17},{2,26},{10... | collective-permute-start | bytes 1327112 | tf_op jit(solution)/shard_map/ppermute | solution.py:214
  94.3 3.7 %collective-permute-start.27 = (f32[8,128]{1,0:T(8,128)S(1)}, f32[8,128]{1,0:T(8,128)S(1)}, u32[]{:S(2)}, u32[]{:S(2)}) collective-permute-start(f32[8,128]{1,0:T(8,128)S(1)} %add_add_fusion.1), channel_id=1, source_target_pairs={{0,32},{32,0},{1,33},{33,1},{2,34},{34,2},{3,35},{35,3},{4,36},{36... | collective-permute-start | bytes 12296 | tf_op jit(solution)/shard_map/ppermute | solution.py:218
  98.0 5.7 %collective-permute-start.30 = (f32[8,128]{1,0:T(8,128)S(1)}, f32[8,128]{1,0:T(8,128)S(1)}, u32[]{:S(2)}, u32[]{:S(2)}) collective-permute-start(f32[8,128]{1,0:T(8,128)S(1)} %add.40), channel_id=1, source_target_pairs={{0,192},{64,128},{128,64},{192,0},{1,193},{65,129},{129,65},{193,1... | collective-permute-start | bytes 12296 | tf_op jit(solution)/shard_map/ppermute | solution.py:218
  101.2 7.5 %collective-permute-start.29 = (f32[8,128]{1,0:T(8,128)S(1)}, f32[8,128]{1,0:T(8,128)S(1)}, u32[]{:S(2)}, u32[]{:S(2)}) collective-permute-start(f32[8,128]{1,0:T(8,128)S(1)} %add.40), channel_id=1, source_target_pairs={{0,128},{64,192},{128,0},{192,64},{1,129},{65,193},{129,1},{193,65... | collective-permute-start | bytes 12296 | tf_op jit(solution)/shard_map/ppermute | solution.py:218
  103.7 6.3 %collective-permute-start.28 = (f32[8,128]{1,0:T(8,128)S(1)}, f32[8,128]{1,0:T(8,128)S(1)}, u32[]{:S(2)}, u32[]{:S(2)}) collective-permute-start(f32[8,128]{1,0:T(8,128)S(1)} %add.40), channel_id=1, source_target_pairs={{0,64},{64,0},{128,192},{192,128},{1,65},{65,1},{129,193},{193,129... | collective-permute-start | bytes 12296 | tf_op jit(solution)/shard_map/ppermute | solution.py:218
  108.7 8.3 %collective-permute-start.13 = (bf16[3,144,128]{2,1,0:T(8,128)(2,1)S(1)}, bf16[3,144,128]{2,1,0:T(8,128)(2,1)S(1)}, u32[]{:S(2)}, u32[]{:S(2)}) collective-permute-start(bf16[3,144,128]{2,1,0:T(8,128)(2,1)S(1)} %get-tuple-element.29), channel_id=1, source_target_pairs={{0,64},{64,128},{128,192},{192,0},{1,65},{65,129},{129,193},{193,1... | collective-permute-start | bytes 331784 | tf_op jit(solution)/shard_map/ppermute | solution.py:214
  110.0 11.8 %collective-permute-start.14 = (bf16[3,144,128]{2,1,0:T(8,128)(2,1)S(1)}, bf16[3,144,128]{2,1,0:T(8,128)(2,1)S(1)}, u32[]{:S(2)}, u32[]{:S(2)}) collective-permute-start(bf16[3,144,128]{2,1,0:T(8,128)(2,1)S(1)} %get-tuple-element.30), channel_id=1, source_target_pairs={{0,128},{64,192},{128,0},{192,64},{1,129},{65,193},{129,1},{193,65... | collective-permute-start | bytes 331784 | tf_op jit(solution)/shard_map/ppermute | solution.py:214
  112.2 10.0 %collective-permute-start.15 = (bf16[3,144,128]{2,1,0:T(8,128)(2,1)S(1)}, bf16[3,144,128]{2,1,0:T(8,128)(2,1)S(1)}, u32[]{:S(2)}, u32[]{:S(2)}) collective-permute-start(bf16[3,144,128]{2,1,0:T(8,128)(2,1)S(1)} %get-tuple-element.31), channel_id=1, source_target_pairs={{0,192},{64,0},{128,64},{192,128},{1,193},{65,1},{129,65},{193,129... | collective-permute-start | bytes 331784 | tf_op jit(solution)/shard_map/ppermute | solution.py:214
  116.3 6.8 %collective-permute-start.19 = (bf16[2,3,144,128]{3,2,1,0:T(8,128)(2,1)S(1)}, bf16[2,3,144,128]{3,2,1,0:T(8,128)(2,1)S(1)}, u32[]{:S(2)}, u32[]{:S(2)}) collective-permute-start(bf16[2,3,144,128]{3,2,1,0:T(8,128)(2,1)S(1)} %get-tuple-element.37), channel_id=1, source_target_pairs={{32,0},{0,32},{33,1},{1,33},{34,2},{2,34},{35,3},{3,35},{36,4},{4,... | collective-permute-start | bytes 663560 | tf_op jit(solution)/shard_map/ppermute | solution.py:210
  (6 other events, 57.6 us)

commit v2 on v1

--- a/solution.py
+++ b/solution.py
@@ -19,6 +19,8 @@
 FACTOR = 1.0 / math.sqrt(HD)
 SCALE2 = FACTOR * math.log2(math.e)
 F32, BF16 = jnp.float32, jnp.bfloat16
+VMEM_LIMIT = 24 * 1024 * 1024
+MESSAGE = NH * BR + 32
 ALL_ROWS = ("zq", "zk", "x")
 
 
@@ -55,7 +57,7 @@
 
 def q_block(slot, place):
     zq, zk, x = place
-    return (2 * lax.rem(zq + slot, NQ) + zk) * NX + x
+    return (2 * (zq ^ slot) + zk) * NX + x
 
 
 def kv_block(xslot, j, place):
@@ -64,7 +66,7 @@
 
 
 def q_offset(slot, place):
-    return pl.multiple_of(lax.rem(place[0] + slot, NQ) * BR, 16)
+    return pl.multiple_of((place[0] ^ slot) * BR, 16)
 
 
 def stat_kernel(*refs):
@@ -110,17 +112,24 @@
         stat_ref[3 * h + 2 : 3 * h + 3, :] = dot
 
 
-def grad_kernel(*refs):
-    s_refs, q_refs = refs[:NQ], refs[NQ : 2 * NQ]
-    kv_refs = refs[2 * NQ : 2 * NQ + NX * NZ]
-    (gq_ref, gk_ref, qn_ref, kn_ref, v_ref, do_ref,
-     dq_own, dq1, dq2, dq3, kv_own, kv1, kv2, kv3, gain_ref, dq_all) = refs[2 * NQ + NX * NZ :]
+def grad_kernel(k, first, last, *refs):
+    s_refs, refs = refs[:NQ], refs[NQ:]
+    kv_refs, refs = refs[:NZ], refs[NZ:]
+    q_refs, refs = (refs[:NQ], refs[NQ:]) if last else ((), refs)
+    qn_ref, kn_ref, v_ref, do_ref, *refs = refs
+    if first:
+        kv_out, dq_ref, gain_ref = refs
+    elif last:
+        dq_in, gain_in, kv_out, dq0, dq1, dq2, dq3, gain_ref, dq_ref = refs
+        dq_outs = (dq0, dq1, dq2, dq3)
+    else:
+        dq_in, gain_in, kv_out, dq_ref, gain_ref = refs
     place = here()
-    kv_outs, dq_outs = (kv_own, kv1, kv2, kv3), (dq_own, dq1, dq2, dq3)
     k_text = jnp.zeros((1, HD), F32)
     k_all = jnp.zeros((1, HD), F32)
     q_text = jnp.zeros((1, HD), F32)
     q_all = jnp.zeros((1, HD), F32)
+    rows = pl.ds(k * KC, KC)
     for h in range(NH):
         tops = [r[3 * h : 3 * h + 1, :] for r in s_refs]
         top = functools.reduce(jnp.maximum, tops)
@@ -128,40 +137,37 @@
         total = sum(r[3 * h + 1 : 3 * h + 2, :] * e for r, e in zip(s_refs, shares))
         row_dot = sum(r[3 * h + 2 : 3 * h + 3, :] * e for r, e in zip(s_refs, shares)) / total
         log_total = top + jnp.log2(total)
-        wg = wk = None
-        for k in range(NX):
-            rows = pl.ds(k * KC, KC)
-            kn = kn_ref[h, rows, :]
-            s = nt_dot(kn, qn_ref[h]) * SCALE2
-            g = nt_dot(v_ref[h, rows, :], do_ref[h])
-            p = jnp.exp2(s - log_total)
-            low = p.astype(BF16)
-            mixed = (p * g).astype(BF16)
-            gs = (p * (g - row_dot)).astype(BF16)
-            dv = nn_dot(low, do_ref[h])
-            dk = nn_dot(gs, qn_ref[h]) * FACTOR
-            a, b = tn_dot(mixed, kn), tn_dot(low, kn)
-            wg, wk = (a, b) if wg is None else (wg + a, wk + b)
-            for j in range(NZ):
-                part = dk[j * BR : (j + 1) * BR]
-                kv_outs[k][j, 0, h] = part.astype(kv_outs[k].dtype)
-                kv_outs[k][j, 1, h] = dv[j * BR : (j + 1) * BR].astype(kv_outs[k].dtype)
-                unit, _ = unit_and_root(kv_refs[k * NZ + j][0, h])
-                term = part * unit
-                k_all += jnp.sum(term, axis=0, keepdims=True)
-                k_text += jnp.sum(jnp.where(text_mask(kv_block(k, j, place)), term, 0.0), axis=0, keepdims=True)
+        kn = kn_ref[h, rows, :]
+        s = nt_dot(kn, qn_ref[h]) * SCALE2
+        g = nt_dot(v_ref[h, rows, :], do_ref[h])
+        p = jnp.exp2(s - log_total)
+        low = p.astype(BF16)
+        mixed = (p * g).astype(BF16)
+        gs = (p * (g - row_dot)).astype(BF16)
+        dv = nn_dot(low, do_ref[h])
+        dk = nn_dot(gs, qn_ref[h]) * FACTOR
         column = jnp.transpose(jnp.broadcast_to(row_dot, (HD, QR)), (1, 0))
-        dq_all[...] = (wg - column * wk) * FACTOR
-        for slot in range(NQ):
-            part = dq_all[pl.ds(q_offset(slot, place), BR), :]
+        dq = (tn_dot(mixed, kn) - column * tn_dot(low, kn)) * FACTOR
+        dq_ref[h] = dq if first else dq_in[h] + dq
+        for j in range(NZ):
+            part = dk[j * BR : (j + 1) * BR]
+            kv_out[j, 0, h] = part.astype(kv_out.dtype)
+            kv_out[j, 1, h] = dv[j * BR : (j + 1) * BR].astype(kv_out.dtype)
+            unit, _ = unit_and_root(kv_refs[j][0, h])
+            term = part * unit
+            k_all += jnp.sum(term, axis=0, keepdims=True)
+            k_text += jnp.sum(jnp.where(text_mask(kv_block(k, j, place)), term, 0.0), axis=0, keepdims=True)
+        for slot in range(NQ if last else 0):
+            part = dq_ref[h, pl.ds(q_offset(slot, place), BR), :]
             dq_outs[slot][h] = part.astype(dq_outs[slot].dtype)
             unit, _ = unit_and_root(q_refs[slot][0, h])
             term = part * unit
             q_all += jnp.sum(term, axis=0, keepdims=True)
             q_text += jnp.sum(jnp.where(text_mask(q_block(slot, place)), term, 0.0), axis=0, keepdims=True)
-    gain_ref[...] = jnp.concatenate(
+    gains = jnp.concatenate(
         [q_text, q_all - q_text, k_text, k_all - k_text, jnp.zeros((4, HD), F32)], axis=0
     )
+    gain_ref[...] = gains if first else gain_in[...] + gains
 
 
 def pair_sum_kernel(own, r1, r2, r3, keep_ref, send_ref):
@@ -178,11 +184,31 @@
     return (grad - unit * jnp.mean(grad * unit, axis=-1, keepdims=True)) / root
 
 
-def q_out_kernel(own, r1, r2, r3, raw, gain_ref, out):
+def pack_kernel(dq1, dq2, dq3, gain_ref, m1, m2, m3):
+    gains = gain_ref[...]
+    high = gains.astype(BF16)
+    gains = gains - high.astype(F32)
+    middle = gains.astype(BF16)
+    low = (gains - middle.astype(F32)).astype(BF16)
+    tail = jnp.concatenate([high.astype(F32), middle.astype(F32), low.astype(F32), jnp.zeros((8, HD), F32)], axis=0)
+    for dq, out in ((dq1, m1), (dq2, m2), (dq3, m3)):
+        for h in range(NH):
+            out[h * BR : (h + 1) * BR, :] = dq[h]
+        out[NH * BR :, :] = tail.astype(BF16)
+
+
+def q_out_kernel(own, own_gain, r1, r2, r3, raw, gain_ref, out, sums):
     gain = gain_of(text_mask(q_block(0, here())), gain_ref)
     for h in range(NH):
-        grad = own[h] + r1[h].astype(F32) + r2[h].astype(F32) + r3[h].astype(F32)
+        rows = slice(h * BR, (h + 1) * BR)
+        grad = own[h] + r1[rows, :].astype(F32) + r2[rows, :].astype(F32) + r3[rows, :].astype(F32)
         out[h] = back(grad, raw[0, h], gain).astype(BF16)
+
+    def whole(ref):
+        tail = ref[NH * BR :, :].astype(F32)
+        return (tail[0:8] + tail[8:16]) + tail[16:24]
+
+    sums[...] = (own_gain[...] + whole(r1)) + (whole(r2) + whole(r3))
 
 
 def kv_out_kernel(keep, got, raw, gain_ref, k_out, v_out):
@@ -201,7 +227,7 @@
         in_specs=[whole] * len(args),
         out_specs=[whole] * len(outs),
         scratch_shapes=list(scratch),
-        compiler_params=pltpu.CompilerParams(vmem_limit_bytes=48 * 1024 * 1024),
+        compiler_params=pltpu.CompilerParams(vmem_limit_bytes=VMEM_LIMIT),
         cost_estimate=pl.CostEstimate(flops=flops, bytes_accessed=size, transcendentals=0),
     )(*args)
 
@@ -210,28 +236,39 @@
     return lax.ppermute(a, axis, [((i + k) % n, i) for i in range(n)])
 
 
+def swap(a, axis, n, k):
+    return lax.ppermute(a, axis, [(i, i ^ k) for i in range(n)])
+
+
 def give(a, axis, n, k):
     return lax.ppermute(a, axis, [(i, (i + k) % n) for i in range(n)])
 
 
 def summed(a, axis, n):
-    terms = [a] + [lax.ppermute(a, axis, [(i, i ^ k) for i in range(n)]) for k in range(1, n)]
+    terms = [a] + [swap(a, axis, n, k) for k in range(1, n)]
     while len(terms) > 1:
         terms = [terms[i] + terms[i + 1] for i in range(0, len(terms), 2)]
     return terms[0]
 
 
+def after(a, *others):
+    return lax.optimization_barrier((a, *others))[0]
+
+
 def local(q_raw, k_raw, values, out_grad, q_gain, k_gain):
     def heads_first(a):
         return jnp.transpose(a, (1, 0, 2))
 
     kv = jnp.stack([heads_first(k_raw), heads_first(values)])
     qd = jnp.stack([heads_first(q_raw), heads_first(out_grad)])
-    kv_pair = fetch(kv, "zk", NZ, 1)
-    kvs = [kv, kv_pair]
+    pair = fetch(kv, "zk", NZ, 1)
+    kv_x = [fetch(kv, "x", NX, k) for k in range(1, NX)]
+    qd_2 = swap(qd, "zq", NQ, 2)
+    pair, qd_now, *_ = lax.optimization_barrier((pair, qd, qd_2, *kv_x))
+    kvs = [kv, pair]
     for k in range(1, NX):
-        kvs += [fetch(kv, "x", NX, k), fetch(kv_pair, "x", NX, k)]
-    qds = [qd] + [fetch(qd, "zq", NQ, k) for k in range(1, NQ)]
+        kvs += [kv_x[k - 1], fetch(pair, "x", NX, k)]
+    qds = [qd, swap(qd_now, "zq", NQ, 1), qd_2, swap(qd_now, "zq", NQ, 3)]
     tile = NH * QR * KR * HD * 2
     stat, qn, kn, v, do = kernel_call(
         stat_kernel,
@@ -239,28 +276,41 @@
         [*qds, *kvs, q_gain, k_gain],
         flops=2 * tile,
     )
-    stats = [stat] + [fetch(stat, "zq", NQ, k) for k in range(1, NQ)]
+    stats = [stat] + [swap(stat, "zq", NQ, k) for k in range(1, NQ)]
     part = (NH, BR, HD)
     kv_part = (NZ, 2, NH, BR, HD)
-    dq0, dq1, dq2, dq3, kv0, kv1, kv2, kv3, gains = kernel_call(
-        grad_kernel,
-        [(part, F32)] + [(part, BF16)] * 3 + [(kv_part, F32)] + [(kv_part, BF16)] * 3 + [((8, HD), F32)],
-        [*stats, *qds, *kvs, q_gain, k_gain, qn, kn, v, do],
-        scratch=[pltpu.VMEM((QR, HD), F32)],
-        flops=6 * tile,
-    )
-    kv_got = [give(a, "x", NX, k) for k, a in ((1, kv1), (2, kv2), (3, kv3))]
-    dq_got = [give(a, "zq", NQ, k) for k, a in ((1, dq1), (2, dq2), (3, dq3))]
-    gains = summed(gains, "core", 2)
+    whole_dq, gain_part = ((NH, QR, HD), F32), ((8, HD), F32)
+    kv_got, carried = [], []
+    for k in (2, 1, 3, 0):
+        first, last = k == 2, k == 0
+        outs = [(kv_part, F32 if last else BF16)]
+        outs += [(part, F32)] + [(part, BF16)] * 3 if last else [whole_dq]
+        args = [*stats, *kvs[NZ * k : NZ * k + NZ], *(qds if last else ()), qn, kn, v, do, *carried]
+        got = kernel_call(
+            functools.partial(grad_kernel, k, first, last),
+            outs + [gain_part],
+            args,
+            scratch=[pltpu.VMEM((NH, QR, HD), F32)] if last else (),
+            flops=6 * tile // NX,
+        )
+        if last:
+            own, dq0, dq1, dq2, dq3, gains = got
+        else:
+            kv_got.append(give(got[0], "x", NX, k))
+            carried = got[1:]
+    gains = summed(after(gains, kv_got[0]), "core", 2)
     gains = summed(gains, "y", 4)
-    gains = summed(gains, "x", NX)
-    gains = summed(gains, "zk", NZ)
-    gains = summed(gains, "zq", NQ)
+    gains = summed(after(gains, *kv_got), "x", NX)
     keep, send = kernel_call(
-        pair_sum_kernel, [((2, NH, BR, HD), F32), ((2, NH, BR, HD), BF16)], [kv0, *kv_got]
+        pair_sum_kernel, [((2, NH, BR, HD), F32), ((2, NH, BR, HD), BF16)], [own, *kv_got]
     )
     got = fetch(send, "zk", NZ, 1)
-    (q_out,) = kernel_call(q_out_kernel, [(part, BF16)], [dq0, *dq_got, qd, q_gain])
+    gains = after(summed(gains, "zk", NZ), got)
+    messages = kernel_call(pack_kernel, [((MESSAGE, HD), BF16)] * 3, [dq1, dq2, dq3, gains])
+    messages = [swap(a, "zq", NQ, k) for k, a in enumerate(messages, 1)]
+    q_out, gains = kernel_call(
+        q_out_kernel, [(part, BF16), ((8, HD), F32)], [dq0, gains, *messages, qd, q_gain]
+    )
     k_out, v_out = kernel_call(kv_out_kernel, [(part, BF16)] * 2, [keep, got, kv, k_gain])
 
     return (

time: 126 us -> 109 us (0.87); the launches traced: 124 us -> 109 us
  starting transfers between devices: 57.7 us -> 51.7 us
  waiting for transfers between devices: 42.5 us -> 37.8 us
  local copies, waits for them, and re-layouts: 3.59 us -> 0.58 us
  Pallas kernels: 18.4 us -> 16.8 us
    ppermute x11 -> x17, waiting for transfers between devices: 12.7 us -> 32.8 us  [swap(): return lax.ppermute(a, axis, [(i, i ^ k) for i in range(n)])]
    ppermute x14 -> x8, waiting for transfers between devices: 24.7 us -> 5.02 us  [fetch(): return lax.ppermute(a, axis, [((i + k) % n, i) for i in range(n)])]
    ppermute x14 -> x8, starting transfers between devices: 31.6 us -> 13.4 us  [fetch(): return lax.ppermute(a, axis, [((i + k) % n, i) for i in range(n)])]
    ppermute x11 -> x17, starting transfers between devices: 15.2 us -> 33.2 us  [swap(): return lax.ppermute(a, axis, [(i, i ^ k) for i in range(n)])]
    ppermute x6 -> x3, starting transfers between devices: 10.9 us -> 5.17 us  [give(): return lax.ppermute(a, axis, [(i, (i + k) % n) for i in range(n)])]
    ppermute x6 -> x3, waiting for transfers between devices: 5.16 us -> 0.01 us  [give(): return lax.ppermute(a, axis, [(i, (i + k) % n) for i in range(n)])]
    unnamed x14 -> x8, local copies, waits for them, and re-layouts: 3.02 us -> 0.02 us
    pallas_call x5 -> x9, Pallas kernels: 18.4 us -> 16.8 us  [kernel_call(): pl.pallas_call(kernel, out_shape=[jax.ShapeDtypeStruct(s, d) for s, d in...]
  transfers between devices with their start and end apart: 31 -> 28, of which waited for: 15 -> 15; matrix products, arithmetic and copies ran while one was open for 0% -> 0% of each run, Pallas kernels for 1% -> 8%
where the time goes in v2:
time: 109 us
  starting transfers between devices  51.7 us (47%)
  waiting for transfers between devices  37.8 us (35%)
  Pallas kernels  16.8 us (15%)
    ppermute x17, starting transfers between devices, swap(): return lax.ppermute(a, axis, [(i, i ^ k) for i in range(n)])  33.2 us
    ppermute x17, waiting for transfers between devices, swap(): return lax.ppermute(a, axis, [(i, i ^ k) for i in range(n)])  32.8 us
    pallas_call x9, Pallas kernels, kernel_call(): pl.pallas_call(kernel, out_shape=[jax.ShapeDtypeStruct(s, d) for s, d in...  16.8 us
    ppermute x8, starting transfers between devices, fetch(): return lax.ppermute(a, axis, [((i + k) % n, i) for i in range(n)])  13.4 us
    ppermute x3, starting transfers between devices, give(): return lax.ppermute(a, axis, [(i, (i + k) % n) for i in range(n)])  5.17 us
    ppermute x8, waiting for transfers between devices, fetch(): return lax.ppermute(a, axis, [((i + k) % n, i) for i in range(n)])  5.02 us
  transfers between devices with their start and end apart: 28, of which 15 were waited for; matrix products, arithmetic and copies ran while one was open for 0% of the time, Pallas kernels for 8%

profile of v2, /device:TPU:32, one launch (start us, length us, event | category | flops | bytes accessed | tf_op | source)
XLA Modules:
  0.0 108.7 jit_solution(18105010828017948753)
XLA Ops:
  1.7 6.4 %collective-permute-start.1 = (bf16[2,3,144,128]{3,2,1,0:T(8,128)(2,1)S(1)}, bf16[2,3,144,128]{3,2,1,0:T(8,128)(2,1)S(1)}, u32[]{:S(2)}, u32[]{:S(2)}) collective-permute-start(bf16[2,3,144,128]{3,2,1,0:T(8,128)(2,1)S(1)} %pad_maximum_fusion.refs_0_.refs_6_.raw), channel_id=1, source_target_pairs={{0,128},{64,192},{128,0},{192,64},{1,129},{65,193},{129,1},{193,65... | collective-permute-start | bytes 663560 | tf_op jit(solution)/shard_map/ppermute | solution.py:240
  8.1 1.6 %collective-permute-start.4 = (bf16[2,3,144,128]{3,2,1,0:T(8,128)(2,1)S(1)}, bf16[2,3,144,128]{3,2,1,0:T(8,128)(2,1)S(1)}, u32[]{:S(2)}, u32[]{:S(2)}) collective-permute-start(bf16[2,3,144,128]{3,2,1,0:T(8,128)(2,1)S(1)} %pad_maximum_fusion.1.refs_4_.raw), channel_id=1, source_target_pairs={{24,0},{0,8},{8,16},{16,24},{25,1},{1,9},{9,17},{17,25},{26,2},{2,... | collective-permute-start | bytes 663560 | tf_op jit(solution)/shard_map/ppermute | solution.py:236
  9.7 2.7 %collective-permute-start.3 = (bf16[2,3,144,128]{3,2,1,0:T(8,128)(2,1)S(1)}, bf16[2,3,144,128]{3,2,1,0:T(8,128)(2,1)S(1)}, u32[]{:S(2)}, u32[]{:S(2)}) collective-permute-start(bf16[2,3,144,128]{3,2,1,0:T(8,128)(2,1)S(1)} %pad_maximum_fusion.1.refs_4_.raw), channel_id=1, source_target_pairs={{16,0},{24,8},{0,16},{8,24},{17,1},{25,9},{1,17},{9,25},{18,2},{26... | collective-permute-start | bytes 663560 | tf_op jit(solution)/shard_map/ppermute | solution.py:236
  12.4 1.4 %collective-permute-start.2 = (bf16[2,3,144,128]{3,2,1,0:T(8,128)(2,1)S(1)}, bf16[2,3,144,128]{3,2,1,0:T(8,128)(2,1)S(1)}, u32[]{:S(2)}, u32[]{:S(2)}) collective-permute-start(bf16[2,3,144,128]{3,2,1,0:T(8,128)(2,1)S(1)} %pad_maximum_fusion.1.refs_4_.raw), channel_id=1, source_target_pairs={{8,0},{16,8},{24,16},{0,24},{9,1},{17,9},{25,17},{1,25},{10,2},{18... | collective-permute-start | bytes 663560 | tf_op jit(solution)/shard_map/ppermute | solution.py:236
  14.8 4.2 %collective-permute-done.1.refs_2_.refs_8_ = bf16[2,3,144,128]{3,2,1,0:T(8,128)(2,1)S(1)} collective-permute-done((bf16[2,3,144,128]{3,2,1,0:T(8,128)(2,1)S(1)}, bf16[2,3,144,128]{3,2,1,0:T(8,128)(2,1)S(1)}, u32[]{:S(2)}, u32[]{:S(2)}) %collective-permute-start.1) | collective-permute-done | bytes 221216 | tf_op jit(solution)/shard_map/ppermute | solution.py:240
  19.0 2.9 %collective-permute-done.3.refs_8_.refs_4_ = bf16[2,3,144,128]{3,2,1,0:T(8,128)(2,1)S(1)} collective-permute-done((bf16[2,3,144,128]{3,2,1,0:T(8,128)(2,1)S(1)}, bf16[2,3,144,128]{3,2,1,0:T(8,128)(2,1)S(1)}, u32[]{:S(2)}, u32[]{:S(2)}) %collective-permute-start.3) | collective-permute-done | bytes 221216 | tf_op jit(solution)/shard_map/ppermute | solution.py:236
  23.3 2.3 %collective-permute-start.5 = (bf16[2,3,144,128]{3,2,1,0:T(8,128)(2,1)S(1)}, bf16[2,3,144,128]{3,2,1,0:T(8,128)(2,1)S(1)}, u32[]{:S(2)}, u32[]{:S(2)}) collective-permute-start(bf16[2,3,144,128]{3,2,1,0:T(8,128)(2,1)S(1)} %pad_maximum_fusion.refs_0_.refs_6_.raw), channel_id=1, source_target_pairs={{0,64},{64,0},{128,192},{192,128},{1,65},{65,1},{129,193},{193,129... | collective-permute-start | bytes 663560 | tf_op jit(solution)/shard_map/ppermute | solution.py:240
  25.7 1.5 %collective-permute-start.9 = (bf16[2,3,144,128]{3,2,1,0:T(8,128)(2,1)S(1)}, bf16[2,3,144,128]{3,2,1,0:T(8,128)(2,1)S(1)}, u32[]{:S(2)}, u32[]{:S(2)}) collective-permute-start(bf16[2,3,144,128]{3,2,1,0:T(8,128)(2,1)S(1)} %collective-permute-done.refs_5_), channel_id=1, source_target_pairs={{24,0},{0,8},{8,16},{16,24},{25,1},{1,9},{9,17},{17,25},{26,2},{2,... | collective-permute-start | bytes 663560 | tf_op jit(solution)/shard_map/ppermute | solution.py:236
  27.2 2.7 %collective-permute-start.8 = (bf16[2,3,144,128]{3,2,1,0:T(8,128)(2,1)S(1)}, bf16[2,3,144,128]{3,2,1,0:T(8,128)(2,1)S(1)}, u32[]{:S(2)}, u32[]{:S(2)}) collective-permute-start(bf16[2,3,144,128]{3,2,1,0:T(8,128)(2,1)S(1)} %collective-permute-done.refs_5_), channel_id=1, source_target_pairs={{16,0},{24,8},{0,16},{8,24},{17,1},{25,9},{1,17},{9,25},{18,2},{26... | collective-permute-start | bytes 663560 | tf_op jit(solution)/shard_map/ppermute | solution.py:236
  29.9 1.4 %collective-permute-start.7 = (bf16[2,3,144,128]{3,2,1,0:T(8,128)(2,1)S(1)}, bf16[2,3,144,128]{3,2,1,0:T(8,128)(2,1)S(1)}, u32[]{:S(2)}, u32[]{:S(2)}) collective-permute-start(bf16[2,3,144,128]{3,2,1,0:T(8,128)(2,1)S(1)} %collective-permute-done.refs_5_), channel_id=1, source_target_pairs={{8,0},{16,8},{24,16},{0,24},{9,1},{17,9},{25,17},{1,25},{10,2},{18... | collective-permute-start | bytes 663560 | tf_op jit(solution)/shard_map/ppermute | solution.py:236
  31.3 5.8 %collective-permute-done.6.refs_3_.refs_9_ = bf16[2,3,144,128]{3,2,1,0:T(8,128)(2,1)S(1)} collective-permute-done((bf16[2,3,144,128]{3,2,1,0:T(8,128)(2,1)S(1)}, bf16[2,3,144,128]{3,2,1,0:T(8,128)(2,1)S(1)}, u32[]{:S(2)}, u32[]{:S(2)}) %collective-permute-start.6) | collective-permute-done | bytes 221216 | tf_op jit(solution)/shard_map/ppermute | solution.py:240
  38.3 4.9 %shard_map.101 = (f32[16,576]{1,0:T(8,128)S(1)}, bf16[3,576,128]{2,1,0:T(8,128)(2,1)S(1)}, bf16[3,1152,128]{2,1,0:T(8,128)(2,1)S(1)}, bf16[3,1152,128]{2,1,0:T(8,128)(2,1)S(1)}, bf16[3,576,128]{2,1,0:T(8,128)(2,1)S(1)}) custom-call(bf16[2,3,144,128]{3,2,1,0:T(8,128)(2,1)S(1)} %pad_maximum_fusion.refs_0_.refs_6_.raw, ...), custom_call_target="tpu_custom_call" | custom-call | flops 1019215872 | bytes 2656256 | tf_op jit(solution)/shard_map/pallas_call | solution.py:224
  43.2 3.9 %collective-permute-start.12 = (f32[16,576]{1,0:T(8,128)S(1)}, f32[16,576]{1,0:T(8,128)S(1)}, u32[]{:S(2)}, u32[]{:S(2)}) collective-permute-start(f32[16,576]{1,0:T(8,128)S(1)} %get-tuple-element.41.refs_0_), channel_id=1, source_target_pairs={{0,192},{64,128},{128,64},{192,0},{1,193},{65,129},{129,65},{193,1... | collective-permute-start | bytes 110600 | tf_op jit(solution)/shard_map/ppermute | solution.py:240
  48.1 1.7 %collective-permute-start.10 = (f32[16,576]{1,0:T(8,128)S(1)}, f32[16,576]{1,0:T(8,128)S(1)}, u32[]{:S(2)}, u32[]{:S(2)}) collective-permute-start(f32[16,576]{1,0:T(8,128)S(1)} %get-tuple-element.41.refs_0_), channel_id=1, source_target_pairs={{0,64},{64,0},{128,192},{192,128},{1,65},{65,1},{129,193},{193,129... | collective-permute-start | bytes 110600 | tf_op jit(solution)/shard_map/ppermute | solution.py:240
  49.8 5.2 %collective-permute-done.11.refs_2_ = f32[16,576]{1,0:T(8,128)S(1)} collective-permute-done((f32[16,576]{1,0:T(8,128)S(1)}, f32[16,576]{1,0:T(8,128)S(1)}, u32[]{:S(2)}, u32[]{:S(2)}) %collective-permute-start.11) | collective-permute-done | bytes 36896 | tf_op jit(solution)/shard_map/ppermute | solution.py:240
  55.1 2.3 %shard_map.102 = (bf16[2,2,3,144,128]{4,3,2,1,0:T(8,128)(2,1)S(1)}, f32[3,576,128]{2,1,0:T(8,128)S(1)}, f32[8,128]{1,0:T(8,128)S(1)}) custom-call(f32[16,576]{1,0:T(8,128)S(1)} %get-tuple-element.41.refs_0_, f32[16,576]{1,0:T(8,128)S(1)} %collective-permute-done.10.refs_1_, f32[16,576]{1,0:T(8,128)S(1)} %collective-permute-done.11.refs_2_, ...), custom_call_target="tpu_custom_call" | custom-call | flops 764411904 | bytes 3244032 | tf_op jit(solution)/shard_map/pallas_call | solution.py:224
  57.3 3.1 %collective-permute-start.13 = (bf16[2,2,3,144,128]{4,3,2,1,0:T(8,128)(2,1)S(1)}, bf16[2,2,3,144,128]{4,3,2,1,0:T(8,128)(2,1)S(1)}, u32[]{:S(2)}, u32[]{:S(2)}) collective-permute-start(bf16[2,2,3,144,128]{4,3,2,1,0:T(8,128)(2,1)S(1)} %get-tuple-element.54), channel_id=1, source_target_pairs={{0,16},{8,24},{16,0},{24,8},{1,17},{9,25},{17,1},{25,9},{2,18},{10... | collective-permute-start | bytes 1327112 | tf_op jit(solution)/shard_map/ppermute | solution.py:244
  60.4 2.3 %shard_map.103 = (bf16[2,2,3,144,128]{4,3,2,1,0:T(8,128)(2,1)S(1)}, f32[3,576,128]{2,1,0:T(8,128)S(1)}, f32[8,128]{1,0:T(8,128)S(1)}) custom-call(f32[16,576]{1,0:T(8,128)S(1)} %get-tuple-element.41.refs_0_, f32[16,576]{1,0:T(8,128)S(1)} %collective-permute-done.10.refs_1_, f32[16,576]{1,0:T(8,128)S(1)} %collective-permute-done.11.refs_2_, ...), custom_call_target="tpu_custom_call" | custom-call | flops 764411904 | bytes 4132864 | tf_op jit(solution)/shard_map/pallas_call | solution.py:224
  62.7 2.3 %shard_map.104 = (bf16[2,2,3,144,128]{4,3,2,1,0:T(8,128)(2,1)S(1)}, f32[3,576,128]{2,1,0:T(8,128)S(1)}, f32[8,128]{1,0:T(8,128)S(1)}) custom-call(f32[16,576]{1,0:T(8,128)S(1)} %get-tuple-element.41.refs_0_, f32[16,576]{1,0:T(8,128)S(1)} %collective-permute-done.10.refs_1_, f32[16,576]{1,0:T(8,128)S(1)} %collective-permute-done.11.refs_2_, ...), custom_call_target="tpu_custom_call" | custom-call | flops 764411904 | bytes 4132864 | tf_op jit(solution)/shard_map/pallas_call | solution.py:224
  65.0 1.3 %collective-permute-start.19 = (bf16[2,2,3,144,128]{4,3,2,1,0:T(8,128)(2,1)S(1)}, bf16[2,2,3,144,128]{4,3,2,1,0:T(8,128)(2,1)S(1)}, u32[]{:S(2)}, u32[]{:S(2)}) collective-permute-start(bf16[2,2,3,144,128]{4,3,2,1,0:T(8,128)(2,1)S(1)} %get-tuple-element.57), channel_id=1, source_target_pairs={{0,24},{8,0},{16,8},{24,16},{1,25},{9,1},{17,9},{25,17},{2,26},{10... | collective-permute-start | bytes 1327112 | tf_op jit(solution)/shard_map/ppermute | solution.py:244
  67.1 2.9 %shard_map.105 = (f32[2,2,3,144,128]{4,3,2,1,0:T(8,128)S(1)}, f32[3,144,128]{2,1,0:T(8,128)S(1)}, bf16[3,144,128]{2,1,0:T(8,128)(2,1)S(1)}, bf16[3,144,128]{2,1,...) custom-call(f32[16,576]{1,0:T(8,128)S(1)} %get-tuple-element.41.refs_0_, ...), custom_call_target="tpu_custom_call" | custom-call | flops 764411904 | bytes 5017600 | tf_op jit(solution)/shard_map/pallas_call | solution.py:224
  71.5 3.0 %collective-permute-start.17 = (f32[8,128]{1,0:T(8,128)S(1)}, f32[8,128]{1,0:T(8,128)S(1)}, u32[]{:S(2)}, u32[]{:S(2)}) collective-permute-start(f32[8,128]{1,0:T(8,128)S(1)} %add.24), channel_id=1, source_target_pairs={{0,6},{2,4},{4,2},{6,0},{1,7},{3,5},{5,3},{7,1},{8,14},{10,12},{12... | collective-permute-start | bytes 12296 | tf_op jit(solution)/shard_map/ppermute | solution.py:240
  76.3 3.3 %collective-permute-done.16 = f32[8,128]{1,0:T(8,128)S(1)} collective-permute-done((f32[8,128]{1,0:T(8,128)S(1)}, f32[8,128]{1,0:T(8,128)S(1)}, u32[]{:S(2)}, u32[]{:S(2)}) %collective-permute-start.16) | collective-permute-done | bytes 4128 | tf_op jit(solution)/shard_map/ppermute | solution.py:240
  79.6 4.1 %collective-permute-start.22 = (f32[8,128]{1,0:T(8,128)S(1)}, f32[8,128]{1,0:T(8,128)S(1)}, u32[]{:S(2)}, u32[]{:S(2)}) collective-permute-start(f32[8,128]{1,0:T(8,128)S(1)} %add_add_fusion.1), channel_id=1, source_target_pairs={{0,24},{8,16},{16,8},{24,0},{1,25},{9,17},{17,9},{25,1},{2,26},{10... | collective-permute-start | bytes 12296 | tf_op jit(solution)/shard_map/ppermute | solution.py:240
  83.7 1.3 %collective-permute-start.21 = (f32[8,128]{1,0:T(8,128)S(1)}, f32[8,128]{1,0:T(8,128)S(1)}, u32[]{:S(2)}, u32[]{:S(2)}) collective-permute-start(f32[8,128]{1,0:T(8,128)S(1)} %add_add_fusion.1), channel_id=1, source_target_pairs={{0,16},{8,24},{16,0},{24,8},{1,17},{9,25},{17,1},{25,9},{2,18},{10... | collective-permute-start | bytes 12296 | tf_op jit(solution)/shard_map/ppermute | solution.py:240
  86.3 2.6 %collective-permute-done.21 = f32[8,128]{1,0:T(8,128)S(1)} collective-permute-done((f32[8,128]{1,0:T(8,128)S(1)}, f32[8,128]{1,0:T(8,128)S(1)}, u32[]{:S(2)}, u32[]{:S(2)}) %collective-permute-start.21) | collective-permute-done | bytes 4128 | tf_op jit(solution)/shard_map/ppermute | solution.py:240
  89.9 2.7 %collective-permute-done.23 = f32[8,128]{1,0:T(8,128)S(1)} collective-permute-done((f32[8,128]{1,0:T(8,128)S(1)}, f32[8,128]{1,0:T(8,128)S(1)}, u32[]{:S(2)}, u32[]{:S(2)}) %collective-permute-start.23) | collective-permute-done | bytes 4128 | tf_op jit(solution)/shard_map/ppermute | solution.py:240
  92.6 1.8 %collective-permute-start.25 = (bf16[464,128]{1,0:T(8,128)(2,1)S(1)}, bf16[464,128]{1,0:T(8,128)(2,1)S(1)}, u32[]{:S(2)}, u32[]{:S(2)}) collective-permute-start(bf16[464,128]{1,0:T(8,128)(2,1)S(1)} %get-tuple-element.65), channel_id=1, source_target_pairs={{0,64},{64,0},{128,192},{192,128},{1,65},{65,1},{129,193},{193,129... | collective-permute-start | bytes 356360 | tf_op jit(solution)/shard_map/ppermute | solution.py:240
  94.4 3.2 %collective-permute-start.26 = (bf16[464,128]{1,0:T(8,128)(2,1)S(1)}, bf16[464,128]{1,0:T(8,128)(2,1)S(1)}, u32[]{:S(2)}, u32[]{:S(2)}) collective-permute-start(bf16[464,128]{1,0:T(8,128)(2,1)S(1)} %get-tuple-element.66), channel_id=1, source_target_pairs={{0,128},{64,192},{128,0},{192,64},{1,129},{65,193},{129,1},{193,65... | collective-permute-start | bytes 356360 | tf_op jit(solution)/shard_map/ppermute | solution.py:240
  97.6 1.6 %collective-permute-start.27 = (bf16[464,128]{1,0:T(8,128)(2,1)S(1)}, bf16[464,128]{1,0:T(8,128)(2,1)S(1)}, u32[]{:S(2)}, u32[]{:S(2)}) collective-permute-start(bf16[464,128]{1,0:T(8,128)(2,1)S(1)} %get-tuple-element.67), channel_id=1, source_target_pairs={{0,192},{64,128},{128,64},{192,0},{1,193},{65,129},{129,65},{193,1... | collective-permute-start | bytes 356360 | tf_op jit(solution)/shard_map/ppermute | solution.py:240
  100.8 4.1 %collective-permute-done.26.r2 = bf16[464,128]{1,0:T(8,128)(2,1)S(1)} collective-permute-done((bf16[464,128]{1,0:T(8,128)(2,1)S(1)}, bf16[464,128]{1,0:T(8,128)(2,1)S(1)}, u32[]{:S(2)}, u32[]{:S(2)}) %collective-permute-start.26) | collective-permute-done | bytes 118816 | tf_op jit(solution)/shard_map/ppermute | solution.py:240
  104.8 2.4 %collective-permute-done.27.r3 = bf16[464,128]{1,0:T(8,128)(2,1)S(1)} collective-permute-done((bf16[464,128]{1,0:T(8,128)(2,1)S(1)}, bf16[464,128]{1,0:T(8,128)(2,1)S(1)}, u32[]{:S(2)}, u32[]{:S(2)}) %collective-permute-start.27) | collective-permute-done | bytes 118816 | tf_op jit(solution)/shard_map/ppermute | solution.py:240
  (48 shorter events, 15.0 us)
Async XLA Ops:
  0.6 7.4 %copy-start.2 = (bf16[144,3,128]{2,0,1:T(8,128)(2,1)S(1)}, bf16[144,3,128]{2,0,1:T(8,128)(2,1)}, u32[]{:S(2)}) copy-start(bf16[144,3,128]{2,0,1:T(8,128)(2,1)} %param.8) | copy-start | bytes 331780
  0.6 7.4 %copy-start.3 = (bf16[144,3,128]{2,0,1:T(8,128)(2,1)S(1)}, bf16[144,3,128]{2,0,1:T(8,128)(2,1)}, u32[]{:S(2)}) copy-start(bf16[144,3,128]{2,0,1:T(8,128)(2,1)} %param.7) | copy-start | bytes 331780
  1.7 17.4 %collective-permute-start.1 = (bf16[2,3,144,128]{3,2,1,0:T(8,128)(2,1)S(1)}, bf16[2,3,144,128]{3,2,1,0:T(8,128)(2,1)S(1)}, u32[]{:S(2)}, u32[]{:S(2)}) collective-permute-start(bf16[2,3,144,128]{3,2,1,0:T(8,128)(2,1)S(1)} %pad_maximum_fusion.refs_0_.refs_6_.raw), channel_id=1, source_target_pairs={{0,128},{64,192},{128,0},{192,64},{1,129},{65,193},{129,1},{193,65... | collective-permute-start | bytes 663560 | tf_op jit(solution)/shard_map/ppermute | solution.py:240
  8.0 30.2 %copy-start = (f32[2,128]{1,0:T(2,128)S(1)}, f32[2,128]{1,0:T(2,128)}, u32[]{:S(2)}) copy-start(f32[2,128]{1,0:T(2,128)} %gain_ref.2) | copy-start | bytes 3076
  8.1 30.2 %copy-start.1 = (f32[2,128]{1,0:T(2,128)S(1)}, f32[2,128]{1,0:T(2,128)}, u32[]{:S(2)}) copy-start(f32[2,128]{1,0:T(2,128)} %gain_ref.3) | copy-start | bytes 3076
  8.1 11.0 %collective-permute-start.4 = (bf16[2,3,144,128]{3,2,1,0:T(8,128)(2,1)S(1)}, bf16[2,3,144,128]{3,2,1,0:T(8,128)(2,1)S(1)}, u32[]{:S(2)}, u32[]{:S(2)}) collective-permute-start(bf16[2,3,144,128]{3,2,1,0:T(8,128)(2,1)S(1)} %pad_maximum_fusion.1.refs_4_.raw), channel_id=1, source_target_pairs={{24,0},{0,8},{8,16},{16,24},{25,1},{1,9},{9,17},{17,25},{26,2},{2,... | collective-permute-start | bytes 663560 | tf_op jit(solution)/shard_map/ppermute | solution.py:236
  9.7 12.3 %collective-permute-start.3 = (bf16[2,3,144,128]{3,2,1,0:T(8,128)(2,1)S(1)}, bf16[2,3,144,128]{3,2,1,0:T(8,128)(2,1)S(1)}, u32[]{:S(2)}, u32[]{:S(2)}) collective-permute-start(bf16[2,3,144,128]{3,2,1,0:T(8,128)(2,1)S(1)} %pad_maximum_fusion.1.refs_4_.raw), channel_id=1, source_target_pairs={{16,0},{24,8},{0,16},{8,24},{17,1},{25,9},{1,17},{9,25},{18,2},{26... | collective-permute-start | bytes 663560 | tf_op jit(solution)/shard_map/ppermute | solution.py:236
  12.4 9.6 %collective-permute-start.2 = (bf16[2,3,144,128]{3,2,1,0:T(8,128)(2,1)S(1)}, bf16[2,3,144,128]{3,2,1,0:T(8,128)(2,1)S(1)}, u32[]{:S(2)}, u32[]{:S(2)}) collective-permute-start(bf16[2,3,144,128]{3,2,1,0:T(8,128)(2,1)S(1)} %pad_maximum_fusion.1.refs_4_.raw), channel_id=1, source_target_pairs={{8,0},{16,8},{24,16},{0,24},{9,1},{17,9},{25,17},{1,25},{10,2},{18... | collective-permute-start | bytes 663560 | tf_op jit(solution)/shard_map/ppermute | solution.py:236
  13.8 9.1 %collective-permute-start = (bf16[2,3,144,128]{3,2,1,0:T(8,128)(2,1)S(1)}, bf16[2,3,144,128]{3,2,1,0:T(8,128)(2,1)S(1)}, u32[]{:S(2)}, u32[]{:S(2)}) collective-permute-start(bf16[2,3,144,128]{3,2,1,0:T(8,128)(2,1)S(1)} %pad_maximum_fusion.1.refs_4_.raw), channel_id=1, source_target_pairs={{32,0},{0,32},{33,1},{1,33},{34,2},{2,34},{35,3},{3,35},{36,4},{4,... | collective-permute-start | bytes 663560 | tf_op jit(solution)/shard_map/ppermute | solution.py:236
  22.9 14.2 %collective-permute-start.6 = (bf16[2,3,144,128]{3,2,1,0:T(8,128)(2,1)S(1)}, bf16[2,3,144,128]{3,2,1,0:T(8,128)(2,1)S(1)}, u32[]{:S(2)}, u32[]{:S(2)}) collective-permute-start(bf16[2,3,144,128]{3,2,1,0:T(8,128)(2,1)S(1)} %pad_maximum_fusion.refs_0_.refs_6_.raw), channel_id=1, source_target_pairs={{0,192},{64,128},{128,64},{192,0},{1,193},{65,129},{129,65},{193,1... | collective-permute-start | bytes 663560 | tf_op jit(solution)/shard_map/ppermute | solution.py:240
  23.3 13.8 %collective-permute-start.5 = (bf16[2,3,144,128]{3,2,1,0:T(8,128)(2,1)S(1)}, bf16[2,3,144,128]{3,2,1,0:T(8,128)(2,1)S(1)}, u32[]{:S(2)}, u32[]{:S(2)}) collective-permute-start(bf16[2,3,144,128]{3,2,1,0:T(8,128)(2,1)S(1)} %pad_maximum_fusion.refs_0_.refs_6_.raw), channel_id=1, source_target_pairs={{0,64},{64,0},{128,192},{192,128},{1,65},{65,1},{129,193},{193,129... | collective-permute-start | bytes 663560 | tf_op jit(solution)/shard_map/ppermute | solution.py:240
  25.7 11.5 %collective-permute-start.9 = (bf16[2,3,144,128]{3,2,1,0:T(8,128)(2,1)S(1)}, bf16[2,3,144,128]{3,2,1,0:T(8,128)(2,1)S(1)}, u32[]{:S(2)}, u32[]{:S(2)}) collective-permute-start(bf16[2,3,144,128]{3,2,1,0:T(8,128)(2,1)S(1)} %collective-permute-done.refs_5_), channel_id=1, source_target_pairs={{24,0},{0,8},{8,16},{16,24},{25,1},{1,9},{9,17},{17,25},{26,2},{2,... | collective-permute-start | bytes 663560 | tf_op jit(solution)/shard_map/ppermute | solution.py:236
  27.2 11.1 %collective-permute-start.8 = (bf16[2,3,144,128]{3,2,1,0:T(8,128)(2,1)S(1)}, bf16[2,3,144,128]{3,2,1,0:T(8,128)(2,1)S(1)}, u32[]{:S(2)}, u32[]{:S(2)}) collective-permute-start(bf16[2,3,144,128]{3,2,1,0:T(8,128)(2,1)S(1)} %collective-permute-done.refs_5_), channel_id=1, source_target_pairs={{16,0},{24,8},{0,16},{8,24},{17,1},{25,9},{1,17},{9,25},{18,2},{26... | collective-permute-start | bytes 663560 | tf_op jit(solution)/shard_map/ppermute | solution.py:236
  29.9 8.4 %collective-permute-start.7 = (bf16[2,3,144,128]{3,2,1,0:T(8,128)(2,1)S(1)}, bf16[2,3,144,128]{3,2,1,0:T(8,128)(2,1)S(1)}, u32[]{:S(2)}, u32[]{:S(2)}) collective-permute-start(bf16[2,3,144,128]{3,2,1,0:T(8,128)(2,1)S(1)} %collective-permute-done.refs_5_), channel_id=1, source_target_pairs={{8,0},{16,8},{24,16},{0,24},{9,1},{17,9},{25,17},{1,25},{10,2},{18... | collective-permute-start | bytes 663560 | tf_op jit(solution)/shard_map/ppermute | solution.py:236
  43.2 6.6 %collective-permute-start.12 = (f32[16,576]{1,0:T(8,128)S(1)}, f32[16,576]{1,0:T(8,128)S(1)}, u32[]{:S(2)}, u32[]{:S(2)}) collective-permute-start(f32[16,576]{1,0:T(8,128)S(1)} %get-tuple-element.41.refs_0_), channel_id=1, source_target_pairs={{0,192},{64,128},{128,64},{192,0},{1,193},{65,129},{129,65},{193,1... | collective-permute-start | bytes 110600 | tf_op jit(solution)/shard_map/ppermute | solution.py:240
  47.1 7.9 %collective-permute-start.11 = (f32[16,576]{1,0:T(8,128)S(1)}, f32[16,576]{1,0:T(8,128)S(1)}, u32[]{:S(2)}, u32[]{:S(2)}) collective-permute-start(f32[16,576]{1,0:T(8,128)S(1)} %get-tuple-element.41.refs_0_), channel_id=1, source_target_pairs={{0,128},{64,192},{128,0},{192,64},{1,129},{65,193},{129,1},{193,65... | collective-permute-start | bytes 110600 | tf_op jit(solution)/shard_map/ppermute | solution.py:240
  48.1 7.0 %collective-permute-start.10 = (f32[16,576]{1,0:T(8,128)S(1)}, f32[16,576]{1,0:T(8,128)S(1)}, u32[]{:S(2)}, u32[]{:S(2)}) collective-permute-start(f32[16,576]{1,0:T(8,128)S(1)} %get-tuple-element.41.refs_0_), channel_id=1, source_target_pairs={{0,64},{64,0},{128,192},{192,128},{1,65},{65,1},{129,193},{193,129... | collective-permute-start | bytes 110600 | tf_op jit(solution)/shard_map/ppermute | solution.py:240
  57.3 12.7 %collective-permute-start.13 = (bf16[2,2,3,144,128]{4,3,2,1,0:T(8,128)(2,1)S(1)}, bf16[2,2,3,144,128]{4,3,2,1,0:T(8,128)(2,1)S(1)}, u32[]{:S(2)}, u32[]{:S(2)}) collective-permute-start(bf16[2,2,3,144,128]{4,3,2,1,0:T(8,128)(2,1)S(1)} %get-tuple-element.54), channel_id=1, source_target_pairs={{0,16},{8,24},{16,0},{24,8},{1,17},{9,25},{17,1},{25,9},{2,18},{10... | collective-permute-start | bytes 1327112 | tf_op jit(solution)/shard_map/ppermute | solution.py:244
  65.0 14.6 %collective-permute-start.19 = (bf16[2,2,3,144,128]{4,3,2,1,0:T(8,128)(2,1)S(1)}, bf16[2,2,3,144,128]{4,3,2,1,0:T(8,128)(2,1)S(1)}, u32[]{:S(2)}, u32[]{:S(2)}) collective-permute-start(bf16[2,2,3,144,128]{4,3,2,1,0:T(8,128)(2,1)S(1)} %get-tuple-element.57), channel_id=1, source_target_pairs={{0,24},{8,0},{16,8},{24,16},{1,25},{9,1},{17,9},{25,17},{2,26},{10... | collective-permute-start | bytes 1327112 | tf_op jit(solution)/shard_map/ppermute | solution.py:244
  66.3 13.3 %collective-permute-start.18 = (bf16[2,2,3,144,128]{4,3,2,1,0:T(8,128)(2,1)S(1)}, bf16[2,2,3,144,128]{4,3,2,1,0:T(8,128)(2,1)S(1)}, u32[]{:S(2)}, u32[]{:S(2)}) collective-permute-start(bf16[2,2,3,144,128]{4,3,2,1,0:T(8,128)(2,1)S(1)} %get-tuple-element.56), channel_id=1, source_target_pairs={{0,8},{8,16},{16,24},{24,0},{1,9},{9,17},{17,25},{25,1},{2,10},{10... | collective-permute-start | bytes 1327112 | tf_op jit(solution)/shard_map/ppermute | solution.py:244
  70.0 1.5 %collective-permute-start.14 = (f32[8,128]{1,0:T(8,128)S(1)}, f32[8,128]{1,0:T(8,128)S(1)}, u32[]{:S(2)}, u32[]{:S(2)}) collective-permute-start(f32[8,128]{1,0:T(8,128)S(1)} %get-tuple-element.55), channel_id=1, source_target_pairs={{0,1},{1,0},{2,3},{3,2},{4,5},{5,4},{6,7},{7,6},{8,9},{9,8},{10,11... | collective-permute-start | bytes 12296 | tf_op jit(solution)/shard_map/ppermute | solution.py:240
  71.5 4.8 %collective-permute-start.17 = (f32[8,128]{1,0:T(8,128)S(1)}, f32[8,128]{1,0:T(8,128)S(1)}, u32[]{:S(2)}, u32[]{:S(2)}) collective-permute-start(f32[8,128]{1,0:T(8,128)S(1)} %add.24), channel_id=1, source_target_pairs={{0,6},{2,4},{4,2},{6,0},{1,7},{3,5},{5,3},{7,1},{8,14},{10,12},{12... | collective-permute-start | bytes 12296 | tf_op jit(solution)/shard_map/ppermute | solution.py:240
  74.5 5.1 %collective-permute-start.16 = (f32[8,128]{1,0:T(8,128)S(1)}, f32[8,128]{1,0:T(8,128)S(1)}, u32[]{:S(2)}, u32[]{:S(2)}) collective-permute-start(f32[8,128]{1,0:T(8,128)S(1)} %add.24), channel_id=1, source_target_pairs={{0,4},{2,6},{4,0},{6,2},{1,5},{3,7},{5,1},{7,3},{8,12},{10,14},{12... | collective-permute-start | bytes 12296 | tf_op jit(solution)/shard_map/ppermute | solution.py:240
  75.1 4.5 %collective-permute-start.15 = (f32[8,128]{1,0:T(8,128)S(1)}, f32[8,128]{1,0:T(8,128)S(1)}, u32[]{:S(2)}, u32[]{:S(2)}) collective-permute-start(f32[8,128]{1,0:T(8,128)S(1)} %add.24), channel_id=1, source_target_pairs={{0,2},{2,0},{4,6},{6,4},{1,3},{3,1},{5,7},{7,5},{8,10},{10,8},{12,... | collective-permute-start | bytes 12296 | tf_op jit(solution)/shard_map/ppermute | solution.py:240
  79.6 6.6 %collective-permute-start.22 = (f32[8,128]{1,0:T(8,128)S(1)}, f32[8,128]{1,0:T(8,128)S(1)}, u32[]{:S(2)}, u32[]{:S(2)}) collective-permute-start(f32[8,128]{1,0:T(8,128)S(1)} %add_add_fusion.1), channel_id=1, source_target_pairs={{0,24},{8,16},{16,8},{24,0},{1,25},{9,17},{17,9},{25,1},{2,26},{10... | collective-permute-start | bytes 12296 | tf_op jit(solution)/shard_map/ppermute | solution.py:240
  83.7 5.1 %collective-permute-start.21 = (f32[8,128]{1,0:T(8,128)S(1)}, f32[8,128]{1,0:T(8,128)S(1)}, u32[]{:S(2)}, u32[]{:S(2)}) collective-permute-start(f32[8,128]{1,0:T(8,128)S(1)} %add_add_fusion.1), channel_id=1, source_target_pairs={{0,16},{8,24},{16,0},{24,8},{1,17},{9,25},{17,1},{25,9},{2,18},{10... | collective-permute-start | bytes 12296 | tf_op jit(solution)/shard_map/ppermute | solution.py:240
  85.1 3.8 %collective-permute-start.20 = (f32[8,128]{1,0:T(8,128)S(1)}, f32[8,128]{1,0:T(8,128)S(1)}, u32[]{:S(2)}, u32[]{:S(2)}) collective-permute-start(f32[8,128]{1,0:T(8,128)S(1)} %add_add_fusion.1), channel_id=1, source_target_pairs={{0,8},{8,0},{16,24},{24,16},{1,9},{9,1},{17,25},{25,17},{2,10},{10... | collective-permute-start | bytes 12296 | tf_op jit(solution)/shard_map/ppermute | solution.py:240
  85.3 7.3 %collective-permute-start.24 = (bf16[2,3,144,128]{3,2,1,0:T(8,128)(2,1)S(1)}, bf16[2,3,144,128]{3,2,1,0:T(8,128)(2,1)S(1)}, u32[]{:S(2)}, u32[]{:S(2)}) collective-permute-start(bf16[2,3,144,128]{3,2,1,0:T(8,128)(2,1)S(1)} %get-tuple-element.60), channel_id=1, source_target_pairs={{32,0},{0,32},{33,1},{1,33},{34,2},{2,34},{35,3},{3,35},{36,4},{4,... | collective-permute-start | bytes 663560 | tf_op jit(solution)/shard_map/ppermute | solution.py:236
  88.8 3.7 %collective-permute-start.23 = (f32[8,128]{1,0:T(8,128)S(1)}, f32[8,128]{1,0:T(8,128)S(1)}, u32[]{:S(2)}, u32[]{:S(2)}) collective-permute-start(f32[8,128]{1,0:T(8,128)S(1)} %add_add_fusion), channel_id=1, source_target_pairs={{0,32},{32,0},{1,33},{33,1},{2,34},{34,2},{3,35},{35,3},{4,36},{36... | collective-permute-start | bytes 12296 | tf_op jit(solution)/shard_map/ppermute | solution.py:240
  92.6 8.1 %collective-permute-start.25 = (bf16[464,128]{1,0:T(8,128)(2,1)S(1)}, bf16[464,128]{1,0:T(8,128)(2,1)S(1)}, u32[]{:S(2)}, u32[]{:S(2)}) collective-permute-start(bf16[464,128]{1,0:T(8,128)(2,1)S(1)} %get-tuple-element.65), channel_id=1, source_target_pairs={{0,64},{64,0},{128,192},{192,128},{1,65},{65,1},{129,193},{193,129... | collective-permute-start | bytes 356360 | tf_op jit(solution)/shard_map/ppermute | solution.py:240
  94.4 10.4 %collective-permute-start.26 = (bf16[464,128]{1,0:T(8,128)(2,1)S(1)}, bf16[464,128]{1,0:T(8,128)(2,1)S(1)}, u32[]{:S(2)}, u32[]{:S(2)}) collective-permute-start(bf16[464,128]{1,0:T(8,128)(2,1)S(1)} %get-tuple-element.66), channel_id=1, source_target_pairs={{0,128},{64,192},{128,0},{192,64},{1,129},{65,193},{129,1},{193,65... | collective-permute-start | bytes 356360 | tf_op jit(solution)/shard_map/ppermute | solution.py:240
  97.6 9.6 %collective-permute-start.27 = (bf16[464,128]{1,0:T(8,128)(2,1)S(1)}, bf16[464,128]{1,0:T(8,128)(2,1)S(1)}, u32[]{:S(2)}, u32[]{:S(2)}) collective-permute-start(bf16[464,128]{1,0:T(8,128)(2,1)S(1)} %get-tuple-element.67), channel_id=1, source_target_pairs={{0,192},{64,128},{128,64},{192,0},{1,193},{65,129},{129,65},{193,1... | collective-permute-start | bytes 356360 | tf_op jit(solution)/shard_map/ppermute | solution.py:240

commit v3 on v2

v3 whole, which is shorter than its diff:
```python
import functools
import math

import jax
import jax.numpy as jnp
from jax import lax
from jax.experimental import pallas as pl
from jax.experimental.pallas import tpu as pltpu
from jax.sharding import Mesh
from jax.sharding import PartitionSpec as P

TXT = 512
EPS = 1e-06
NH, HD, BR = 3, 128, 144
NQ, NX, NZ = 4, 4, 2
QR = NQ * BR
KC = NZ * BR
KR = NX * KC
FACTOR = 1.0 / math.sqrt(HD)
SCALE2 = FACTOR * math.log2(math.e)
F32, BF16 = jnp.float32, jnp.bfloat16
VMEM_LIMIT = 24 * 1024 * 1024
MESSAGE = NH * BR + 32
ALL_ROWS = ("zk", "zq", "x")


def nt_dot(a, b):
    return lax.dot_general(a, b, (((1,), (1,)), ((), ())), preferred_element_type=F32)


def nn_dot(a, b):
    return lax.dot_general(a, b, (((1,), (0,)), ((), ())), preferred_element_type=F32)


def tn_dot(a, b):
    return lax.dot_general(a, b, (((0,), (0,)), ((), ())), preferred_element_type=F32)


def text_mask(block):
    row = block * BR + lax.broadcasted_iota(jnp.int32, (BR, 1), 0)
    return row < TXT


def unit_and_root(raw):
    wide = raw.astype(F32)
    root = jnp.sqrt(jnp.mean(wide * wide, axis=-1, keepdims=True) + EPS)
    return wide * (1.0 / root), root


def gain_of(mask, gain_ref):
    return jnp.where(mask, gain_ref[0:1, :], gain_ref[1:2, :])


def here():
    return lax.axis_index("zq"), lax.axis_index("zk"), lax.axis_index("x")


def q_block(slot, place):
    zq, zk, x = place
    return (NQ * zk + (zq ^ slot)) * NX + x


def kv_block(xslot, j, place):
    zq, zk, x = place
    z = NQ * zk + zq
    return ((NQ * NZ - 1 - z) if j else z) * NX + lax.rem(x + xslot, NX)


def q_offset(slot, place):
    return pl.multiple_of((place[0] ^ slot) * BR, 16)


def place_keys(refs, j, gk_ref, kn_ref, v_ref):
    for k in range(NX):
        gain = gain_of(text_mask(kv_block(k, j, here())), gk_ref)
        rows = pl.ds(k * BR, BR)
        for h in range(NH):
            unit, _ = unit_and_root(refs[k][0, h])
            kn_ref[h, rows, :] = (unit * gain).astype(BF16)
            v_ref[h, rows, :] = refs[k][1, h]


def fold_stats(qn_ref, do_ref, kn_ref, v_ref, before_ref, stat_ref):
    for h in range(NH):
        top = total = dot = None
        if before_ref is not None:
            top, total, dot = [before_ref[3 * h + i : 3 * h + i + 1, :] for i in range(3)]
        for at in range(0, NX * BR, KC):
            rows = pl.ds(at, KC)
            s = nt_dot(kn_ref[h, rows, :], qn_ref[h]) * SCALE2
            g = nt_dot(v_ref[h, rows, :], do_ref[h])
            peak = jnp.max(s, axis=0, keepdims=True)
            new = peak if top is None else jnp.maximum(top, peak)
            w = jnp.exp2(s - new)
            part = jnp.sum(w, axis=0, keepdims=True)
            dpart = jnp.sum(w * g, axis=0, keepdims=True)
            if top is None:
                total, dot = part, dpart
            else:
                keep = jnp.exp2(top - new)
                total, dot = total * keep + part, dot * keep + dpart
            top = new
        stat_ref[3 * h : 3 * h + 1, :] = top
        stat_ref[3 * h + 1 : 3 * h + 2, :] = total
        stat_ref[3 * h + 2 : 3 * h + 3, :] = dot


def own_stat_kernel(q0, q1, q2, q3, kv0, kv1, kv2, kv3, gq_ref, gk_ref, stat_ref, qn_ref, do_ref, kn_ref, v_ref):
    place = here()
    for slot, ref in enumerate((q0, q1, q2, q3)):
        gain = gain_of(text_mask(q_block(slot, place)), gq_ref)
        rows = pl.ds(q_offset(slot, place), BR)
        for h in range(NH):
            unit, _ = unit_and_root(ref[0, h])
            qn_ref[h, rows, :] = (unit * gain).astype(BF16)
            do_ref[h, rows, :] = ref[1, h]
    place_keys((kv0, kv1, kv2, kv3), 0, gk_ref, kn_ref, v_ref)
    stat_ref[...] = jnp.zeros_like(stat_ref)
    fold_stats(qn_ref, do_ref, kn_ref, v_ref, None, stat_ref)


def pair_stat_kernel(before_ref, qn_ref, do_ref, kv0, kv1, kv2, kv3, gk_ref, stat_ref, kn_ref, v_ref):
    place_keys((kv0, kv1, kv2, kv3), 1, gk_ref, kn_ref, v_ref)
    stat_ref[...] = jnp.zeros_like(stat_ref)
    fold_stats(qn_ref, do_ref, kn_ref, v_ref, before_ref, stat_ref)


def in_three(sums):
    high = sums.astype(BF16).astype(F32)
    middle = (sums - high).astype(BF16).astype(F32)
    low = ((sums - high) - middle).astype(BF16).astype(F32)
    tail = jnp.concatenate([high, middle, low, jnp.zeros_like(sums)], axis=0).astype(BF16)
    return tail, (high + middle) + low


def grad_kernel(k, first, last, *refs):
    s_refs, refs = refs[:NQ], refs[NQ:]
    kv_refs, refs = refs[:NZ], refs[NZ:]
    q_refs, refs = (refs[:NQ], refs[NQ:]) if last else ((), refs)
    qn_ref, do_ref, kn_own, v_own, kn_pair, v_pair, *refs = refs
    if first:
        kv_out, dq_ref, gain_ref = refs
    elif last:
        dq_in, gain_in, kv_out, dq_own, *messages, gain_ref, dq_ref = refs
    else:
        dq_in, gain_in, kv_out, dq_ref, gain_ref = refs
    place = here()
    k_text = jnp.zeros((1, HD), F32)
    k_all = jnp.zeros((1, HD), F32)
    q_text = jnp.zeros((1, HD), F32)
    q_all = jnp.zeros((1, HD), F32)
    rows = pl.ds(k * BR, BR)
    for h in range(NH):
        tops = [r[3 * h : 3 * h + 1, :] for r in s_refs]
        top = functools.reduce(jnp.maximum, tops)
        shares = [jnp.exp2(t - top) for t in tops]
        total = sum(r[3 * h + 1 : 3 * h + 2, :] * e for r, e in zip(s_refs, shares))
        row_dot = sum(r[3 * h + 2 : 3 * h + 3, :] * e for r, e in zip(s_refs, shares)) / total
        log_total = top + jnp.log2(total)
        kn = jnp.concatenate([kn_own[h, rows, :], kn_pair[h, rows, :]], axis=0)
        v = jnp.concatenate([v_own[h, rows, :], v_pair[h, rows, :]], axis=0)
        s = nt_dot(kn, qn_ref[h]) * SCALE2
        g = nt_dot(v, do_ref[h])
        p = jnp.exp2(s - log_total)
        low = p.astype(BF16)
        mixed = (p * g).astype(BF16)
        gs = (p * (g - row_dot)).astype(BF16)
        dv = nn_dot(low, do_ref[h])
        dk = nn_dot(gs, qn_ref[h]) * FACTOR
        dq = (tn_dot(kn, mixed) - row_dot * tn_dot(kn, low)) * FACTOR
        dq = jnp.transpose(dq, (1, 0))
        dq_ref[h] = dq if first else dq_in[h] + dq
        for j in range(NZ):
            part = dk[j * BR : (j + 1) * BR]
            kv_out[j, 0, h] = part.astype(kv_out.dtype)
            kv_out[j, 1, h] = dv[j * BR : (j + 1) * BR].astype(kv_out.dtype)
            unit, _ = unit_and_root(kv_refs[j][0, h])
            term = part * unit
            k_all += jnp.sum(term, axis=0, keepdims=True)
            k_text += jnp.sum(jnp.where(text_mask(kv_block(k, j, place)), term, 0.0), axis=0, keepdims=True)
        for slot in range(NQ if last else 0):
            part = dq_ref[h, pl.ds(q_offset(slot, place), BR), :]
            if slot == 0:
                dq_own[h] = part
            else:
                messages[slot - 1][h * BR : (h + 1) * BR, :] = part.astype(BF16)
            unit, _ = unit_and_root(q_refs[slot][0, h])
            term = part * unit
            q_all += jnp.sum(term, axis=0, keepdims=True)
            q_text += jnp.sum(jnp.where(text_mask(q_block(slot, place)), term, 0.0), axis=0, keepdims=True)
    gains = jnp.concatenate(
        [q_text, q_all - q_text, k_text, k_all - k_text, jnp.zeros((4, HD), F32)], axis=0
    )
    gains = gains if first else gain_in[...] + gains
    if last:
        tail, gains = in_three(gains)
        for out in messages:
            out[NH * BR :, :] = tail
    gain_ref[...] = gains


def pair_sum_kernel(own, r1, r2, r3, keep_ref, send_k, send_v):
    def total(j, i):
        return own[j, i] + r1[j, i].astype(F32) + r2[j, i].astype(F32) + r3[j, i].astype(F32)

    for i, send in ((0, send_k), (1, send_v)):
        send[...] = total(1, i).astype(BF16)
        keep_ref[i] = total(0, i)


def back(grad, raw, gain):
    unit, root = unit_and_root(raw)
    grad = grad * gain
    return (grad - unit * jnp.mean(grad * unit, axis=-1, keepdims=True)) * (1.0 / root)


def q_out_kernel(own, own_gain, r1, r2, r3, raw, gain_ref, out, sums):
    gain = gain_of(text_mask(q_block(0, here())), gain_ref)
    for h in range(NH):
        rows = slice(h * BR, (h + 1) * BR)
        grad = own[h] + r1[rows, :].astype(F32) + r2[rows, :].astype(F32) + r3[rows, :].astype(F32)
        out[h] = back(grad, raw[0, h], gain).astype(BF16)

    def whole(ref):
        tail = ref[NH * BR :, :].astype(F32)
        return (tail[0:8] + tail[8:16]) + tail[16:24]

    sums[...] = (own_gain[...] + whole(r1)) + (whole(r2) + whole(r3))


def kv_out_kernel(keep, got_k, got_v, raw, gain_ref, k_out, v_out):
    gain = gain_of(text_mask(q_block(0, here())), gain_ref)
    for h in range(NH):
        k_out[h] = back(keep[0, h] + got_k[h].astype(F32), raw[0, h], gain).astype(BF16)
        v_out[h] = (keep[1, h] + got_v[h].astype(F32)).astype(BF16)


def kernel_call(kernel, outs, args, scratch=(), flops=0):
    whole = pl.BlockSpec(memory_space=pltpu.VMEM)
    size = sum(a.size * a.dtype.itemsize for a in args)
    return pl.pallas_call(
        kernel,
        out_shape=[jax.ShapeDtypeStruct(s, d) for s, d in outs],
        in_specs=[whole] * len(args),
        out_specs=[whole] * len(outs),
        scratch_shapes=list(scratch),
        compiler_params=pltpu.CompilerParams(vmem_limit_bytes=VMEM_LIMIT),
        cost_estimate=pl.CostEstimate(flops=flops, bytes_accessed=size, transcendentals=0),
    )(*args)


def fetch(a, axis, n, k):
    return lax.ppermute(a, axis, [((i + k) % n, i) for i in range(n)])


def swap(a, axis, n, k):
    return lax.ppermute(a, axis, [(i, i ^ k) for i in range(n)])


def give(a, axis, n, k):
    return lax.ppermute(a, axis, [(i, (i + k) % n) for i in range(n)])


def mirror(a):
    n = NZ * NQ
    return lax.ppermute(a, ("zk", "zq"), [(i, n - 1 - i) for i in range(n)])


def summed(a, axis, n, *others):
    terms = [a] + [swap(a, axis, n, k) for k in range(1, n)]
    terms = lax.optimization_barrier((*terms, *others))[:n]
    return (terms[0] + terms[1]) + (terms[2] + terms[3])


def after(a, *others):
    return lax.optimization_barrier((a, *others))[0]


def local(q_raw, k_raw, values, out_grad, q_gain, k_gain):
    def heads_first(a):
        return jnp.transpose(a, (1, 0, 2))

    kv = jnp.stack([heads_first(k_raw), heads_first(values)])
    qd = jnp.stack([heads_first(q_raw), heads_first(out_grad)])
    pair = mirror(kv)
    x1, x2, x3 = [fetch(kv, "x", NX, k) for k in range(1, NX)]
    q3 = swap(qd, "zq", NQ, 3)
    q2 = swap(after(qd, q3), "zq", NQ, 2)
    x1, x3, x2, pair, qd_now = lax.optimization_barrier((x1, x3, x2, pair, qd))
    p1, p2, p3 = [fetch(pair, "x", NX, k) for k in range(1, NX)]
    q1 = swap(qd_now, "zq", NQ, 1)
    kvs = [kv, pair, x1, p1, x2, p2, x3, p3]
    qds = [qd, q1, q2, q3]
    tile = NH * QR * KR * HD * 2
    stat_shape, q_shape, k_shape = ((16, QR), F32), ((NH, QR, HD), BF16), ((NH, NX * BR, HD), BF16)
    stat, qn, do, kn_own, v_own = kernel_call(
        own_stat_kernel,
        [stat_shape, q_shape, q_shape, k_shape, k_shape],
        [*qds, kv, x1, x2, x3, q_gain, k_gain],
        flops=tile,
    )
    stat, kn_pair, v_pair = kernel_call(
        pair_stat_kernel,
        [stat_shape, k_shape, k_shape],
        [stat, qn, do, pair, p1, p2, p3, k_gain],
        flops=tile,
    )
    stats = [stat] + [swap(stat, "zq", NQ, k) for k in (1, 2, 3)]
    part = (NH, BR, HD)
    kv_part = (NZ, 2, NH, BR, HD)
    whole_dq, gain_part = ((NH, QR, HD), F32), ((8, HD), F32)
    kv_got, carried = [], []
    for k in (2, 1, 3, 0):
        first, last = k == 2, k == 0
        outs = [(kv_part, F32 if last else BF16)]
        outs += [(part, F32)] + [((MESSAGE, HD), BF16)] * 3 if last else [whole_dq]
        args = [*stats, *kvs[NZ * k : NZ * k + NZ], *(qds if last else ()), qn, do, kn_own, v_own, kn_pair, v_pair, *carried]
        got = kernel_call(
            functools.partial(grad_kernel, k, first, last),
            outs + [gain_part],
            args,
            scratch=[pltpu.VMEM((NH, QR, HD), F32)] if last else (),
            flops=6 * tile // NX,
        )
        if last:
            own, dq_own, *messages, gains = got
        else:
            kv_got.append(give(got[0], "x", NX, k))
            carried = got[1:]
    m1, m2, m3 = messages
    m2 = swap(after(m2, kv_got[0]), "zq", NQ, 2)
    m1, m3 = swap(m1, "zq", NQ, 1), swap(m3, "zq", NQ, 3)
    q_out, gains = kernel_call(
        q_out_kernel, [(part, BF16), ((8, HD), F32)], [dq_own, gains, m1, m2, m3, qd, q_gain]
    )
    gains = gains + swap(gains, "core", 2, 1)
    gains = gains + mirror(gains)
    keep, send_k, send_v = kernel_call(
        pair_sum_kernel, [((2, NH, BR, HD), F32), (part, BF16), (part, BF16)], [own, *kv_got]
    )
    got_k = mirror(send_k)
    gains = summed(after(gains, send_k), "y", 4, got_k)
    gains = summed(gains, "x", NX)
    k_out, v_out = kernel_call(
        kv_out_kernel, [(part, BF16)] * 2, [keep, got_k, mirror(send_v), kv, k_gain]
    )

    return (
        heads_first(q_out), heads_first(k_out), heads_first(v_out), gains[0:2], gains[2:4],
    )


def solution(mesh):
    torus = Mesh(mesh.devices.reshape(2, 4, 4, 4, 2), ("zk", "zq", "x", "y", "core"))
    placed = P(ALL_ROWS, ("y", "core"), None)
    return jax.shard_map(
        local,
        mesh=torus,
        in_specs=(placed,) * 4 + (P(), P()),
        out_specs=(placed,) * 3 + (P(), P()),
        check_vma=False,
    )
```

time: 109 us -> 96 us (0.88)
  waiting for transfers between devices: 37.8 us -> 27.3 us
  starting transfers between devices: 51.7 us -> 50 us
    ppermute x17 -> x16, waiting for transfers between devices: 32.8 us -> 10.9 us  [swap(): return lax.ppermute(a, axis, [(i, i ^ k) for i in range(n)])]
    ppermute x0 -> x4, starting transfers between devices: none -> 13.7 us  [mirror(): return lax.ppermute(a, ('zk', 'zq'), [(i, n - 1 - i) for i in range(n)])]
    ppermute x17 -> x16, starting transfers between devices: 33.2 us -> 20.8 us  [swap(): return lax.ppermute(a, axis, [(i, i ^ k) for i in range(n)])]
    ppermute x3, waiting for transfers between devices: 0.01 us -> 5.38 us  [give(): return lax.ppermute(a, axis, [(i, (i + k) % n) for i in range(n)])]
    ppermute x0 -> x4, waiting for transfers between devices: none -> 4.76 us  [mirror(): return lax.ppermute(a, ('zk', 'zq'), [(i, n - 1 - i) for i in range(n)])]
    ppermute x8 -> x6, starting transfers between devices: 13.4 us -> 11 us  [fetch(): return lax.ppermute(a, axis, [((i + k) % n, i) for i in range(n)])]
    ppermute x8 -> x6, waiting for transfers between devices: 5.02 us -> 6.19 us  [fetch(): return lax.ppermute(a, axis, [((i + k) % n, i) for i in range(n)])]
  transfers between devices with their start and end apart: 28 -> 29, of which waited for: 15 -> 14; matrix products, arithmetic and copies ran while one was open for 0% -> 0% of each run, Pallas kernels for 8% -> 12%
where the time goes in v3:
time: 96 us; the launch traced here: 95.9 us
  starting transfers between devices  50 us (52%)
  waiting for transfers between devices  27.3 us (28%)
  Pallas kernels  16.2 us (17%)
  other arithmetic  1.05 us (1%)
    ppermute x16, starting transfers between devices, swap(): return lax.ppermute(a, axis, [(i, i ^ k) for i in range(n)])  20.8 us
    pallas_call x9, Pallas kernels, kernel_call(): pl.pallas_call(kernel, out_shape=[jax.ShapeDtypeStruct(s, d) for s, d in...  16.2 us
    ppermute x4, starting transfers between devices, mirror(): return lax.ppermute(a, ('zk', 'zq'), [(i, n - 1 - i) for i in range(n)])  13.7 us
    ppermute x6, starting transfers between devices, fetch(): return lax.ppermute(a, axis, [((i + k) % n, i) for i in range(n)])  11 us
    ppermute x16, waiting for transfers between devices, swap(): return lax.ppermute(a, axis, [(i, i ^ k) for i in range(n)])  10.9 us
    ppermute x6, waiting for transfers between devices, fetch(): return lax.ppermute(a, axis, [((i + k) % n, i) for i in range(n)])  6.19 us
    ppermute x3, waiting for transfers between devices, give(): return lax.ppermute(a, axis, [(i, (i + k) % n) for i in range(n)])  5.38 us
    ppermute x4, waiting for transfers between devices, mirror(): return lax.ppermute(a, ('zk', 'zq'), [(i, n - 1 - i) for i in range(n)])  4.76 us
  transfers between devices with their start and end apart: 29, of which 14 were waited for; matrix products, arithmetic and copies ran while one was open for 0% of the time, Pallas kernels for 12%

profile of v3, /device:TPU:32, one launch (start us, length us, event | category | flops | bytes accessed | tf_op | source)
XLA Modules:
  0.0 95.9 jit_solution(1263972481448002738)
XLA Ops:
  1.7 2.0 %collective-permute-start.5 = (bf16[2,3,144,128]{3,2,1,0:T(8,128)(2,1)S(1)}, bf16[2,3,144,128]{3,2,1,0:T(8,128)(2,1)S(1)}, u32[]{:S(2)}, u32[]{:S(2)}) collective-permute-start(bf16[2,3,144,128]{3,2,1,0:T(8,128)(2,1)S(1)} %pad_maximum_fusion.q0.refs_6_.raw), channel_id=1, source_target_pairs={{0,96},{32,64},{64,32},{96,0},{1,97},{33,65},{65,33},{97,1},{2,98}... | collective-permute-start | bytes 663560 | tf_op jit(solution)/shard_map/ppermute | solution.py:257
  3.7 5.0 %collective-permute-start.3 = (bf16[2,3,144,128]{3,2,1,0:T(8,128)(2,1)S(1)}, bf16[2,3,144,128]{3,2,1,0:T(8,128)(2,1)S(1)}, u32[]{:S(2)}, u32[]{:S(2)}) collective-permute-start(bf16[2,3,144,128]{3,2,1,0:T(8,128)(2,1)S(1)} %pad_maximum_fusion.1.kv0.refs_4_.raw), channel_id=1, source_target_pairs={{0,224},{32,192},{64,160},{96,128},{128,96},{160,64},{192,32},{224... | collective-permute-start | bytes 663560 | tf_op jit(solution)/shard_map/ppermute | solution.py:266
  8.7 3.0 %collective-permute-start.2 = (bf16[2,3,144,128]{3,2,1,0:T(8,128)(2,1)S(1)}, bf16[2,3,144,128]{3,2,1,0:T(8,128)(2,1)S(1)}, u32[]{:S(2)}, u32[]{:S(2)}) collective-permute-start(bf16[2,3,144,128]{3,2,1,0:T(8,128)(2,1)S(1)} %pad_maximum_fusion.1.kv0.refs_4_.raw), channel_id=1, source_target_pairs={{16,0},{24,8},{0,16},{8,24},{17,1},{25,9},{1,17},{9,25},{18,2},{26... | collective-permute-start | bytes 663560 | tf_op jit(solution)/shard_map/ppermute | solution.py:253
  12.4 2.6 %collective-permute-start = (bf16[2,3,144,128]{3,2,1,0:T(8,128)(2,1)S(1)}, bf16[2,3,144,128]{3,2,1,0:T(8,128)(2,1)S(1)}, u32[]{:S(2)}, u32[]{:S(2)}) collective-permute-start(bf16[2,3,144,128]{3,2,1,0:T(8,128)(2,1)S(1)} %pad_maximum_fusion.1.kv0.refs_4_.raw), channel_id=1, source_target_pairs={{8,0},{16,8},{24,16},{0,24},{9,1},{17,9},{25,17},{1,25},{10,2},{18... | collective-permute-start | bytes 663560 | tf_op jit(solution)/shard_map/ppermute | solution.py:253
  15.0 1.5 %collective-permute-start.6 = (bf16[2,3,144,128]{3,2,1,0:T(8,128)(2,1)S(1)}, bf16[2,3,144,128]{3,2,1,0:T(8,128)(2,1)S(1)}, u32[]{:S(2)}, u32[]{:S(2)}) collective-permute-start(bf16[2,3,144,128]{3,2,1,0:T(8,128)(2,1)S(1)} %pad_maximum_fusion.q0.refs_6_.raw), channel_id=1, source_target_pairs={{0,64},{32,96},{64,0},{96,32},{1,65},{33,97},{65,1},{97,33},{2,66}... | collective-permute-start | bytes 663560 | tf_op jit(solution)/shard_map/ppermute | solution.py:257
  16.5 2.3 %collective-permute-done.3.kv0.refs_5_ = bf16[2,3,144,128]{3,2,1,0:T(8,128)(2,1)S(1)} collective-permute-done((bf16[2,3,144,128]{3,2,1,0:T(8,128)(2,1)S(1)}, bf16[2,3,144,128]{3,2,1,0:T(8,128)(2,1)S(1)}, u32[]{:S(2)}, u32[]{:S(2)}) %collective-permute-start.3) | collective-permute-done | bytes 221216 | tf_op jit(solution)/shard_map/ppermute | solution.py:266
  18.8 2.8 %collective-permute-done.1.kv3.refs_4_ = bf16[2,3,144,128]{3,2,1,0:T(8,128)(2,1)S(1)} collective-permute-done((bf16[2,3,144,128]{3,2,1,0:T(8,128)(2,1)S(1)}, bf16[2,3,144,128]{3,2,1,0:T(8,128)(2,1)S(1)}, u32[]{:S(2)}, u32[]{:S(2)}) %collective-permute-start.1) | collective-permute-done | bytes 221216 | tf_op jit(solution)/shard_map/ppermute | solution.py:253
  22.7 1.5 %collective-permute-start.9 = (bf16[2,3,144,128]{3,2,1,0:T(8,128)(2,1)S(1)}, bf16[2,3,144,128]{3,2,1,0:T(8,128)(2,1)S(1)}, u32[]{:S(2)}, u32[]{:S(2)}) collective-permute-start(bf16[2,3,144,128]{3,2,1,0:T(8,128)(2,1)S(1)} %collective-permute-done.3.kv0.refs_5_), channel_id=1, source_target_pairs={{24,0},{0,8},{8,16},{16,24},{25,1},{1,9},{9,17},{17,25},{26,2},{2,... | collective-permute-start | bytes 663560 | tf_op jit(solution)/shard_map/ppermute | solution.py:253
  24.2 2.6 %collective-permute-start.8 = (bf16[2,3,144,128]{3,2,1,0:T(8,128)(2,1)S(1)}, bf16[2,3,144,128]{3,2,1,0:T(8,128)(2,1)S(1)}, u32[]{:S(2)}, u32[]{:S(2)}) collective-permute-start(bf16[2,3,144,128]{3,2,1,0:T(8,128)(2,1)S(1)} %collective-permute-done.3.kv0.refs_5_), channel_id=1, source_target_pairs={{16,0},{24,8},{0,16},{8,24},{17,1},{25,9},{1,17},{9,25},{18,2},{26... | collective-permute-start | bytes 663560 | tf_op jit(solution)/shard_map/ppermute | solution.py:253
  27.4 2.3 %collective-permute-done.4.q1.refs_7_ = bf16[2,3,144,128]{3,2,1,0:T(8,128)(2,1)S(1)} collective-permute-done((bf16[2,3,144,128]{3,2,1,0:T(8,128)(2,1)S(1)}, bf16[2,3,144,128]{3,2,1,0:T(8,128)(2,1)S(1)}, u32[]{:S(2)}, u32[]{:S(2)}) %collective-permute-start.4) | collective-permute-done | bytes 221216 | tf_op jit(solution)/shard_map/ppermute | solution.py:257
  29.7 2.7 %shard_map.101 = (f32[16,576]{1,0:T(8,128)S(1)}, bf16[3,576,128]{2,1,0:T(8,128)(2,1)S(1)}, bf16[3,576,128]{2,1,0:T(8,128)(2,1)S(1)}, bf16[3,576,128]{2,1,0:T(8,128)(2,1)S(1)}, bf16[3,576,128]{2,1,0:T(8,128)(2,1)S(1)}) custom-call(bf16[2,3,144,128]{3,2,1,0:T(8,128)(2,1)S(1)} %pad_maximum_fusion.q0.refs_6_.raw, ...), custom_call_target="tpu_custom_call" | custom-call | flops 509607936 | bytes 1771520 | tf_op jit(solution)/shard_map/pallas_call | solution.py:241
  32.4 3.3 %collective-permute-done.8.kv2.refs_5_ = bf16[2,3,144,128]{3,2,1,0:T(8,128)(2,1)S(1)} collective-permute-done((bf16[2,3,144,128]{3,2,1,0:T(8,128)(2,1)S(1)}, bf16[2,3,144,128]{3,2,1,0:T(8,128)(2,1)S(1)}, u32[]{:S(2)}, u32[]{:S(2)}) %collective-permute-start.8) | collective-permute-done | bytes 221216 | tf_op jit(solution)/shard_map/ppermute | solution.py:253
  35.7 2.4 %shard_map.102 = (f32[16,576]{1,0:T(8,128)S(1)}, bf16[3,576,128]{2,1,0:T(8,128)(2,1)S(1)}, bf16[3,576,128]{2,1,0:T(8,128)(2,1)S(1)}) custom-call(f32[16,576]{1,0:T(8,128)S(1)} %get-tuple-element.56.before_ref, bf16[3,576,128]{2,1,0:T(8,128)(2,1)S(1)} %get-tuple-element.57.qn_ref.refs_6_.refs_10_, ...), custom_call_target="tpu_custom_call" | custom-call | flops 509607936 | bytes 1807360 | tf_op jit(solution)/shard_map/pallas_call | solution.py:241
  39.2 2.4 %collective-permute-start.11 = (f32[16,576]{1,0:T(8,128)S(1)}, f32[16,576]{1,0:T(8,128)S(1)}, u32[]{:S(2)}, u32[]{:S(2)}) collective-permute-start(f32[16,576]{1,0:T(8,128)S(1)} %get-tuple-element.60.refs_0_), channel_id=1, source_target_pairs={{0,64},{32,96},{64,0},{96,32},{1,65},{33,97},{65,1},{97,33},{2,66}... | collective-permute-start | bytes 110600 | tf_op jit(solution)/shard_map/ppermute | solution.py:257
  42.2 1.9 %collective-permute-done.11.refs_2_ = f32[16,576]{1,0:T(8,128)S(1)} collective-permute-done((f32[16,576]{1,0:T(8,128)S(1)}, f32[16,576]{1,0:T(8,128)S(1)}, u32[]{:S(2)}, u32[]{:S(2)}) %collective-permute-start.11) | collective-permute-done | bytes 36896 | tf_op jit(solution)/shard_map/ppermute | solution.py:257
  44.1 1.5 %collective-permute-done.10.refs_1_ = f32[16,576]{1,0:T(8,128)S(1)} collective-permute-done((f32[16,576]{1,0:T(8,128)S(1)}, f32[16,576]{1,0:T(8,128)S(1)}, u32[]{:S(2)}, u32[]{:S(2)}) %collective-permute-start.10) | collective-permute-done | bytes 36896 | tf_op jit(solution)/shard_map/ppermute | solution.py:257
  45.5 2.1 %shard_map.103 = (bf16[2,2,3,144,128]{4,3,2,1,0:T(8,128)(2,1)S(1)}, f32[3,576,128]{2,1,0:T(8,128)S(1)}, f32[8,128]{1,0:T(8,128)S(1)}) custom-call(f32[16,576]{1,0:T(8,128)S(1)} %get-tuple-element.60.refs_0_, f32[16,576]{1,0:T(8,128)S(1)} %collective-permute-done.10.refs_1_, f32[16,576]{1,0:T(8,128)S(1)} %collective-permute-done.11.refs_2_, ...), custom_call_target="tpu_custom_call" | custom-call | flops 764411904 | bytes 3244032 | tf_op jit(solution)/shard_map/pallas_call | solution.py:241
  47.6 2.5 %collective-permute-start.14 = (bf16[2,2,3,144,128]{4,3,2,1,0:T(8,128)(2,1)S(1)}, bf16[2,2,3,144,128]{4,3,2,1,0:T(8,128)(2,1)S(1)}, u32[]{:S(2)}, u32[]{:S(2)}) collective-permute-start(bf16[2,2,3,144,128]{4,3,2,1,0:T(8,128)(2,1)S(1)} %get-tuple-element.75), channel_id=1, source_target_pairs={{0,16},{8,24},{16,0},{24,8},{1,17},{9,25},{17,1},{25,9},{2,18},{10... | collective-permute-start | bytes 1327112 | tf_op jit(solution)/shard_map/ppermute | solution.py:261
  50.1 2.1 %shard_map.104 = (bf16[2,2,3,144,128]{4,3,2,1,0:T(8,128)(2,1)S(1)}, f32[3,576,128]{2,1,0:T(8,128)S(1)}, f32[8,128]{1,0:T(8,128)S(1)}) custom-call(f32[16,576]{1,0:T(8,128)S(1)} %get-tuple-element.60.refs_0_, f32[16,576]{1,0:T(8,128)S(1)} %collective-permute-done.10.refs_1_, f32[16,576]{1,0:T(8,128)S(1)} %collective-permute-done.11.refs_2_, ...), custom_call_target="tpu_custom_call" | custom-call | flops 764411904 | bytes 4132864 | tf_op jit(solution)/shard_map/pallas_call | solution.py:241
  52.3 2.1 %shard_map.105 = (bf16[2,2,3,144,128]{4,3,2,1,0:T(8,128)(2,1)S(1)}, f32[3,576,128]{2,1,0:T(8,128)S(1)}, f32[8,128]{1,0:T(8,128)S(1)}) custom-call(f32[16,576]{1,0:T(8,128)S(1)} %get-tuple-element.60.refs_0_, f32[16,576]{1,0:T(8,128)S(1)} %collective-permute-done.10.refs_1_, f32[16,576]{1,0:T(8,128)S(1)} %collective-permute-done.11.refs_2_, ...), custom_call_target="tpu_custom_call" | custom-call | flops 764411904 | bytes 4132864 | tf_op jit(solution)/shard_map/pallas_call | solution.py:241
  54.4 2.0 %collective-permute-start.18 = (bf16[2,2,3,144,128]{4,3,2,1,0:T(8,128)(2,1)S(1)}, bf16[2,2,3,144,128]{4,3,2,1,0:T(8,128)(2,1)S(1)}, u32[]{:S(2)}, u32[]{:S(2)}) collective-permute-start(bf16[2,2,3,144,128]{4,3,2,1,0:T(8,128)(2,1)S(1)} %get-tuple-element.81), channel_id=1, source_target_pairs={{0,24},{8,0},{16,8},{24,16},{1,25},{9,1},{17,9},{25,17},{2,26},{10... | collective-permute-start | bytes 1327112 | tf_op jit(solution)/shard_map/ppermute | solution.py:261
  56.5 2.7 %shard_map.106 = (f32[2,2,3,144,128]{4,3,2,1,0:T(8,128)S(1)}, f32[3,144,128]{2,1,0:T(8,128)S(1)}, bf16[464,128]{1,0:T(8,128)(2,1)S(1)}, bf16[464,128]{1,0:T(8,12...) custom-call(f32[16,576]{1,0:T(8,128)S(1)} %get-tuple-element.60.refs_0_, ...), custom_call_target="tpu_custom_call" | custom-call | flops 764411904 | bytes 5017600 | tf_op jit(solution)/shard_map/pallas_call | solution.py:241
  61.0 2.7 %collective-permute-start.15 = (bf16[464,128]{1,0:T(8,128)(2,1)S(1)}, bf16[464,128]{1,0:T(8,128)(2,1)S(1)}, u32[]{:S(2)}, u32[]{:S(2)}) collective-permute-start(bf16[464,128]{1,0:T(8,128)(2,1)S(1)} %get-tuple-element.76), channel_id=1, source_target_pairs={{0,64},{32,96},{64,0},{96,32},{1,65},{33,97},{65,1},{97,33},{2,66}... | collective-permute-start | bytes 356360 | tf_op jit(solution)/shard_map/ppermute | solution.py:257
  63.7 5.4 %collective-permute-done.18.r3 = bf16[2,2,3,144,128]{4,3,2,1,0:T(8,128)(2,1)S(1)} collective-permute-done((bf16[2,2,3,144,128]{4,3,2,1,0:T(8,128)(2,1)S(1)}, bf16[2,2,3,144,128]{4,3,2,1,0:T(8,128)(2,1)S(1)}, u32[]{:S(2)}, u32[]{:S(2)}) %collective-permute-start.18) | collective-permute-done | bytes 442400 | tf_op jit(solution)/shard_map/ppermute | solution.py:261
  71.2 1.2 %collective-permute-done.21 = f32[8,128]{1,0:T(8,128)S(1)} collective-permute-done((f32[8,128]{1,0:T(8,128)S(1)}, f32[8,128]{1,0:T(8,128)S(1)}, u32[]{:S(2)}, u32[]{:S(2)}) %collective-permute-start.21) | collective-permute-done | bytes 4128 | tf_op jit(solution)/shard_map/ppermute | solution.py:257
  72.4 4.1 %collective-permute-start.22 = (f32[8,128]{1,0:T(8,128)S(1)}, f32[8,128]{1,0:T(8,128)S(1)}, u32[]{:S(2)}, u32[]{:S(2)}) collective-permute-start(f32[8,128]{1,0:T(8,128)S(1)} %add.24), channel_id=1, source_target_pairs={{0,224},{32,192},{64,160},{96,128},{128,96},{160,64},{192,32},{224... | collective-permute-start | bytes 12296 | tf_op jit(solution)/shard_map/ppermute | solution.py:266
  76.5 2.5 %collective-permute-done.22 = f32[8,128]{1,0:T(8,128)S(1)} collective-permute-done((f32[8,128]{1,0:T(8,128)S(1)}, f32[8,128]{1,0:T(8,128)S(1)}, u32[]{:S(2)}, u32[]{:S(2)}) %collective-permute-start.22) | collective-permute-done | bytes 4128 | tf_op jit(solution)/shard_map/ppermute | solution.py:266
  79.0 3.0 %collective-permute-start.25 = (f32[8,128]{1,0:T(8,128)S(1)}, f32[8,128]{1,0:T(8,128)S(1)}, u32[]{:S(2)}, u32[]{:S(2)}) collective-permute-start(f32[8,128]{1,0:T(8,128)S(1)} %add.25), channel_id=1, source_target_pairs={{0,6},{2,4},{4,2},{6,0},{1,7},{3,5},{5,3},{7,1},{8,14},{10,12},{12... | collective-permute-start | bytes 12296 | tf_op jit(solution)/shard_map/ppermute | solution.py:257
  83.1 4.1 %collective-permute-start.20 = (bf16[3,144,128]{2,1,0:T(8,128)(2,1)S(1)}, bf16[3,144,128]{2,1,0:T(8,128)(2,1)S(1)}, u32[]{:S(2)}, u32[]{:S(2)}) collective-permute-start(bf16[3,144,128]{2,1,0:T(8,128)(2,1)S(1)} %get-tuple-element.84), channel_id=1, source_target_pairs={{0,224},{32,192},{64,160},{96,128},{128,96},{160,64},{192,32},{224... | collective-permute-start | bytes 331784 | tf_op jit(solution)/shard_map/ppermute | solution.py:266
  87.3 2.9 %collective-permute-start.28 = (f32[8,128]{1,0:T(8,128)S(1)}, f32[8,128]{1,0:T(8,128)S(1)}, u32[]{:S(2)}, u32[]{:S(2)}) collective-permute-start(f32[8,128]{1,0:T(8,128)S(1)} %add_add_fusion.1), channel_id=1, source_target_pairs={{0,24},{8,16},{16,8},{24,0},{1,25},{9,17},{17,9},{25,1},{2,26},{10... | collective-permute-start | bytes 12296 | tf_op jit(solution)/shard_map/ppermute | solution.py:257
  90.2 1.2 %collective-permute-start.27 = (f32[8,128]{1,0:T(8,128)S(1)}, f32[8,128]{1,0:T(8,128)S(1)}, u32[]{:S(2)}, u32[]{:S(2)}) collective-permute-start(f32[8,128]{1,0:T(8,128)S(1)} %add_add_fusion.1), channel_id=1, source_target_pairs={{0,16},{8,24},{16,0},{24,8},{1,17},{9,25},{17,1},{25,9},{2,18},{10... | collective-permute-start | bytes 12296 | tf_op jit(solution)/shard_map/ppermute | solution.py:257
  92.4 2.9 %collective-permute-done.27 = f32[8,128]{1,0:T(8,128)S(1)} collective-permute-done((f32[8,128]{1,0:T(8,128)S(1)}, f32[8,128]{1,0:T(8,128)S(1)}, u32[]{:S(2)}, u32[]{:S(2)}) %collective-permute-start.27) | collective-permute-done | bytes 4128 | tf_op jit(solution)/shard_map/ppermute | solution.py:257
  (50 shorter events, 11.9 us)
Async XLA Ops:
  0.6 3.0 %copy-start.2 = (bf16[144,3,128]{2,0,1:T(8,128)(2,1)S(1)}, bf16[144,3,128]{2,0,1:T(8,128)(2,1)}, u32[]{:S(2)}) copy-start(bf16[144,3,128]{2,0,1:T(8,128)(2,1)} %param.8) | copy-start | bytes 331780
  1.7 13.3 %collective-permute-start.5 = (bf16[2,3,144,128]{3,2,1,0:T(8,128)(2,1)S(1)}, bf16[2,3,144,128]{3,2,1,0:T(8,128)(2,1)S(1)}, u32[]{:S(2)}, u32[]{:S(2)}) collective-permute-start(bf16[2,3,144,128]{3,2,1,0:T(8,128)(2,1)S(1)} %pad_maximum_fusion.q0.refs_6_.raw), channel_id=1, source_target_pairs={{0,96},{32,64},{64,32},{96,0},{1,97},{33,65},{65,33},{97,1},{2,98}... | collective-permute-start | bytes 663560 | tf_op jit(solution)/shard_map/ppermute | solution.py:257
  3.7 26.0 %copy-start = (f32[2,128]{1,0:T(2,128)S(1)}, f32[2,128]{1,0:T(2,128)}, u32[]{:S(2)}) copy-start(f32[2,128]{1,0:T(2,128)} %gain_ref.2) | copy-start | bytes 3076
  3.7 26.0 %copy-start.1 = (f32[2,128]{1,0:T(2,128)S(1)}, f32[2,128]{1,0:T(2,128)}, u32[]{:S(2)}) copy-start(f32[2,128]{1,0:T(2,128)} %gain_ref.3) | copy-start | bytes 3076
  3.7 15.1 %collective-permute-start.3 = (bf16[2,3,144,128]{3,2,1,0:T(8,128)(2,1)S(1)}, bf16[2,3,144,128]{3,2,1,0:T(8,128)(2,1)S(1)}, u32[]{:S(2)}, u32[]{:S(2)}) collective-permute-start(bf16[2,3,144,128]{3,2,1,0:T(8,128)(2,1)S(1)} %pad_maximum_fusion.1.kv0.refs_4_.raw), channel_id=1, source_target_pairs={{0,224},{32,192},{64,160},{96,128},{128,96},{160,64},{192,32},{224... | collective-permute-start | bytes 663560 | tf_op jit(solution)/shard_map/ppermute | solution.py:266
  8.7 10.0 %collective-permute-start.2 = (bf16[2,3,144,128]{3,2,1,0:T(8,128)(2,1)S(1)}, bf16[2,3,144,128]{3,2,1,0:T(8,128)(2,1)S(1)}, u32[]{:S(2)}, u32[]{:S(2)}) collective-permute-start(bf16[2,3,144,128]{3,2,1,0:T(8,128)(2,1)S(1)} %pad_maximum_fusion.1.kv0.refs_4_.raw), channel_id=1, source_target_pairs={{16,0},{24,8},{0,16},{8,24},{17,1},{25,9},{1,17},{9,25},{18,2},{26... | collective-permute-start | bytes 663560 | tf_op jit(solution)/shard_map/ppermute | solution.py:253
  11.8 9.8 %collective-permute-start.1 = (bf16[2,3,144,128]{3,2,1,0:T(8,128)(2,1)S(1)}, bf16[2,3,144,128]{3,2,1,0:T(8,128)(2,1)S(1)}, u32[]{:S(2)}, u32[]{:S(2)}) collective-permute-start(bf16[2,3,144,128]{3,2,1,0:T(8,128)(2,1)S(1)} %pad_maximum_fusion.1.kv0.refs_4_.raw), channel_id=1, source_target_pairs={{24,0},{0,8},{8,16},{16,24},{25,1},{1,9},{9,17},{17,25},{26,2},{2,... | collective-permute-start | bytes 663560 | tf_op jit(solution)/shard_map/ppermute | solution.py:253
  12.4 9.3 %collective-permute-start = (bf16[2,3,144,128]{3,2,1,0:T(8,128)(2,1)S(1)}, bf16[2,3,144,128]{3,2,1,0:T(8,128)(2,1)S(1)}, u32[]{:S(2)}, u32[]{:S(2)}) collective-permute-start(bf16[2,3,144,128]{3,2,1,0:T(8,128)(2,1)S(1)} %pad_maximum_fusion.1.kv0.refs_4_.raw), channel_id=1, source_target_pairs={{8,0},{16,8},{24,16},{0,24},{9,1},{17,9},{25,17},{1,25},{10,2},{18... | collective-permute-start | bytes 663560 | tf_op jit(solution)/shard_map/ppermute | solution.py:253
  15.0 12.4 %collective-permute-start.6 = (bf16[2,3,144,128]{3,2,1,0:T(8,128)(2,1)S(1)}, bf16[2,3,144,128]{3,2,1,0:T(8,128)(2,1)S(1)}, u32[]{:S(2)}, u32[]{:S(2)}) collective-permute-start(bf16[2,3,144,128]{3,2,1,0:T(8,128)(2,1)S(1)} %pad_maximum_fusion.q0.refs_6_.raw), channel_id=1, source_target_pairs={{0,64},{32,96},{64,0},{96,32},{1,65},{33,97},{65,1},{97,33},{2,66}... | collective-permute-start | bytes 663560 | tf_op jit(solution)/shard_map/ppermute | solution.py:257
  21.7 8.0 %collective-permute-start.4 = (bf16[2,3,144,128]{3,2,1,0:T(8,128)(2,1)S(1)}, bf16[2,3,144,128]{3,2,1,0:T(8,128)(2,1)S(1)}, u32[]{:S(2)}, u32[]{:S(2)}) collective-permute-start(bf16[2,3,144,128]{3,2,1,0:T(8,128)(2,1)S(1)} %pad_maximum_fusion.q0.refs_6_.raw), channel_id=1, source_target_pairs={{0,32},{32,0},{64,96},{96,64},{1,33},{33,1},{65,97},{97,65},{2,34}... | collective-permute-start | bytes 663560 | tf_op jit(solution)/shard_map/ppermute | solution.py:257
  22.7 9.7 %collective-permute-start.9 = (bf16[2,3,144,128]{3,2,1,0:T(8,128)(2,1)S(1)}, bf16[2,3,144,128]{3,2,1,0:T(8,128)(2,1)S(1)}, u32[]{:S(2)}, u32[]{:S(2)}) collective-permute-start(bf16[2,3,144,128]{3,2,1,0:T(8,128)(2,1)S(1)} %collective-permute-done.3.kv0.refs_5_), channel_id=1, source_target_pairs={{24,0},{0,8},{8,16},{16,24},{25,1},{1,9},{9,17},{17,25},{26,2},{2,... | collective-permute-start | bytes 663560 | tf_op jit(solution)/shard_map/ppermute | solution.py:253
  24.2 11.5 %collective-permute-start.8 = (bf16[2,3,144,128]{3,2,1,0:T(8,128)(2,1)S(1)}, bf16[2,3,144,128]{3,2,1,0:T(8,128)(2,1)S(1)}, u32[]{:S(2)}, u32[]{:S(2)}) collective-permute-start(bf16[2,3,144,128]{3,2,1,0:T(8,128)(2,1)S(1)} %collective-permute-done.3.kv0.refs_5_), channel_id=1, source_target_pairs={{16,0},{24,8},{0,16},{8,24},{17,1},{25,9},{1,17},{9,25},{18,2},{26... | collective-permute-start | bytes 663560 | tf_op jit(solution)/shard_map/ppermute | solution.py:253
  26.8 8.9 %collective-permute-start.7 = (bf16[2,3,144,128]{3,2,1,0:T(8,128)(2,1)S(1)}, bf16[2,3,144,128]{3,2,1,0:T(8,128)(2,1)S(1)}, u32[]{:S(2)}, u32[]{:S(2)}) collective-permute-start(bf16[2,3,144,128]{3,2,1,0:T(8,128)(2,1)S(1)} %collective-permute-done.3.kv0.refs_5_), channel_id=1, source_target_pairs={{8,0},{16,8},{24,16},{0,24},{9,1},{17,9},{25,17},{1,25},{10,2},{18... | collective-permute-start | bytes 663560 | tf_op jit(solution)/shard_map/ppermute | solution.py:253
  38.0 4.1 %collective-permute-start.12 = (f32[16,576]{1,0:T(8,128)S(1)}, f32[16,576]{1,0:T(8,128)S(1)}, u32[]{:S(2)}, u32[]{:S(2)}) collective-permute-start(f32[16,576]{1,0:T(8,128)S(1)} %get-tuple-element.60.refs_0_), channel_id=1, source_target_pairs={{0,96},{32,64},{64,32},{96,0},{1,97},{33,65},{65,33},{97,1},{2,98}... | collective-permute-start | bytes 110600 | tf_op jit(solution)/shard_map/ppermute | solution.py:257
  39.2 4.9 %collective-permute-start.11 = (f32[16,576]{1,0:T(8,128)S(1)}, f32[16,576]{1,0:T(8,128)S(1)}, u32[]{:S(2)}, u32[]{:S(2)}) collective-permute-start(f32[16,576]{1,0:T(8,128)S(1)} %get-tuple-element.60.refs_0_), channel_id=1, source_target_pairs={{0,64},{32,96},{64,0},{96,32},{1,65},{33,97},{65,1},{97,33},{2,66}... | collective-permute-start | bytes 110600 | tf_op jit(solution)/shard_map/ppermute | solution.py:257
  41.5 4.0 %collective-permute-start.10 = (f32[16,576]{1,0:T(8,128)S(1)}, f32[16,576]{1,0:T(8,128)S(1)}, u32[]{:S(2)}, u32[]{:S(2)}) collective-permute-start(f32[16,576]{1,0:T(8,128)S(1)} %get-tuple-element.60.refs_0_), channel_id=1, source_target_pairs={{0,32},{32,0},{64,96},{96,64},{1,33},{33,1},{65,97},{97,65},{2,34}... | collective-permute-start | bytes 110600 | tf_op jit(solution)/shard_map/ppermute | solution.py:257
  47.6 13.4 %collective-permute-start.14 = (bf16[2,2,3,144,128]{4,3,2,1,0:T(8,128)(2,1)S(1)}, bf16[2,2,3,144,128]{4,3,2,1,0:T(8,128)(2,1)S(1)}, u32[]{:S(2)}, u32[]{:S(2)}) collective-permute-start(bf16[2,2,3,144,128]{4,3,2,1,0:T(8,128)(2,1)S(1)} %get-tuple-element.75), channel_id=1, source_target_pairs={{0,16},{8,24},{16,0},{24,8},{1,17},{9,25},{17,1},{25,9},{2,18},{10... | collective-permute-start | bytes 1327112 | tf_op jit(solution)/shard_map/ppermute | solution.py:261
  54.4 14.7 %collective-permute-start.18 = (bf16[2,2,3,144,128]{4,3,2,1,0:T(8,128)(2,1)S(1)}, bf16[2,2,3,144,128]{4,3,2,1,0:T(8,128)(2,1)S(1)}, u32[]{:S(2)}, u32[]{:S(2)}) collective-permute-start(bf16[2,2,3,144,128]{4,3,2,1,0:T(8,128)(2,1)S(1)} %get-tuple-element.81), channel_id=1, source_target_pairs={{0,24},{8,0},{16,8},{24,16},{1,25},{9,1},{17,9},{25,17},{2,26},{10... | collective-permute-start | bytes 1327112 | tf_op jit(solution)/shard_map/ppermute | solution.py:261
  56.4 12.7 %collective-permute-start.17 = (bf16[2,2,3,144,128]{4,3,2,1,0:T(8,128)(2,1)S(1)}, bf16[2,2,3,144,128]{4,3,2,1,0:T(8,128)(2,1)S(1)}, u32[]{:S(2)}, u32[]{:S(2)}) collective-permute-start(bf16[2,2,3,144,128]{4,3,2,1,0:T(8,128)(2,1)S(1)} %get-tuple-element.80), channel_id=1, source_target_pairs={{0,8},{8,16},{16,24},{24,0},{1,9},{9,17},{17,25},{25,1},{2,10},{10... | collective-permute-start | bytes 1327112 | tf_op jit(solution)/shard_map/ppermute | solution.py:261
  59.2 10.4 %collective-permute-start.13 = (bf16[464,128]{1,0:T(8,128)(2,1)S(1)}, bf16[464,128]{1,0:T(8,128)(2,1)S(1)}, u32[]{:S(2)}, u32[]{:S(2)}) collective-permute-start(bf16[464,128]{1,0:T(8,128)(2,1)S(1)} %get-tuple-element.73), channel_id=1, source_target_pairs={{0,32},{32,0},{64,96},{96,64},{1,33},{33,1},{65,97},{97,65},{2,34}... | collective-permute-start | bytes 356360 | tf_op jit(solution)/shard_map/ppermute | solution.py:257
  59.9 10.2 %collective-permute-start.16 = (bf16[464,128]{1,0:T(8,128)(2,1)S(1)}, bf16[464,128]{1,0:T(8,128)(2,1)S(1)}, u32[]{:S(2)}, u32[]{:S(2)}) collective-permute-start(bf16[464,128]{1,0:T(8,128)(2,1)S(1)} %get-tuple-element.77), channel_id=1, source_target_pairs={{0,96},{32,64},{64,32},{96,0},{1,97},{33,65},{65,33},{97,1},{2,98}... | collective-permute-start | bytes 356360 | tf_op jit(solution)/shard_map/ppermute | solution.py:257
  61.0 9.2 %collective-permute-start.15 = (bf16[464,128]{1,0:T(8,128)(2,1)S(1)}, bf16[464,128]{1,0:T(8,128)(2,1)S(1)}, u32[]{:S(2)}, u32[]{:S(2)}) collective-permute-start(bf16[464,128]{1,0:T(8,128)(2,1)S(1)} %get-tuple-element.76), channel_id=1, source_target_pairs={{0,64},{32,96},{64,0},{96,32},{1,65},{33,97},{65,1},{97,33},{2,66}... | collective-permute-start | bytes 356360 | tf_op jit(solution)/shard_map/ppermute | solution.py:257
  69.3 18.0 %collective-permute-start.19 = (bf16[3,144,128]{2,1,0:T(8,128)(2,1)S(1)}, bf16[3,144,128]{2,1,0:T(8,128)(2,1)S(1)}, u32[]{:S(2)}, u32[]{:S(2)}) collective-permute-start(bf16[3,144,128]{2,1,0:T(8,128)(2,1)S(1)} %get-tuple-element.83), channel_id=1, source_target_pairs={{0,224},{32,192},{64,160},{96,128},{128,96},{160,64},{192,32},{224... | collective-permute-start | bytes 331784 | tf_op jit(solution)/shard_map/ppermute | solution.py:266
  71.2 1.2 %collective-permute-start.21 = (f32[8,128]{1,0:T(8,128)S(1)}, f32[8,128]{1,0:T(8,128)S(1)}, u32[]{:S(2)}, u32[]{:S(2)}) collective-permute-start(f32[8,128]{1,0:T(8,128)S(1)} %get-tuple-element.87), channel_id=1, source_target_pairs={{0,1},{1,0},{2,3},{3,2},{4,5},{5,4},{6,7},{7,6},{8,9},{9,8},{10,11... | collective-permute-start | bytes 12296 | tf_op jit(solution)/shard_map/ppermute | solution.py:257
  72.4 6.6 %collective-permute-start.22 = (f32[8,128]{1,0:T(8,128)S(1)}, f32[8,128]{1,0:T(8,128)S(1)}, u32[]{:S(2)}, u32[]{:S(2)}) collective-permute-start(f32[8,128]{1,0:T(8,128)S(1)} %add.24), channel_id=1, source_target_pairs={{0,224},{32,192},{64,160},{96,128},{128,96},{160,64},{192,32},{224... | collective-permute-start | bytes 12296 | tf_op jit(solution)/shard_map/ppermute | solution.py:266
  79.0 8.3 %collective-permute-start.25 = (f32[8,128]{1,0:T(8,128)S(1)}, f32[8,128]{1,0:T(8,128)S(1)}, u32[]{:S(2)}, u32[]{:S(2)}) collective-permute-start(f32[8,128]{1,0:T(8,128)S(1)} %add.25), channel_id=1, source_target_pairs={{0,6},{2,4},{4,2},{6,0},{1,7},{3,5},{5,3},{7,1},{8,14},{10,12},{12... | collective-permute-start | bytes 12296 | tf_op jit(solution)/shard_map/ppermute | solution.py:257
  82.0 5.3 %collective-permute-start.24 = (f32[8,128]{1,0:T(8,128)S(1)}, f32[8,128]{1,0:T(8,128)S(1)}, u32[]{:S(2)}, u32[]{:S(2)}) collective-permute-start(f32[8,128]{1,0:T(8,128)S(1)} %add.25), channel_id=1, source_target_pairs={{0,4},{2,6},{4,0},{6,2},{1,5},{3,7},{5,1},{7,3},{8,12},{10,14},{12... | collective-permute-start | bytes 12296 | tf_op jit(solution)/shard_map/ppermute | solution.py:257
  82.6 4.6 %collective-permute-start.23 = (f32[8,128]{1,0:T(8,128)S(1)}, f32[8,128]{1,0:T(8,128)S(1)}, u32[]{:S(2)}, u32[]{:S(2)}) collective-permute-start(f32[8,128]{1,0:T(8,128)S(1)} %add.25), channel_id=1, source_target_pairs={{0,2},{2,0},{4,6},{6,4},{1,3},{3,1},{5,7},{7,5},{8,10},{10,8},{12,... | collective-permute-start | bytes 12296 | tf_op jit(solution)/shard_map/ppermute | solution.py:257
  83.1 8.4 %collective-permute-start.20 = (bf16[3,144,128]{2,1,0:T(8,128)(2,1)S(1)}, bf16[3,144,128]{2,1,0:T(8,128)(2,1)S(1)}, u32[]{:S(2)}, u32[]{:S(2)}) collective-permute-start(bf16[3,144,128]{2,1,0:T(8,128)(2,1)S(1)} %get-tuple-element.84), channel_id=1, source_target_pairs={{0,224},{32,192},{64,160},{96,128},{128,96},{160,64},{192,32},{224... | collective-permute-start | bytes 331784 | tf_op jit(solution)/shard_map/ppermute | solution.py:266
  87.3 5.1 %collective-permute-start.28 = (f32[8,128]{1,0:T(8,128)S(1)}, f32[8,128]{1,0:T(8,128)S(1)}, u32[]{:S(2)}, u32[]{:S(2)}) collective-permute-start(f32[8,128]{1,0:T(8,128)S(1)} %add_add_fusion.1), channel_id=1, source_target_pairs={{0,24},{8,16},{16,8},{24,0},{1,25},{9,17},{17,9},{25,1},{2,26},{10... | collective-permute-start | bytes 12296 | tf_op jit(solution)/shard_map/ppermute | solution.py:257
  90.2 5.1 %collective-permute-start.27 = (f32[8,128]{1,0:T(8,128)S(1)}, f32[8,128]{1,0:T(8,128)S(1)}, u32[]{:S(2)}, u32[]{:S(2)}) collective-permute-start(f32[8,128]{1,0:T(8,128)S(1)} %add_add_fusion.1), channel_id=1, source_target_pairs={{0,16},{8,24},{16,0},{24,8},{1,17},{9,25},{17,1},{25,9},{2,18},{10... | collective-permute-start | bytes 12296 | tf_op jit(solution)/shard_map/ppermute | solution.py:257
  91.4 3.9 %collective-permute-start.26 = (f32[8,128]{1,0:T(8,128)S(1)}, f32[8,128]{1,0:T(8,128)S(1)}, u32[]{:S(2)}, u32[]{:S(2)}) collective-permute-start(f32[8,128]{1,0:T(8,128)S(1)} %add_add_fusion.1), channel_id=1, source_target_pairs={{0,8},{8,0},{16,24},{24,16},{1,9},{9,1},{17,25},{25,17},{2,10},{10... | collective-permute-start | bytes 12296 | tf_op jit(solution)/shard_map/ppermute | solution.py:257
  (1 other events, 3.0 us)

commit v4 on v3

--- a/solution.py
+++ b/solution.py
@@ -20,7 +20,6 @@
 SCALE2 = FACTOR * math.log2(math.e)
 F32, BF16 = jnp.float32, jnp.bfloat16
 VMEM_LIMIT = 24 * 1024 * 1024
-MESSAGE = NH * BR + 32
 ALL_ROWS = ("zk", "zq", "x")
 
 
@@ -123,14 +122,6 @@
     place_keys((kv0, kv1, kv2, kv3), 1, gk_ref, kn_ref, v_ref)
     stat_ref[...] = jnp.zeros_like(stat_ref)
     fold_stats(qn_ref, do_ref, kn_ref, v_ref, before_ref, stat_ref)
-
-
-def in_three(sums):
-    high = sums.astype(BF16).astype(F32)
-    middle = (sums - high).astype(BF16).astype(F32)
-    low = ((sums - high) - middle).astype(BF16).astype(F32)
-    tail = jnp.concatenate([high, middle, low, jnp.zeros_like(sums)], axis=0).astype(BF16)
-    return tail, (high + middle) + low
 
 
 def grad_kernel(k, first, last, *refs):
@@ -183,7 +174,7 @@
             if slot == 0:
                 dq_own[h] = part
             else:
-                messages[slot - 1][h * BR : (h + 1) * BR, :] = part.astype(BF16)
+                messages[slot - 1][h] = part.astype(BF16)
             unit, _ = unit_and_root(q_refs[slot][0, h])
             term = part * unit
             q_all += jnp.sum(term, axis=0, keepdims=True)
@@ -192,19 +183,15 @@
         [q_text, q_all - q_text, k_text, k_all - k_text, jnp.zeros((4, HD), F32)], axis=0
     )
     gains = gains if first else gain_in[...] + gains
-    if last:
-        tail, gains = in_three(gains)
-        for out in messages:
-            out[NH * BR :, :] = tail
     gain_ref[...] = gains
 
 
-def pair_sum_kernel(own, r1, r2, r3, keep_ref, send_k, send_v):
+def pair_sum_kernel(own, r1, r2, r3, keep_ref, send_ref):
     def total(j, i):
         return own[j, i] + r1[j, i].astype(F32) + r2[j, i].astype(F32) + r3[j, i].astype(F32)
 
-    for i, send in ((0, send_k), (1, send_v)):
-        send[...] = total(1, i).astype(BF16)
+    for i in range(2):
+        send_ref[i] = total(1, i).astype(BF16)
         keep_ref[i] = total(0, i)
 
 
@@ -214,25 +201,18 @@
     return (grad - unit * jnp.mean(grad * unit, axis=-1, keepdims=True)) * (1.0 / root)
 
 
-def q_out_kernel(own, own_gain, r1, r2, r3, raw, gain_ref, out, sums):
+def q_out_kernel(own, r1, r2, r3, raw, gain_ref, out):
     gain = gain_of(text_mask(q_block(0, here())), gain_ref)
     for h in range(NH):
-        rows = slice(h * BR, (h + 1) * BR)
-        grad = own[h] + r1[rows, :].astype(F32) + r2[rows, :].astype(F32) + r3[rows, :].astype(F32)
+        grad = own[h] + r1[h].astype(F32) + r2[h].astype(F32) + r3[h].astype(F32)
         out[h] = back(grad, raw[0, h], gain).astype(BF16)
 
-    def whole(ref):
-        tail = ref[NH * BR :, :].astype(F32)
-        return (tail[0:8] + tail[8:16]) + tail[16:24]
-
-    sums[...] = (own_gain[...] + whole(r1)) + (whole(r2) + whole(r3))
-
-
-def kv_out_kernel(keep, got_k, got_v, raw, gain_ref, k_out, v_out):
+
+def kv_out_kernel(keep, got, raw, gain_ref, k_out, v_out):
     gain = gain_of(text_mask(q_block(0, here())), gain_ref)
     for h in range(NH):
-        k_out[h] = back(keep[0, h] + got_k[h].astype(F32), raw[0, h], gain).astype(BF16)
-        v_out[h] = (keep[1, h] + got_v[h].astype(F32)).astype(BF16)
+        k_out[h] = back(keep[0, h] + got[0, h].astype(F32), raw[0, h], gain).astype(BF16)
+        v_out[h] = (keep[1, h] + got[1, h].astype(F32)).astype(BF16)
 
 
 def kernel_call(kernel, outs, args, scratch=(), flops=0):
@@ -313,7 +293,7 @@
     for k in (2, 1, 3, 0):
         first, last = k == 2, k == 0
         outs = [(kv_part, F32 if last else BF16)]
-        outs += [(part, F32)] + [((MESSAGE, HD), BF16)] * 3 if last else [whole_dq]
+        outs += [(part, F32)] + [(part, BF16)] * 3 if last else [whole_dq]
         args = [*stats, *kvs[NZ * k : NZ * k + NZ], *(qds if last else ()), qn, do, kn_own, v_own, kn_pair, v_pair, *carried]
         got = kernel_call(
             functools.partial(grad_kernel, k, first, last),
@@ -327,22 +307,19 @@
         else:
             kv_got.append(give(got[0], "x", NX, k))
             carried = got[1:]
-    m1, m2, m3 = messages
-    m2 = swap(after(m2, kv_got[0]), "zq", NQ, 2)
-    m1, m3 = swap(m1, "zq", NQ, 1), swap(m3, "zq", NQ, 3)
-    q_out, gains = kernel_call(
-        q_out_kernel, [(part, BF16), ((8, HD), F32)], [dq_own, gains, m1, m2, m3, qd, q_gain]
-    )
+    gains = summed(gains, "zq", NQ, kv_got[0])
+    messages = [swap(m, "zq", NQ, k) for k, m in enumerate(messages, 1)]
     gains = gains + swap(gains, "core", 2, 1)
     gains = gains + mirror(gains)
-    keep, send_k, send_v = kernel_call(
-        pair_sum_kernel, [((2, NH, BR, HD), F32), (part, BF16), (part, BF16)], [own, *kv_got]
-    )
-    got_k = mirror(send_k)
-    gains = summed(after(gains, send_k), "y", 4, got_k)
-    gains = summed(gains, "x", NX)
+    keep, send = kernel_call(
+        pair_sum_kernel, [((2, NH, BR, HD), F32), ((2, NH, BR, HD), BF16)], [own, *kv_got]
+    )
+    got = mirror(send)
+    gains = summed(gains, "y", 4, *messages)
+    (q_out,) = kernel_call(q_out_kernel, [(part, BF16)], [dq_own, *messages, qd, q_gain])
+    gains = summed(after(gains, send), "x", NX, got)
     k_out, v_out = kernel_call(
-        kv_out_kernel, [(part, BF16)] * 2, [keep, got_k, mirror(send_v), kv, k_gain]
+        kv_out_kernel, [(part, BF16)] * 2, [keep, got, kv, k_gain]
     )
 
     return (

time: 96 us -> 95.4 us (level)
  waiting for transfers between devices: 27.3 us -> 26.1 us
    ppermute x3, waiting for transfers between devices: 5.38 us -> 0.01 us  [give(): return lax.ppermute(a, axis, [(i, (i + k) % n) for i in range(n)])]
    ppermute x16 -> x19, starting transfers between devices: 20.8 us -> 26.1 us  [swap(): return lax.ppermute(a, axis, [(i, i ^ k) for i in range(n)])]
    ppermute x4 -> x3, starting transfers between devices: 13.7 us -> 8.98 us  [mirror(): return lax.ppermute(a, ('zk', 'zq'), [(i, n - 1 - i) for i in range(n)])]
    ppermute x4 -> x3, waiting for transfers between devices: 4.76 us -> 7.43 us  [mirror(): return lax.ppermute(a, ('zk', 'zq'), [(i, n - 1 - i) for i in range(n)])]
    ppermute x16 -> x19, waiting for transfers between devices: 10.9 us -> 12.4 us  [swap(): return lax.ppermute(a, axis, [(i, i ^ k) for i in range(n)])]
  transfers between devices with their start and end apart: 29 -> 31, of which waited for: 14 -> 13; matrix products, arithmetic and copies ran while one was open for 0% -> 0% of each run, Pallas kernels for 12% -> 11%
where the time goes in v4:
time: 95.4 us; the launch traced here: 95.3 us
  starting transfers between devices  50.7 us (53%)
  waiting for transfers between devices  26.1 us (27%)
  Pallas kernels  16.2 us (17%)
  other arithmetic  1.06 us (1%)
    ppermute x19, starting transfers between devices, swap(): return lax.ppermute(a, axis, [(i, i ^ k) for i in range(n)])  26.1 us
    pallas_call x9, Pallas kernels, kernel_call(): pl.pallas_call(kernel, out_shape=[jax.ShapeDtypeStruct(s, d) for s, d in...  16.2 us
    ppermute x19, waiting for transfers between devices, swap(): return lax.ppermute(a, axis, [(i, i ^ k) for i in range(n)])  12.4 us
    ppermute x6, starting transfers between devices, fetch(): return lax.ppermute(a, axis, [((i + k) % n, i) for i in range(n)])  11 us
    ppermute x3, starting transfers between devices, mirror(): return lax.ppermute(a, ('zk', 'zq'), [(i, n - 1 - i) for i in range(n)])  8.98 us
    ppermute x3, waiting for transfers between devices, mirror(): return lax.ppermute(a, ('zk', 'zq'), [(i, n - 1 - i) for i in range(n)])  7.43 us
    ppermute x6, waiting for transfers between devices, fetch(): return lax.ppermute(a, axis, [((i + k) % n, i) for i in range(n)])  6.19 us
    ppermute x3, starting transfers between devices, give(): return lax.ppermute(a, axis, [(i, (i + k) % n) for i in range(n)])  4.57 us
  transfers between devices with their start and end apart: 31, of which 13 were waited for; matrix products, arithmetic and copies ran while one was open for 0% of the time, Pallas kernels for 11%

profile of v4, /device:TPU:32, one launch (start us, length us, event | category | flops | bytes accessed | tf_op | source)
XLA Modules:
  0.0 95.3 jit_solution(9841415376971730352)
XLA Ops:
  1.7 2.0 %collective-permute-start.5 = (bf16[2,3,144,128]{3,2,1,0:T(8,128)(2,1)S(1)}, bf16[2,3,144,128]{3,2,1,0:T(8,128)(2,1)S(1)}, u32[]{:S(2)}, u32[]{:S(2)}) collective-permute-start(bf16[2,3,144,128]{3,2,1,0:T(8,128)(2,1)S(1)} %pad_maximum_fusion.q0.refs_6_.raw), channel_id=1, source_target_pairs={{0,96},{32,64},{64,32},{96,0},{1,97},{33,65},{65,33},{97,1},{2,98}... | collective-permute-start | bytes 663560 | tf_op jit(solution)/shard_map/ppermute | solution.py:237
  3.7 5.0 %collective-permute-start.3 = (bf16[2,3,144,128]{3,2,1,0:T(8,128)(2,1)S(1)}, bf16[2,3,144,128]{3,2,1,0:T(8,128)(2,1)S(1)}, u32[]{:S(2)}, u32[]{:S(2)}) collective-permute-start(bf16[2,3,144,128]{3,2,1,0:T(8,128)(2,1)S(1)} %pad_maximum_fusion.1.kv0.refs_4_.raw), channel_id=1, source_target_pairs={{0,224},{32,192},{64,160},{96,128},{128,96},{160,64},{192,32},{224... | collective-permute-start | bytes 663560 | tf_op jit(solution)/shard_map/ppermute | solution.py:246
  8.7 3.0 %collective-permute-start.2 = (bf16[2,3,144,128]{3,2,1,0:T(8,128)(2,1)S(1)}, bf16[2,3,144,128]{3,2,1,0:T(8,128)(2,1)S(1)}, u32[]{:S(2)}, u32[]{:S(2)}) collective-permute-start(bf16[2,3,144,128]{3,2,1,0:T(8,128)(2,1)S(1)} %pad_maximum_fusion.1.kv0.refs_4_.raw), channel_id=1, source_target_pairs={{16,0},{24,8},{0,16},{8,24},{17,1},{25,9},{1,17},{9,25},{18,2},{26... | collective-permute-start | bytes 663560 | tf_op jit(solution)/shard_map/ppermute | solution.py:233
  12.4 2.6 %collective-permute-start = (bf16[2,3,144,128]{3,2,1,0:T(8,128)(2,1)S(1)}, bf16[2,3,144,128]{3,2,1,0:T(8,128)(2,1)S(1)}, u32[]{:S(2)}, u32[]{:S(2)}) collective-permute-start(bf16[2,3,144,128]{3,2,1,0:T(8,128)(2,1)S(1)} %pad_maximum_fusion.1.kv0.refs_4_.raw), channel_id=1, source_target_pairs={{8,0},{16,8},{24,16},{0,24},{9,1},{17,9},{25,17},{1,25},{10,2},{18... | collective-permute-start | bytes 663560 | tf_op jit(solution)/shard_map/ppermute | solution.py:233
  15.0 1.5 %collective-permute-start.6 = (bf16[2,3,144,128]{3,2,1,0:T(8,128)(2,1)S(1)}, bf16[2,3,144,128]{3,2,1,0:T(8,128)(2,1)S(1)}, u32[]{:S(2)}, u32[]{:S(2)}) collective-permute-start(bf16[2,3,144,128]{3,2,1,0:T(8,128)(2,1)S(1)} %pad_maximum_fusion.q0.refs_6_.raw), channel_id=1, source_target_pairs={{0,64},{32,96},{64,0},{96,32},{1,65},{33,97},{65,1},{97,33},{2,66}... | collective-permute-start | bytes 663560 | tf_op jit(solution)/shard_map/ppermute | solution.py:237
  16.5 2.3 %collective-permute-done.3.kv0.refs_5_ = bf16[2,3,144,128]{3,2,1,0:T(8,128)(2,1)S(1)} collective-permute-done((bf16[2,3,144,128]{3,2,1,0:T(8,128)(2,1)S(1)}, bf16[2,3,144,128]{3,2,1,0:T(8,128)(2,1)S(1)}, u32[]{:S(2)}, u32[]{:S(2)}) %collective-permute-start.3) | collective-permute-done | bytes 221216 | tf_op jit(solution)/shard_map/ppermute | solution.py:246
  18.8 2.8 %collective-permute-done.1.kv3.refs_4_ = bf16[2,3,144,128]{3,2,1,0:T(8,128)(2,1)S(1)} collective-permute-done((bf16[2,3,144,128]{3,2,1,0:T(8,128)(2,1)S(1)}, bf16[2,3,144,128]{3,2,1,0:T(8,128)(2,1)S(1)}, u32[]{:S(2)}, u32[]{:S(2)}) %collective-permute-start.1) | collective-permute-done | bytes 221216 | tf_op jit(solution)/shard_map/ppermute | solution.py:233
  22.7 1.5 %collective-permute-start.9 = (bf16[2,3,144,128]{3,2,1,0:T(8,128)(2,1)S(1)}, bf16[2,3,144,128]{3,2,1,0:T(8,128)(2,1)S(1)}, u32[]{:S(2)}, u32[]{:S(2)}) collective-permute-start(bf16[2,3,144,128]{3,2,1,0:T(8,128)(2,1)S(1)} %collective-permute-done.3.kv0.refs_5_), channel_id=1, source_target_pairs={{24,0},{0,8},{8,16},{16,24},{25,1},{1,9},{9,17},{17,25},{26,2},{2,... | collective-permute-start | bytes 663560 | tf_op jit(solution)/shard_map/ppermute | solution.py:233
  24.2 2.6 %collective-permute-start.8 = (bf16[2,3,144,128]{3,2,1,0:T(8,128)(2,1)S(1)}, bf16[2,3,144,128]{3,2,1,0:T(8,128)(2,1)S(1)}, u32[]{:S(2)}, u32[]{:S(2)}) collective-permute-start(bf16[2,3,144,128]{3,2,1,0:T(8,128)(2,1)S(1)} %collective-permute-done.3.kv0.refs_5_), channel_id=1, source_target_pairs={{16,0},{24,8},{0,16},{8,24},{17,1},{25,9},{1,17},{9,25},{18,2},{26... | collective-permute-start | bytes 663560 | tf_op jit(solution)/shard_map/ppermute | solution.py:233
  27.4 2.3 %collective-permute-done.4.q1.refs_7_ = bf16[2,3,144,128]{3,2,1,0:T(8,128)(2,1)S(1)} collective-permute-done((bf16[2,3,144,128]{3,2,1,0:T(8,128)(2,1)S(1)}, bf16[2,3,144,128]{3,2,1,0:T(8,128)(2,1)S(1)}, u32[]{:S(2)}, u32[]{:S(2)}) %collective-permute-start.4) | collective-permute-done | bytes 221216 | tf_op jit(solution)/shard_map/ppermute | solution.py:237
  29.7 2.7 %shard_map.101 = (f32[16,576]{1,0:T(8,128)S(1)}, bf16[3,576,128]{2,1,0:T(8,128)(2,1)S(1)}, bf16[3,576,128]{2,1,0:T(8,128)(2,1)S(1)}, bf16[3,576,128]{2,1,0:T(8,128)(2,1)S(1)}, bf16[3,576,128]{2,1,0:T(8,128)(2,1)S(1)}) custom-call(bf16[2,3,144,128]{3,2,1,0:T(8,128)(2,1)S(1)} %pad_maximum_fusion.q0.refs_6_.raw, ...), custom_call_target="tpu_custom_call" | custom-call | flops 509607936 | bytes 1771520 | tf_op jit(solution)/shard_map/pallas_call | solution.py:221
  32.4 3.3 %collective-permute-done.8.kv2.refs_5_ = bf16[2,3,144,128]{3,2,1,0:T(8,128)(2,1)S(1)} collective-permute-done((bf16[2,3,144,128]{3,2,1,0:T(8,128)(2,1)S(1)}, bf16[2,3,144,128]{3,2,1,0:T(8,128)(2,1)S(1)}, u32[]{:S(2)}, u32[]{:S(2)}) %collective-permute-start.8) | collective-permute-done | bytes 221216 | tf_op jit(solution)/shard_map/ppermute | solution.py:233
  35.7 2.4 %shard_map.102 = (f32[16,576]{1,0:T(8,128)S(1)}, bf16[3,576,128]{2,1,0:T(8,128)(2,1)S(1)}, bf16[3,576,128]{2,1,0:T(8,128)(2,1)S(1)}) custom-call(f32[16,576]{1,0:T(8,128)S(1)} %get-tuple-element.56.before_ref, bf16[3,576,128]{2,1,0:T(8,128)(2,1)S(1)} %get-tuple-element.57.qn_ref.refs_6_.refs_10_, ...), custom_call_target="tpu_custom_call" | custom-call | flops 509607936 | bytes 1807360 | tf_op jit(solution)/shard_map/pallas_call | solution.py:221
  39.2 2.4 %collective-permute-start.11 = (f32[16,576]{1,0:T(8,128)S(1)}, f32[16,576]{1,0:T(8,128)S(1)}, u32[]{:S(2)}, u32[]{:S(2)}) collective-permute-start(f32[16,576]{1,0:T(8,128)S(1)} %get-tuple-element.60.refs_0_), channel_id=1, source_target_pairs={{0,64},{32,96},{64,0},{96,32},{1,65},{33,97},{65,1},{97,33},{2,66}... | collective-permute-start | bytes 110600 | tf_op jit(solution)/shard_map/ppermute | solution.py:237
  42.2 1.9 %collective-permute-done.11.refs_2_ = f32[16,576]{1,0:T(8,128)S(1)} collective-permute-done((f32[16,576]{1,0:T(8,128)S(1)}, f32[16,576]{1,0:T(8,128)S(1)}, u32[]{:S(2)}, u32[]{:S(2)}) %collective-permute-start.11) | collective-permute-done | bytes 36896 | tf_op jit(solution)/shard_map/ppermute | solution.py:237
  44.1 1.5 %collective-permute-done.10.refs_1_ = f32[16,576]{1,0:T(8,128)S(1)} collective-permute-done((f32[16,576]{1,0:T(8,128)S(1)}, f32[16,576]{1,0:T(8,128)S(1)}, u32[]{:S(2)}, u32[]{:S(2)}) %collective-permute-start.10) | collective-permute-done | bytes 36896 | tf_op jit(solution)/shard_map/ppermute | solution.py:237
  45.5 2.1 %shard_map.103 = (bf16[2,2,3,144,128]{4,3,2,1,0:T(8,128)(2,1)S(1)}, f32[3,576,128]{2,1,0:T(8,128)S(1)}, f32[8,128]{1,0:T(8,128)S(1)}) custom-call(f32[16,576]{1,0:T(8,128)S(1)} %get-tuple-element.60.refs_0_, f32[16,576]{1,0:T(8,128)S(1)} %collective-permute-done.10.refs_1_, f32[16,576]{1,0:T(8,128)S(1)} %collective-permute-done.11.refs_2_, ...), custom_call_target="tpu_custom_call" | custom-call | flops 764411904 | bytes 3244032 | tf_op jit(solution)/shard_map/pallas_call | solution.py:221
  47.6 2.5 %collective-permute-start.16 = (bf16[2,2,3,144,128]{4,3,2,1,0:T(8,128)(2,1)S(1)}, bf16[2,2,3,144,128]{4,3,2,1,0:T(8,128)(2,1)S(1)}, u32[]{:S(2)}, u32[]{:S(2)}) collective-permute-start(bf16[2,2,3,144,128]{4,3,2,1,0:T(8,128)(2,1)S(1)} %get-tuple-element.76), channel_id=1, source_target_pairs={{0,16},{8,24},{16,0},{24,8},{1,17},{9,25},{17,1},{25,9},{2,18},{10... | collective-permute-start | bytes 1327112 | tf_op jit(solution)/shard_map/ppermute | solution.py:241
  50.1 2.1 %shard_map.104 = (bf16[2,2,3,144,128]{4,3,2,1,0:T(8,128)(2,1)S(1)}, f32[3,576,128]{2,1,0:T(8,128)S(1)}, f32[8,128]{1,0:T(8,128)S(1)}) custom-call(f32[16,576]{1,0:T(8,128)S(1)} %get-tuple-element.60.refs_0_, f32[16,576]{1,0:T(8,128)S(1)} %collective-permute-done.10.refs_1_, f32[16,576]{1,0:T(8,128)S(1)} %collective-permute-done.11.refs_2_, ...), custom_call_target="tpu_custom_call" | custom-call | flops 764411904 | bytes 4132864 | tf_op jit(solution)/shard_map/pallas_call | solution.py:221
  52.3 2.1 %shard_map.105 = (bf16[2,2,3,144,128]{4,3,2,1,0:T(8,128)(2,1)S(1)}, f32[3,576,128]{2,1,0:T(8,128)S(1)}, f32[8,128]{1,0:T(8,128)S(1)}) custom-call(f32[16,576]{1,0:T(8,128)S(1)} %get-tuple-element.60.refs_0_, f32[16,576]{1,0:T(8,128)S(1)} %collective-permute-done.10.refs_1_, f32[16,576]{1,0:T(8,128)S(1)} %collective-permute-done.11.refs_2_, ...), custom_call_target="tpu_custom_call" | custom-call | flops 764411904 | bytes 4132864 | tf_op jit(solution)/shard_map/pallas_call | solution.py:221
  54.4 1.9 %collective-permute-start.18 = (bf16[2,2,3,144,128]{4,3,2,1,0:T(8,128)(2,1)S(1)}, bf16[2,2,3,144,128]{4,3,2,1,0:T(8,128)(2,1)S(1)}, u32[]{:S(2)}, u32[]{:S(2)}) collective-permute-start(bf16[2,2,3,144,128]{4,3,2,1,0:T(8,128)(2,1)S(1)} %get-tuple-element.78), channel_id=1, source_target_pairs={{0,24},{8,0},{16,8},{24,16},{1,25},{9,1},{17,9},{25,17},{2,26},{10... | collective-permute-start | bytes 1327112 | tf_op jit(solution)/shard_map/ppermute | solution.py:241
  56.5 2.7 %shard_map.106 = (f32[2,2,3,144,128]{4,3,2,1,0:T(8,128)S(1)}, f32[3,144,128]{2,1,0:T(8,128)S(1)}, bf16[3,144,128]{2,1,0:T(8,128)(2,1)S(1)}, bf16[3,144,128]{2,1,...) custom-call(f32[16,576]{1,0:T(8,128)S(1)} %get-tuple-element.60.refs_0_, ...), custom_call_target="tpu_custom_call" | custom-call | flops 764411904 | bytes 5017600 | tf_op jit(solution)/shard_map/pallas_call | solution.py:221
  59.2 1.1 %collective-permute-start.22 = (f32[8,128]{1,0:T(8,128)S(1)}, f32[8,128]{1,0:T(8,128)S(1)}, u32[]{:S(2)}, u32[]{:S(2)}) collective-permute-start(f32[8,128]{1,0:T(8,128)S(1)} %get-tuple-element.84), channel_id=1, source_target_pairs={{0,96},{32,64},{64,32},{96,0},{1,97},{33,65},{65,33},{97,1},{2,98}... | collective-permute-start | bytes 12296 | tf_op jit(solution)/shard_map/ppermute | solution.py:237
  60.3 2.0 %collective-permute-start.21 = (f32[8,128]{1,0:T(8,128)S(1)}, f32[8,128]{1,0:T(8,128)S(1)}, u32[]{:S(2)}, u32[]{:S(2)}) collective-permute-start(f32[8,128]{1,0:T(8,128)S(1)} %get-tuple-element.84), channel_id=1, source_target_pairs={{0,64},{32,96},{64,0},{96,32},{1,65},{33,97},{65,1},{97,33},{2,66}... | collective-permute-start | bytes 12296 | tf_op jit(solution)/shard_map/ppermute | solution.py:237
  62.9 2.4 %collective-permute-start.20 = (f32[8,128]{1,0:T(8,128)S(1)}, f32[8,128]{1,0:T(8,128)S(1)}, u32[]{:S(2)}, u32[]{:S(2)}) collective-permute-start(f32[8,128]{1,0:T(8,128)S(1)} %get-tuple-element.84), channel_id=1, source_target_pairs={{0,32},{32,0},{64,96},{96,64},{1,33},{33,1},{65,97},{97,65},{2,34}... | collective-permute-start | bytes 12296 | tf_op jit(solution)/shard_map/ppermute | solution.py:237
  65.3 1.6 %collective-permute-done.20 = f32[8,128]{1,0:T(8,128)S(1)} collective-permute-done((f32[8,128]{1,0:T(8,128)S(1)}, f32[8,128]{1,0:T(8,128)S(1)}, u32[]{:S(2)}, u32[]{:S(2)}) %collective-permute-start.20) | collective-permute-done | bytes 4128 | tf_op jit(solution)/shard_map/ppermute | solution.py:237
  67.0 2.1 %collective-permute-start.13 = (bf16[3,144,128]{2,1,0:T(8,128)(2,1)S(1)}, bf16[3,144,128]{2,1,0:T(8,128)(2,1)S(1)}, u32[]{:S(2)}, u32[]{:S(2)}) collective-permute-start(bf16[3,144,128]{2,1,0:T(8,128)(2,1)S(1)} %get-tuple-element.72), channel_id=1, source_target_pairs={{0,32},{32,0},{64,96},{96,64},{1,33},{33,1},{65,97},{97,65},{2,34}... | collective-permute-start | bytes 331784 | tf_op jit(solution)/shard_map/ppermute | solution.py:237
  71.0 5.1 %collective-permute-done.24 = f32[8,128]{1,0:T(8,128)S(1)} collective-permute-done((f32[8,128]{1,0:T(8,128)S(1)}, f32[8,128]{1,0:T(8,128)S(1)}, u32[]{:S(2)}, u32[]{:S(2)}) %collective-permute-start.24) | collective-permute-done | bytes 4128 | tf_op jit(solution)/shard_map/ppermute | solution.py:246
  77.2 3.0 %collective-permute-start.27 = (f32[8,128]{1,0:T(8,128)S(1)}, f32[8,128]{1,0:T(8,128)S(1)}, u32[]{:S(2)}, u32[]{:S(2)}) collective-permute-start(f32[8,128]{1,0:T(8,128)S(1)} %add.37), channel_id=1, source_target_pairs={{0,6},{2,4},{4,2},{6,0},{1,7},{3,5},{5,3},{7,1},{8,14},{10,12},{12... | collective-permute-start | bytes 12296 | tf_op jit(solution)/shard_map/ppermute | solution.py:237
  81.6 3.0 %collective-permute-start.19 = (bf16[2,3,144,128]{3,2,1,0:T(8,128)(2,1)S(1)}, bf16[2,3,144,128]{3,2,1,0:T(8,128)(2,1)S(1)}, u32[]{:S(2)}, u32[]{:S(2)}) collective-permute-start(bf16[2,3,144,128]{3,2,1,0:T(8,128)(2,1)S(1)} %get-tuple-element.80), channel_id=1, source_target_pairs={{0,224},{32,192},{64,160},{96,128},{128,96},{160,64},{192,32},{224... | collective-permute-start | bytes 663560 | tf_op jit(solution)/shard_map/ppermute | solution.py:246
  85.4 3.3 %collective-permute-start.30 = (f32[8,128]{1,0:T(8,128)S(1)}, f32[8,128]{1,0:T(8,128)S(1)}, u32[]{:S(2)}, u32[]{:S(2)}) collective-permute-start(f32[8,128]{1,0:T(8,128)S(1)} %add_add_fusion.1), channel_id=1, source_target_pairs={{0,24},{8,16},{16,8},{24,0},{1,25},{9,17},{17,9},{25,1},{2,26},{10... | collective-permute-start | bytes 12296 | tf_op jit(solution)/shard_map/ppermute | solution.py:237
  90.6 3.2 %collective-permute-done.29 = f32[8,128]{1,0:T(8,128)S(1)} collective-permute-done((f32[8,128]{1,0:T(8,128)S(1)}, f32[8,128]{1,0:T(8,128)S(1)}, u32[]{:S(2)}, u32[]{:S(2)}) %collective-permute-start.29) | collective-permute-done | bytes 4128 | tf_op jit(solution)/shard_map/ppermute | solution.py:237
  (55 shorter events, 14.4 us)
Async XLA Ops:
  1.7 13.3 %collective-permute-start.5 = (bf16[2,3,144,128]{3,2,1,0:T(8,128)(2,1)S(1)}, bf16[2,3,144,128]{3,2,1,0:T(8,128)(2,1)S(1)}, u32[]{:S(2)}, u32[]{:S(2)}) collective-permute-start(bf16[2,3,144,128]{3,2,1,0:T(8,128)(2,1)S(1)} %pad_maximum_fusion.q0.refs_6_.raw), channel_id=1, source_target_pairs={{0,96},{32,64},{64,32},{96,0},{1,97},{33,65},{65,33},{97,1},{2,98}... | collective-permute-start | bytes 663560 | tf_op jit(solution)/shard_map/ppermute | solution.py:237
  3.7 26.0 %copy-start.1 = (f32[2,128]{1,0:T(2,128)S(1)}, f32[2,128]{1,0:T(2,128)}, u32[]{:S(2)}) copy-start(f32[2,128]{1,0:T(2,128)} %gain_ref.3) | copy-start | bytes 3076
  3.7 15.1 %collective-permute-start.3 = (bf16[2,3,144,128]{3,2,1,0:T(8,128)(2,1)S(1)}, bf16[2,3,144,128]{3,2,1,0:T(8,128)(2,1)S(1)}, u32[]{:S(2)}, u32[]{:S(2)}) collective-permute-start(bf16[2,3,144,128]{3,2,1,0:T(8,128)(2,1)S(1)} %pad_maximum_fusion.1.kv0.refs_4_.raw), channel_id=1, source_target_pairs={{0,224},{32,192},{64,160},{96,128},{128,96},{160,64},{192,32},{224... | collective-permute-start | bytes 663560 | tf_op jit(solution)/shard_map/ppermute | solution.py:246
  8.7 10.0 %collective-permute-start.2 = (bf16[2,3,144,128]{3,2,1,0:T(8,128)(2,1)S(1)}, bf16[2,3,144,128]{3,2,1,0:T(8,128)(2,1)S(1)}, u32[]{:S(2)}, u32[]{:S(2)}) collective-permute-start(bf16[2,3,144,128]{3,2,1,0:T(8,128)(2,1)S(1)} %pad_maximum_fusion.1.kv0.refs_4_.raw), channel_id=1, source_target_pairs={{16,0},{24,8},{0,16},{8,24},{17,1},{25,9},{1,17},{9,25},{18,2},{26... | collective-permute-start | bytes 663560 | tf_op jit(solution)/shard_map/ppermute | solution.py:233
  11.8 9.8 %collective-permute-start.1 = (bf16[2,3,144,128]{3,2,1,0:T(8,128)(2,1)S(1)}, bf16[2,3,144,128]{3,2,1,0:T(8,128)(2,1)S(1)}, u32[]{:S(2)}, u32[]{:S(2)}) collective-permute-start(bf16[2,3,144,128]{3,2,1,0:T(8,128)(2,1)S(1)} %pad_maximum_fusion.1.kv0.refs_4_.raw), channel_id=1, source_target_pairs={{24,0},{0,8},{8,16},{16,24},{25,1},{1,9},{9,17},{17,25},{26,2},{2,... | collective-permute-start | bytes 663560 | tf_op jit(solution)/shard_map/ppermute | solution.py:233
  12.4 9.3 %collective-permute-start = (bf16[2,3,144,128]{3,2,1,0:T(8,128)(2,1)S(1)}, bf16[2,3,144,128]{3,2,1,0:T(8,128)(2,1)S(1)}, u32[]{:S(2)}, u32[]{:S(2)}) collective-permute-start(bf16[2,3,144,128]{3,2,1,0:T(8,128)(2,1)S(1)} %pad_maximum_fusion.1.kv0.refs_4_.raw), channel_id=1, source_target_pairs={{8,0},{16,8},{24,16},{0,24},{9,1},{17,9},{25,17},{1,25},{10,2},{18... | collective-permute-start | bytes 663560 | tf_op jit(solution)/shard_map/ppermute | solution.py:233
  15.0 12.4 %collective-permute-start.6 = (bf16[2,3,144,128]{3,2,1,0:T(8,128)(2,1)S(1)}, bf16[2,3,144,128]{3,2,1,0:T(8,128)(2,1)S(1)}, u32[]{:S(2)}, u32[]{:S(2)}) collective-permute-start(bf16[2,3,144,128]{3,2,1,0:T(8,128)(2,1)S(1)} %pad_maximum_fusion.q0.refs_6_.raw), channel_id=1, source_target_pairs={{0,64},{32,96},{64,0},{96,32},{1,65},{33,97},{65,1},{97,33},{2,66}... | collective-permute-start | bytes 663560 | tf_op jit(solution)/shard_map/ppermute | solution.py:237
  21.7 8.0 %collective-permute-start.4 = (bf16[2,3,144,128]{3,2,1,0:T(8,128)(2,1)S(1)}, bf16[2,3,144,128]{3,2,1,0:T(8,128)(2,1)S(1)}, u32[]{:S(2)}, u32[]{:S(2)}) collective-permute-start(bf16[2,3,144,128]{3,2,1,0:T(8,128)(2,1)S(1)} %pad_maximum_fusion.q0.refs_6_.raw), channel_id=1, source_target_pairs={{0,32},{32,0},{64,96},{96,64},{1,33},{33,1},{65,97},{97,65},{2,34}... | collective-permute-start | bytes 663560 | tf_op jit(solution)/shard_map/ppermute | solution.py:237
  22.7 9.7 %collective-permute-start.9 = (bf16[2,3,144,128]{3,2,1,0:T(8,128)(2,1)S(1)}, bf16[2,3,144,128]{3,2,1,0:T(8,128)(2,1)S(1)}, u32[]{:S(2)}, u32[]{:S(2)}) collective-permute-start(bf16[2,3,144,128]{3,2,1,0:T(8,128)(2,1)S(1)} %collective-permute-done.3.kv0.refs_5_), channel_id=1, source_target_pairs={{24,0},{0,8},{8,16},{16,24},{25,1},{1,9},{9,17},{17,25},{26,2},{2,... | collective-permute-start | bytes 663560 | tf_op jit(solution)/shard_map/ppermute | solution.py:233
  24.2 11.5 %collective-permute-start.8 = (bf16[2,3,144,128]{3,2,1,0:T(8,128)(2,1)S(1)}, bf16[2,3,144,128]{3,2,1,0:T(8,128)(2,1)S(1)}, u32[]{:S(2)}, u32[]{:S(2)}) collective-permute-start(bf16[2,3,144,128]{3,2,1,0:T(8,128)(2,1)S(1)} %collective-permute-done.3.kv0.refs_5_), channel_id=1, source_target_pairs={{16,0},{24,8},{0,16},{8,24},{17,1},{25,9},{1,17},{9,25},{18,2},{26... | collective-permute-start | bytes 663560 | tf_op jit(solution)/shard_map/ppermute | solution.py:233
  26.8 8.9 %collective-permute-start.7 = (bf16[2,3,144,128]{3,2,1,0:T(8,128)(2,1)S(1)}, bf16[2,3,144,128]{3,2,1,0:T(8,128)(2,1)S(1)}, u32[]{:S(2)}, u32[]{:S(2)}) collective-permute-start(bf16[2,3,144,128]{3,2,1,0:T(8,128)(2,1)S(1)} %collective-permute-done.3.kv0.refs_5_), channel_id=1, source_target_pairs={{8,0},{16,8},{24,16},{0,24},{9,1},{17,9},{25,17},{1,25},{10,2},{18... | collective-permute-start | bytes 663560 | tf_op jit(solution)/shard_map/ppermute | solution.py:233
  38.0 4.1 %collective-permute-start.12 = (f32[16,576]{1,0:T(8,128)S(1)}, f32[16,576]{1,0:T(8,128)S(1)}, u32[]{:S(2)}, u32[]{:S(2)}) collective-permute-start(f32[16,576]{1,0:T(8,128)S(1)} %get-tuple-element.60.refs_0_), channel_id=1, source_target_pairs={{0,96},{32,64},{64,32},{96,0},{1,97},{33,65},{65,33},{97,1},{2,98}... | collective-permute-start | bytes 110600 | tf_op jit(solution)/shard_map/ppermute | solution.py:237
  39.2 4.9 %collective-permute-start.11 = (f32[16,576]{1,0:T(8,128)S(1)}, f32[16,576]{1,0:T(8,128)S(1)}, u32[]{:S(2)}, u32[]{:S(2)}) collective-permute-start(f32[16,576]{1,0:T(8,128)S(1)} %get-tuple-element.60.refs_0_), channel_id=1, source_target_pairs={{0,64},{32,96},{64,0},{96,32},{1,65},{33,97},{65,1},{97,33},{2,66}... | collective-permute-start | bytes 110600 | tf_op jit(solution)/shard_map/ppermute | solution.py:237
  41.5 4.0 %collective-permute-start.10 = (f32[16,576]{1,0:T(8,128)S(1)}, f32[16,576]{1,0:T(8,128)S(1)}, u32[]{:S(2)}, u32[]{:S(2)}) collective-permute-start(f32[16,576]{1,0:T(8,128)S(1)} %get-tuple-element.60.refs_0_), channel_id=1, source_target_pairs={{0,32},{32,0},{64,96},{96,64},{1,33},{33,1},{65,97},{97,65},{2,34}... | collective-permute-start | bytes 110600 | tf_op jit(solution)/shard_map/ppermute | solution.py:237
  47.6 19.3 %collective-permute-start.16 = (bf16[2,2,3,144,128]{4,3,2,1,0:T(8,128)(2,1)S(1)}, bf16[2,2,3,144,128]{4,3,2,1,0:T(8,128)(2,1)S(1)}, u32[]{:S(2)}, u32[]{:S(2)}) collective-permute-start(bf16[2,2,3,144,128]{4,3,2,1,0:T(8,128)(2,1)S(1)} %get-tuple-element.76), channel_id=1, source_target_pairs={{0,16},{8,24},{16,0},{24,8},{1,17},{9,25},{17,1},{25,9},{2,18},{10... | collective-permute-start | bytes 1327112 | tf_op jit(solution)/shard_map/ppermute | solution.py:241
  54.4 25.9 %collective-permute-start.18 = (bf16[2,2,3,144,128]{4,3,2,1,0:T(8,128)(2,1)S(1)}, bf16[2,2,3,144,128]{4,3,2,1,0:T(8,128)(2,1)S(1)}, u32[]{:S(2)}, u32[]{:S(2)}) collective-permute-start(bf16[2,2,3,144,128]{4,3,2,1,0:T(8,128)(2,1)S(1)} %get-tuple-element.78), channel_id=1, source_target_pairs={{0,24},{8,0},{16,8},{24,16},{1,25},{9,1},{17,9},{25,17},{2,26},{10... | collective-permute-start | bytes 1327112 | tf_op jit(solution)/shard_map/ppermute | solution.py:241
  56.3 24.5 %collective-permute-start.17 = (bf16[2,2,3,144,128]{4,3,2,1,0:T(8,128)(2,1)S(1)}, bf16[2,2,3,144,128]{4,3,2,1,0:T(8,128)(2,1)S(1)}, u32[]{:S(2)}, u32[]{:S(2)}) collective-permute-start(bf16[2,2,3,144,128]{4,3,2,1,0:T(8,128)(2,1)S(1)} %get-tuple-element.77), channel_id=1, source_target_pairs={{0,8},{8,16},{16,24},{24,0},{1,9},{9,17},{17,25},{25,1},{2,10},{10... | collective-permute-start | bytes 1327112 | tf_op jit(solution)/shard_map/ppermute | solution.py:241
  59.2 3.7 %collective-permute-start.22 = (f32[8,128]{1,0:T(8,128)S(1)}, f32[8,128]{1,0:T(8,128)S(1)}, u32[]{:S(2)}, u32[]{:S(2)}) collective-permute-start(f32[8,128]{1,0:T(8,128)S(1)} %get-tuple-element.84), channel_id=1, source_target_pairs={{0,96},{32,64},{64,32},{96,0},{1,97},{33,65},{65,33},{97,1},{2,98}... | collective-permute-start | bytes 12296 | tf_op jit(solution)/shard_map/ppermute | solution.py:237
  60.3 5.0 %collective-permute-start.21 = (f32[8,128]{1,0:T(8,128)S(1)}, f32[8,128]{1,0:T(8,128)S(1)}, u32[]{:S(2)}, u32[]{:S(2)}) collective-permute-start(f32[8,128]{1,0:T(8,128)S(1)} %get-tuple-element.84), channel_id=1, source_target_pairs={{0,64},{32,96},{64,0},{96,32},{1,65},{33,97},{65,1},{97,33},{2,66}... | collective-permute-start | bytes 12296 | tf_op jit(solution)/shard_map/ppermute | solution.py:237
  62.9 4.0 %collective-permute-start.20 = (f32[8,128]{1,0:T(8,128)S(1)}, f32[8,128]{1,0:T(8,128)S(1)}, u32[]{:S(2)}, u32[]{:S(2)}) collective-permute-start(f32[8,128]{1,0:T(8,128)S(1)} %get-tuple-element.84), channel_id=1, source_target_pairs={{0,32},{32,0},{64,96},{96,64},{1,33},{33,1},{65,97},{97,65},{2,34}... | collective-permute-start | bytes 12296 | tf_op jit(solution)/shard_map/ppermute | solution.py:237
  66.9 2.2 %collective-permute-start.23 = (f32[8,128]{1,0:T(8,128)S(1)}, f32[8,128]{1,0:T(8,128)S(1)}, u32[]{:S(2)}, u32[]{:S(2)}) collective-permute-start(f32[8,128]{1,0:T(8,128)S(1)} %add_add_fusion.2), channel_id=1, source_target_pairs={{0,1},{1,0},{2,3},{3,2},{4,5},{5,4},{6,7},{7,6},{8,9},{9,8},{10,11... | collective-permute-start | bytes 12296 | tf_op jit(solution)/shard_map/ppermute | solution.py:237
  67.0 10.2 %collective-permute-start.13 = (bf16[3,144,128]{2,1,0:T(8,128)(2,1)S(1)}, bf16[3,144,128]{2,1,0:T(8,128)(2,1)S(1)}, u32[]{:S(2)}, u32[]{:S(2)}) collective-permute-start(bf16[3,144,128]{2,1,0:T(8,128)(2,1)S(1)} %get-tuple-element.72), channel_id=1, source_target_pairs={{0,32},{32,0},{64,96},{96,64},{1,33},{33,1},{65,97},{97,65},{2,34}... | collective-permute-start | bytes 331784 | tf_op jit(solution)/shard_map/ppermute | solution.py:237
  69.2 7.0 %collective-permute-start.24 = (f32[8,128]{1,0:T(8,128)S(1)}, f32[8,128]{1,0:T(8,128)S(1)}, u32[]{:S(2)}, u32[]{:S(2)}) collective-permute-start(f32[8,128]{1,0:T(8,128)S(1)} %add.36), channel_id=1, source_target_pairs={{0,224},{32,192},{64,160},{96,128},{128,96},{160,64},{192,32},{224... | collective-permute-start | bytes 12296 | tf_op jit(solution)/shard_map/ppermute | solution.py:246
  70.1 11.4 %collective-permute-start.14 = (bf16[3,144,128]{2,1,0:T(8,128)(2,1)S(1)}, bf16[3,144,128]{2,1,0:T(8,128)(2,1)S(1)}, u32[]{:S(2)}, u32[]{:S(2)}) collective-permute-start(bf16[3,144,128]{2,1,0:T(8,128)(2,1)S(1)} %get-tuple-element.73), channel_id=1, source_target_pairs={{0,64},{32,96},{64,0},{96,32},{1,65},{33,97},{65,1},{97,33},{2,66}... | collective-permute-start | bytes 331784 | tf_op jit(solution)/shard_map/ppermute | solution.py:237
  76.2 8.4 %collective-permute-start.15 = (bf16[3,144,128]{2,1,0:T(8,128)(2,1)S(1)}, bf16[3,144,128]{2,1,0:T(8,128)(2,1)S(1)}, u32[]{:S(2)}, u32[]{:S(2)}) collective-permute-start(bf16[3,144,128]{2,1,0:T(8,128)(2,1)S(1)} %get-tuple-element.74), channel_id=1, source_target_pairs={{0,96},{32,64},{64,32},{96,0},{1,97},{33,65},{65,33},{97,1},{2,98}... | collective-permute-start | bytes 331784 | tf_op jit(solution)/shard_map/ppermute | solution.py:237
  77.2 7.3 %collective-permute-start.27 = (f32[8,128]{1,0:T(8,128)S(1)}, f32[8,128]{1,0:T(8,128)S(1)}, u32[]{:S(2)}, u32[]{:S(2)}) collective-permute-start(f32[8,128]{1,0:T(8,128)S(1)} %add.37), channel_id=1, source_target_pairs={{0,6},{2,4},{4,2},{6,0},{1,7},{3,5},{5,3},{7,1},{8,14},{10,12},{12... | collective-permute-start | bytes 12296 | tf_op jit(solution)/shard_map/ppermute | solution.py:237
  80.3 5.1 %collective-permute-start.26 = (f32[8,128]{1,0:T(8,128)S(1)}, f32[8,128]{1,0:T(8,128)S(1)}, u32[]{:S(2)}, u32[]{:S(2)}) collective-permute-start(f32[8,128]{1,0:T(8,128)S(1)} %add.37), channel_id=1, source_target_pairs={{0,4},{2,6},{4,0},{6,2},{1,5},{3,7},{5,1},{7,3},{8,12},{10,14},{12... | collective-permute-start | bytes 12296 | tf_op jit(solution)/shard_map/ppermute | solution.py:237
  80.9 4.5 %collective-permute-start.25 = (f32[8,128]{1,0:T(8,128)S(1)}, f32[8,128]{1,0:T(8,128)S(1)}, u32[]{:S(2)}, u32[]{:S(2)}) collective-permute-start(f32[8,128]{1,0:T(8,128)S(1)} %add.37), channel_id=1, source_target_pairs={{0,2},{2,0},{4,6},{6,4},{1,3},{3,1},{5,7},{7,5},{8,10},{10,8},{12,... | collective-permute-start | bytes 12296 | tf_op jit(solution)/shard_map/ppermute | solution.py:237
  81.6 12.3 %collective-permute-start.19 = (bf16[2,3,144,128]{3,2,1,0:T(8,128)(2,1)S(1)}, bf16[2,3,144,128]{3,2,1,0:T(8,128)(2,1)S(1)}, u32[]{:S(2)}, u32[]{:S(2)}) collective-permute-start(bf16[2,3,144,128]{3,2,1,0:T(8,128)(2,1)S(1)} %get-tuple-element.80), channel_id=1, source_target_pairs={{0,224},{32,192},{64,160},{96,128},{128,96},{160,64},{192,32},{224... | collective-permute-start | bytes 663560 | tf_op jit(solution)/shard_map/ppermute | solution.py:246
  85.4 5.2 %collective-permute-start.30 = (f32[8,128]{1,0:T(8,128)S(1)}, f32[8,128]{1,0:T(8,128)S(1)}, u32[]{:S(2)}, u32[]{:S(2)}) collective-permute-start(f32[8,128]{1,0:T(8,128)S(1)} %add_add_fusion.1), channel_id=1, source_target_pairs={{0,24},{8,16},{16,8},{24,0},{1,25},{9,17},{17,9},{25,1},{2,26},{10... | collective-permute-start | bytes 12296 | tf_op jit(solution)/shard_map/ppermute | solution.py:237
  88.7 5.1 %collective-permute-start.29 = (f32[8,128]{1,0:T(8,128)S(1)}, f32[8,128]{1,0:T(8,128)S(1)}, u32[]{:S(2)}, u32[]{:S(2)}) collective-permute-start(f32[8,128]{1,0:T(8,128)S(1)} %add_add_fusion.1), channel_id=1, source_target_pairs={{0,16},{8,24},{16,0},{24,8},{1,17},{9,25},{17,1},{25,9},{2,18},{10... | collective-permute-start | bytes 12296 | tf_op jit(solution)/shard_map/ppermute | solution.py:237
  88.7 5.1 %collective-permute-start.28 = (f32[8,128]{1,0:T(8,128)S(1)}, f32[8,128]{1,0:T(8,128)S(1)}, u32[]{:S(2)}, u32[]{:S(2)}) collective-permute-start(f32[8,128]{1,0:T(8,128)S(1)} %add_add_fusion.1), channel_id=1, source_target_pairs={{0,8},{8,0},{16,24},{24,16},{1,9},{9,1},{17,25},{25,17},{2,10},{10... | collective-permute-start | bytes 12296 | tf_op jit(solution)/shard_map/ppermute | solution.py:237
  (3 other events, 32.1 us)

commit v5 on v4

--- a/solution.py
+++ b/solution.py
@@ -69,14 +69,14 @@
     return pl.multiple_of((place[0] ^ slot) * BR, 16)
 
 
-def place_keys(refs, j, gk_ref, kn_ref, v_ref):
-    for k in range(NX):
+def place_keys(refs, slots, j, gk_ref, kn_ref, v_ref):
+    for at, (k, ref) in enumerate(zip(slots, refs)):
         gain = gain_of(text_mask(kv_block(k, j, here())), gk_ref)
-        rows = pl.ds(k * BR, BR)
+        rows = pl.ds(at * BR, BR)
         for h in range(NH):
-            unit, _ = unit_and_root(refs[k][0, h])
+            unit, _ = unit_and_root(ref[0, h])
             kn_ref[h, rows, :] = (unit * gain).astype(BF16)
-            v_ref[h, rows, :] = refs[k][1, h]
+            v_ref[h, rows, :] = ref[1, h]
 
 
 def fold_stats(qn_ref, do_ref, kn_ref, v_ref, before_ref, stat_ref):
@@ -84,7 +84,7 @@
         top = total = dot = None
         if before_ref is not None:
             top, total, dot = [before_ref[3 * h + i : 3 * h + i + 1, :] for i in range(3)]
-        for at in range(0, NX * BR, KC):
+        for at in range(0, kn_ref.shape[1], KC):
             rows = pl.ds(at, KC)
             s = nt_dot(kn_ref[h, rows, :], qn_ref[h]) * SCALE2
             g = nt_dot(v_ref[h, rows, :], do_ref[h])
@@ -113,13 +113,13 @@
             unit, _ = unit_and_root(ref[0, h])
             qn_ref[h, rows, :] = (unit * gain).astype(BF16)
             do_ref[h, rows, :] = ref[1, h]
-    place_keys((kv0, kv1, kv2, kv3), 0, gk_ref, kn_ref, v_ref)
+    place_keys((kv0, kv1, kv2, kv3), range(NX), 0, gk_ref, kn_ref, v_ref)
     stat_ref[...] = jnp.zeros_like(stat_ref)
     fold_stats(qn_ref, do_ref, kn_ref, v_ref, None, stat_ref)
 
 
-def pair_stat_kernel(before_ref, qn_ref, do_ref, kv0, kv1, kv2, kv3, gk_ref, stat_ref, kn_ref, v_ref):
-    place_keys((kv0, kv1, kv2, kv3), 1, gk_ref, kn_ref, v_ref)
+def pair_stat_kernel(slots, before_ref, qn_ref, do_ref, kv_a, kv_b, gk_ref, stat_ref, kn_ref, v_ref):
+    place_keys((kv_a, kv_b), slots, 1, gk_ref, kn_ref, v_ref)
     stat_ref[...] = jnp.zeros_like(stat_ref)
     fold_stats(qn_ref, do_ref, kn_ref, v_ref, before_ref, stat_ref)
 
@@ -140,7 +140,7 @@
     k_all = jnp.zeros((1, HD), F32)
     q_text = jnp.zeros((1, HD), F32)
     q_all = jnp.zeros((1, HD), F32)
-    rows = pl.ds(k * BR, BR)
+    rows, pair_rows = pl.ds(k * BR, BR), pl.ds(k // 2 * BR, BR)
     for h in range(NH):
         tops = [r[3 * h : 3 * h + 1, :] for r in s_refs]
         top = functools.reduce(jnp.maximum, tops)
@@ -148,8 +148,8 @@
         total = sum(r[3 * h + 1 : 3 * h + 2, :] * e for r, e in zip(s_refs, shares))
         row_dot = sum(r[3 * h + 2 : 3 * h + 3, :] * e for r, e in zip(s_refs, shares)) / total
         log_total = top + jnp.log2(total)
-        kn = jnp.concatenate([kn_own[h, rows, :], kn_pair[h, rows, :]], axis=0)
-        v = jnp.concatenate([v_own[h, rows, :], v_pair[h, rows, :]], axis=0)
+        kn = jnp.concatenate([kn_own[h, rows, :], kn_pair[h, pair_rows, :]], axis=0)
+        v = jnp.concatenate([v_own[h, rows, :], v_pair[h, pair_rows, :]], axis=0)
         s = nt_dot(kn, qn_ref[h]) * SCALE2
         g = nt_dot(v, do_ref[h])
         p = jnp.exp2(s - log_total)
@@ -266,9 +266,9 @@
     x1, x2, x3 = [fetch(kv, "x", NX, k) for k in range(1, NX)]
     q3 = swap(qd, "zq", NQ, 3)
     q2 = swap(after(qd, q3), "zq", NQ, 2)
-    x1, x3, x2, pair, qd_now = lax.optimization_barrier((x1, x3, x2, pair, qd))
+    q1 = swap(after(qd, pair), "zq", NQ, 1)
+    x1, x3, x2, pair = lax.optimization_barrier((x1, x3, x2, pair))
     p1, p2, p3 = [fetch(pair, "x", NX, k) for k in range(1, NX)]
-    q1 = swap(qd_now, "zq", NQ, 1)
     kvs = [kv, pair, x1, p1, x2, p2, x3, p3]
     qds = [qd, q1, q2, q3]
     tile = NH * QR * KR * HD * 2
@@ -279,12 +279,15 @@
         [*qds, kv, x1, x2, x3, q_gain, k_gain],
         flops=tile,
     )
-    stat, kn_pair, v_pair = kernel_call(
-        pair_stat_kernel,
-        [stat_shape, k_shape, k_shape],
-        [stat, qn, do, pair, p1, p2, p3, k_gain],
-        flops=tile,
-    )
+    pairs = []
+    for slots, blocks in (((0, 2), (pair, p2)), ((1, 3), (p1, p3))):
+        stat, *kn_and_v = kernel_call(
+            functools.partial(pair_stat_kernel, slots),
+            [stat_shape, ((NH, KC, HD), BF16), ((NH, KC, HD), BF16)],
+            [stat, qn, do, *blocks, k_gain],
+            flops=tile // 2,
+        )
+        pairs.append(kn_and_v)
     stats = [stat] + [swap(stat, "zq", NQ, k) for k in (1, 2, 3)]
     part = (NH, BR, HD)
     kv_part = (NZ, 2, NH, BR, HD)
@@ -294,7 +297,7 @@
         first, last = k == 2, k == 0
         outs = [(kv_part, F32 if last else BF16)]
         outs += [(part, F32)] + [(part, BF16)] * 3 if last else [whole_dq]
-        args = [*stats, *kvs[NZ * k : NZ * k + NZ], *(qds if last else ()), qn, do, kn_own, v_own, kn_pair, v_pair, *carried]
+        args = [*stats, *kvs[NZ * k : NZ * k + NZ], *(qds if last else ()), qn, do, kn_own, v_own, *pairs[k % 2], *carried]
         got = kernel_call(
             functools.partial(grad_kernel, k, first, last),
             outs + [gain_part],

time: 95.4 us -> 93.7 us (0.982)
  waiting for transfers between devices: 26.1 us -> 23.7 us
    ppermute x19, waiting for transfers between devices: 12.4 us -> 10.2 us  [swap(): return lax.ppermute(a, axis, [(i, i ^ k) for i in range(n)])]
    pallas_call x9 -> x10, Pallas kernels: 16.2 us -> 16.3 us  [kernel_call(): pl.pallas_call(kernel, out_shape=[jax.ShapeDtypeStruct(s, d) for s, d in...]
  transfers between devices with their start and end apart: 31 -> 31, of which waited for: 13 -> 14; matrix products, arithmetic and copies ran while one was open for 0% -> 0% of each run, Pallas kernels for 11% -> 13%
where the time goes in v5:
time: 93.7 us; the launch traced here: 93.6 us
  starting transfers between devices  51.2 us (55%)
  waiting for transfers between devices  23.7 us (25%)
  Pallas kernels  16.3 us (17%)
  other arithmetic  1.06 us (1%)
    ppermute x19, starting transfers between devices, swap(): return lax.ppermute(a, axis, [(i, i ^ k) for i in range(n)])  25.4 us
    pallas_call x10, Pallas kernels, kernel_call(): pl.pallas_call(kernel, out_shape=[jax.ShapeDtypeStruct(s, d) for s, d in...  16.3 us
    ppermute x6, starting transfers between devices, fetch(): return lax.ppermute(a, axis, [((i + k) % n, i) for i in range(n)])  11.6 us
    ppermute x19, waiting for transfers between devices, swap(): return lax.ppermute(a, axis, [(i, i ^ k) for i in range(n)])  10.2 us
    ppermute x3, starting transfers between devices, mirror(): return lax.ppermute(a, ('zk', 'zq'), [(i, n - 1 - i) for i in range(n)])  9.21 us
    ppermute x3, waiting for transfers between devices, mirror(): return lax.ppermute(a, ('zk', 'zq'), [(i, n - 1 - i) for i in range(n)])  7.46 us
    ppermute x6, waiting for transfers between devices, fetch(): return lax.ppermute(a, axis, [((i + k) % n, i) for i in range(n)])  6.11 us
    ppermute x3, starting transfers between devices, give(): return lax.ppermute(a, axis, [(i, (i + k) % n) for i in range(n)])  5.01 us
  transfers between devices with their start and end apart: 31, of which 14 were waited for; matrix products, arithmetic and copies ran while one was open for 0% of the time, Pallas kernels for 13%

profile of v5, /device:TPU:32, one launch (start us, length us, event | category | flops | bytes accessed | tf_op | source)
XLA Modules:
  0.0 93.6 jit_solution(2670911828403363764)
XLA Ops:
  1.7 2.0 %collective-permute-start.2 = (bf16[2,3,144,128]{3,2,1,0:T(8,128)(2,1)S(1)}, bf16[2,3,144,128]{3,2,1,0:T(8,128)(2,1)S(1)}, u32[]{:S(2)}, u32[]{:S(2)}) collective-permute-start(bf16[2,3,144,128]{3,2,1,0:T(8,128)(2,1)S(1)} %pad_maximum_fusion.q0.refs_6_.raw), channel_id=1, source_target_pairs={{0,96},{32,64},{64,32},{96,0},{1,97},{33,65},{65,33},{97,1},{2,98}... | collective-permute-start | bytes 663560 | tf_op jit(solution)/shard_map/ppermute | solution.py:237
  3.7 5.0 %collective-permute-start = (bf16[2,3,144,128]{3,2,1,0:T(8,128)(2,1)S(1)}, bf16[2,3,144,128]{3,2,1,0:T(8,128)(2,1)S(1)}, u32[]{:S(2)}, u32[]{:S(2)}) collective-permute-start(bf16[2,3,144,128]{3,2,1,0:T(8,128)(2,1)S(1)} %pad_maximum_fusion.1.kv0.refs_4_.raw), channel_id=1, source_target_pairs={{0,224},{32,192},{64,160},{96,128},{128,96},{160,64},{192,32},{224... | collective-permute-start | bytes 663560 | tf_op jit(solution)/shard_map/ppermute | solution.py:246
  8.7 3.0 %collective-permute-start.6 = (bf16[2,3,144,128]{3,2,1,0:T(8,128)(2,1)S(1)}, bf16[2,3,144,128]{3,2,1,0:T(8,128)(2,1)S(1)}, u32[]{:S(2)}, u32[]{:S(2)}) collective-permute-start(bf16[2,3,144,128]{3,2,1,0:T(8,128)(2,1)S(1)} %pad_maximum_fusion.1.kv0.refs_4_.raw), channel_id=1, source_target_pairs={{16,0},{24,8},{0,16},{8,24},{17,1},{25,9},{1,17},{9,25},{18,2},{26... | collective-permute-start | bytes 663560 | tf_op jit(solution)/shard_map/ppermute | solution.py:233
  12.4 2.6 %collective-permute-start.4 = (bf16[2,3,144,128]{3,2,1,0:T(8,128)(2,1)S(1)}, bf16[2,3,144,128]{3,2,1,0:T(8,128)(2,1)S(1)}, u32[]{:S(2)}, u32[]{:S(2)}) collective-permute-start(bf16[2,3,144,128]{3,2,1,0:T(8,128)(2,1)S(1)} %pad_maximum_fusion.1.kv0.refs_4_.raw), channel_id=1, source_target_pairs={{8,0},{16,8},{24,16},{0,24},{9,1},{17,9},{25,17},{1,25},{10,2},{18... | collective-permute-start | bytes 663560 | tf_op jit(solution)/shard_map/ppermute | solution.py:233
  15.0 1.5 %collective-permute-start.3 = (bf16[2,3,144,128]{3,2,1,0:T(8,128)(2,1)S(1)}, bf16[2,3,144,128]{3,2,1,0:T(8,128)(2,1)S(1)}, u32[]{:S(2)}, u32[]{:S(2)}) collective-permute-start(bf16[2,3,144,128]{3,2,1,0:T(8,128)(2,1)S(1)} %pad_maximum_fusion.q0.refs_6_.raw), channel_id=1, source_target_pairs={{0,64},{32,96},{64,0},{96,32},{1,65},{33,97},{65,1},{97,33},{2,66}... | collective-permute-start | bytes 663560 | tf_op jit(solution)/shard_map/ppermute | solution.py:237
  16.5 2.3 %collective-permute-done.kv_a.refs_5_ = bf16[2,3,144,128]{3,2,1,0:T(8,128)(2,1)S(1)} collective-permute-done((bf16[2,3,144,128]{3,2,1,0:T(8,128)(2,1)S(1)}, bf16[2,3,144,128]{3,2,1,0:T(8,128)(2,1)S(1)}, u32[]{:S(2)}, u32[]{:S(2)}) %collective-permute-start) | collective-permute-done | bytes 221216 | tf_op jit(solution)/shard_map/ppermute | solution.py:246
  18.9 2.7 %collective-permute-done.5.kv3.refs_4_ = bf16[2,3,144,128]{3,2,1,0:T(8,128)(2,1)S(1)} collective-permute-done((bf16[2,3,144,128]{3,2,1,0:T(8,128)(2,1)S(1)}, bf16[2,3,144,128]{3,2,1,0:T(8,128)(2,1)S(1)}, u32[]{:S(2)}, u32[]{:S(2)}) %collective-permute-start.5) | collective-permute-done | bytes 221216 | tf_op jit(solution)/shard_map/ppermute | solution.py:233
  21.7 2.1 %collective-permute-start.7 = (bf16[2,3,144,128]{3,2,1,0:T(8,128)(2,1)S(1)}, bf16[2,3,144,128]{3,2,1,0:T(8,128)(2,1)S(1)}, u32[]{:S(2)}, u32[]{:S(2)}) collective-permute-start(bf16[2,3,144,128]{3,2,1,0:T(8,128)(2,1)S(1)} %collective-permute-done.kv_a.refs_5_), channel_id=1, source_target_pairs={{16,0},{24,8},{0,16},{8,24},{17,1},{25,9},{1,17},{9,25},{18,2},{26... | collective-permute-start | bytes 663560 | tf_op jit(solution)/shard_map/ppermute | solution.py:233
  23.8 1.5 %collective-permute-start.9 = (bf16[2,3,144,128]{3,2,1,0:T(8,128)(2,1)S(1)}, bf16[2,3,144,128]{3,2,1,0:T(8,128)(2,1)S(1)}, u32[]{:S(2)}, u32[]{:S(2)}) collective-permute-start(bf16[2,3,144,128]{3,2,1,0:T(8,128)(2,1)S(1)} %collective-permute-done.kv_a.refs_5_), channel_id=1, source_target_pairs={{24,0},{0,8},{8,16},{16,24},{25,1},{1,9},{9,17},{17,25},{26,2},{2,... | collective-permute-start | bytes 663560 | tf_op jit(solution)/shard_map/ppermute | solution.py:233
  25.2 1.8 %collective-permute-start.8 = (bf16[2,3,144,128]{3,2,1,0:T(8,128)(2,1)S(1)}, bf16[2,3,144,128]{3,2,1,0:T(8,128)(2,1)S(1)}, u32[]{:S(2)}, u32[]{:S(2)}) collective-permute-start(bf16[2,3,144,128]{3,2,1,0:T(8,128)(2,1)S(1)} %collective-permute-done.kv_a.refs_5_), channel_id=1, source_target_pairs={{8,0},{16,8},{24,16},{0,24},{9,1},{17,9},{25,17},{1,25},{10,2},{18... | collective-permute-start | bytes 663560 | tf_op jit(solution)/shard_map/ppermute | solution.py:233
  27.2 2.7 %shard_map.101 = (f32[16,576]{1,0:T(8,128)S(1)}, bf16[3,576,128]{2,1,0:T(8,128)(2,1)S(1)}, bf16[3,576,128]{2,1,0:T(8,128)(2,1)S(1)}, bf16[3,576,128]{2,1,0:T(8,128)(2,1)S(1)}, bf16[3,576,128]{2,1,0:T(8,128)(2,1)S(1)}) custom-call(bf16[2,3,144,128]{3,2,1,0:T(8,128)(2,1)S(1)} %pad_maximum_fusion.q0.refs_6_.raw, ...), custom_call_target="tpu_custom_call" | custom-call | flops 509607936 | bytes 1771520 | tf_op jit(solution)/shard_map/pallas_call | solution.py:221
  29.9 1.6 %collective-permute-done.7.kv_b.refs_5_ = bf16[2,3,144,128]{3,2,1,0:T(8,128)(2,1)S(1)} collective-permute-done((bf16[2,3,144,128]{3,2,1,0:T(8,128)(2,1)S(1)}, bf16[2,3,144,128]{3,2,1,0:T(8,128)(2,1)S(1)}, u32[]{:S(2)}, u32[]{:S(2)}) %collective-permute-start.7) | collective-permute-done | bytes 221216 | tf_op jit(solution)/shard_map/ppermute | solution.py:233
  31.6 1.2 %shard_map.102 = (f32[16,576]{1,0:T(8,128)S(1)}, bf16[3,288,128]{2,1,0:T(8,128)(2,1)S(1)}, bf16[3,288,128]{2,1,0:T(8,128)(2,1)S(1)}) custom-call(f32[16,576]{1,0:T(8,128)S(1)} %get-tuple-element.59.before_ref, bf16[3,576,128]{2,1,0:T(8,128)(2,1)S(1)} %get-tuple-element.60.qn_ref.refs_6_.refs_10_, ...), custom_call_target="tpu_custom_call" | custom-call | flops 254803968 | bytes 1364992 | tf_op jit(solution)/shard_map/pallas_call | solution.py:221
  32.8 1.7 %collective-permute-done.9.kv_b.refs_5_ = bf16[2,3,144,128]{3,2,1,0:T(8,128)(2,1)S(1)} collective-permute-done((bf16[2,3,144,128]{3,2,1,0:T(8,128)(2,1)S(1)}, bf16[2,3,144,128]{3,2,1,0:T(8,128)(2,1)S(1)}, u32[]{:S(2)}, u32[]{:S(2)}) %collective-permute-start.9) | collective-permute-done | bytes 221216 | tf_op jit(solution)/shard_map/ppermute | solution.py:233
  36.8 2.4 %collective-permute-start.11 = (f32[16,576]{1,0:T(8,128)S(1)}, f32[16,576]{1,0:T(8,128)S(1)}, u32[]{:S(2)}, u32[]{:S(2)}) collective-permute-start(f32[16,576]{1,0:T(8,128)S(1)} %get-tuple-element.64.refs_0_), channel_id=1, source_target_pairs={{0,64},{32,96},{64,0},{96,32},{1,65},{33,97},{65,1},{97,33},{2,66}... | collective-permute-start | bytes 110600 | tf_op jit(solution)/shard_map/ppermute | solution.py:237
  39.3 2.0 %collective-permute-done.12.refs_3_ = f32[16,576]{1,0:T(8,128)S(1)} collective-permute-done((f32[16,576]{1,0:T(8,128)S(1)}, f32[16,576]{1,0:T(8,128)S(1)}, u32[]{:S(2)}, u32[]{:S(2)}) %collective-permute-start.12) | collective-permute-done | bytes 36896 | tf_op jit(solution)/shard_map/ppermute | solution.py:237
  42.0 1.2 %collective-permute-done.10.refs_1_ = f32[16,576]{1,0:T(8,128)S(1)} collective-permute-done((f32[16,576]{1,0:T(8,128)S(1)}, f32[16,576]{1,0:T(8,128)S(1)}, u32[]{:S(2)}, u32[]{:S(2)}) %collective-permute-start.10) | collective-permute-done | bytes 36896 | tf_op jit(solution)/shard_map/ppermute | solution.py:237
  43.2 2.1 %shard_map.104 = (bf16[2,2,3,144,128]{4,3,2,1,0:T(8,128)(2,1)S(1)}, f32[3,576,128]{2,1,0:T(8,128)S(1)}, f32[8,128]{1,0:T(8,128)S(1)}) custom-call(f32[16,576]{1,0:T(8,128)S(1)} %get-tuple-element.64.refs_0_, f32[16,576]{1,0:T(8,128)S(1)} %collective-permute-done.10.refs_1_, f32[16,576]{1,0:T(8,128)S(1)} %collective-permute-done.11.refs_2_, ...), custom_call_target="tpu_custom_call" | custom-call | flops 764411904 | bytes 2801664 | tf_op jit(solution)/shard_map/pallas_call | solution.py:221
  45.3 2.9 %collective-permute-start.16 = (bf16[2,2,3,144,128]{4,3,2,1,0:T(8,128)(2,1)S(1)}, bf16[2,2,3,144,128]{4,3,2,1,0:T(8,128)(2,1)S(1)}, u32[]{:S(2)}, u32[]{:S(2)}) collective-permute-start(bf16[2,2,3,144,128]{4,3,2,1,0:T(8,128)(2,1)S(1)} %get-tuple-element.82), channel_id=1, source_target_pairs={{0,16},{8,24},{16,0},{24,8},{1,17},{9,25},{17,1},{25,9},{2,18},{10... | collective-permute-start | bytes 1327112 | tf_op jit(solution)/shard_map/ppermute | solution.py:241
  48.2 2.1 %shard_map.105 = (bf16[2,2,3,144,128]{4,3,2,1,0:T(8,128)(2,1)S(1)}, f32[3,576,128]{2,1,0:T(8,128)S(1)}, f32[8,128]{1,0:T(8,128)S(1)}) custom-call(f32[16,576]{1,0:T(8,128)S(1)} %get-tuple-element.64.refs_0_, f32[16,576]{1,0:T(8,128)S(1)} %collective-permute-done.10.refs_1_, f32[16,576]{1,0:T(8,128)S(1)} %collective-permute-done.11.refs_2_, ...), custom_call_target="tpu_custom_call" | custom-call | flops 764411904 | bytes 3690496 | tf_op jit(solution)/shard_map/pallas_call | solution.py:221
  50.4 2.1 %shard_map.106 = (bf16[2,2,3,144,128]{4,3,2,1,0:T(8,128)(2,1)S(1)}, f32[3,576,128]{2,1,0:T(8,128)S(1)}, f32[8,128]{1,0:T(8,128)S(1)}) custom-call(f32[16,576]{1,0:T(8,128)S(1)} %get-tuple-element.64.refs_0_, f32[16,576]{1,0:T(8,128)S(1)} %collective-permute-done.10.refs_1_, f32[16,576]{1,0:T(8,128)S(1)} %collective-permute-done.11.refs_2_, ...), custom_call_target="tpu_custom_call" | custom-call | flops 764411904 | bytes 3690496 | tf_op jit(solution)/shard_map/pallas_call | solution.py:221
  52.5 2.1 %collective-permute-start.18 = (bf16[2,2,3,144,128]{4,3,2,1,0:T(8,128)(2,1)S(1)}, bf16[2,2,3,144,128]{4,3,2,1,0:T(8,128)(2,1)S(1)}, u32[]{:S(2)}, u32[]{:S(2)}) collective-permute-start(bf16[2,2,3,144,128]{4,3,2,1,0:T(8,128)(2,1)S(1)} %get-tuple-element.84), channel_id=1, source_target_pairs={{0,24},{8,0},{16,8},{24,16},{1,25},{9,1},{17,9},{25,17},{2,26},{10... | collective-permute-start | bytes 1327112 | tf_op jit(solution)/shard_map/ppermute | solution.py:241
  54.6 2.7 %shard_map.107 = (f32[2,2,3,144,128]{4,3,2,1,0:T(8,128)S(1)}, f32[3,144,128]{2,1,0:T(8,128)S(1)}, bf16[3,144,128]{2,1,0:T(8,128)(2,1)S(1)}, bf16[3,144,128]{2,1,...) custom-call(f32[16,576]{1,0:T(8,128)S(1)} %get-tuple-element.64.refs_0_, ...), custom_call_target="tpu_custom_call" | custom-call | flops 764411904 | bytes 4575232 | tf_op jit(solution)/shard_map/pallas_call | solution.py:221
  58.4 2.2 %collective-permute-start.21 = (f32[8,128]{1,0:T(8,128)S(1)}, f32[8,128]{1,0:T(8,128)S(1)}, u32[]{:S(2)}, u32[]{:S(2)}) collective-permute-start(f32[8,128]{1,0:T(8,128)S(1)} %get-tuple-element.90), channel_id=1, source_target_pairs={{0,64},{32,96},{64,0},{96,32},{1,65},{33,97},{65,1},{97,33},{2,66}... | collective-permute-start | bytes 12296 | tf_op jit(solution)/shard_map/ppermute | solution.py:237
  61.0 2.6 %collective-permute-start.20 = (f32[8,128]{1,0:T(8,128)S(1)}, f32[8,128]{1,0:T(8,128)S(1)}, u32[]{:S(2)}, u32[]{:S(2)}) collective-permute-start(f32[8,128]{1,0:T(8,128)S(1)} %get-tuple-element.90), channel_id=1, source_target_pairs={{0,32},{32,0},{64,96},{96,64},{1,33},{33,1},{65,97},{97,65},{2,34}... | collective-permute-start | bytes 12296 | tf_op jit(solution)/shard_map/ppermute | solution.py:237
  63.7 1.6 %collective-permute-done.20 = f32[8,128]{1,0:T(8,128)S(1)} collective-permute-done((f32[8,128]{1,0:T(8,128)S(1)}, f32[8,128]{1,0:T(8,128)S(1)}, u32[]{:S(2)}, u32[]{:S(2)}) %collective-permute-start.20) | collective-permute-done | bytes 4128 | tf_op jit(solution)/shard_map/ppermute | solution.py:237
  65.4 2.1 %collective-permute-start.13 = (bf16[3,144,128]{2,1,0:T(8,128)(2,1)S(1)}, bf16[3,144,128]{2,1,0:T(8,128)(2,1)S(1)}, u32[]{:S(2)}, u32[]{:S(2)}) collective-permute-start(bf16[3,144,128]{2,1,0:T(8,128)(2,1)S(1)} %get-tuple-element.78), channel_id=1, source_target_pairs={{0,32},{32,0},{64,96},{96,64},{1,33},{33,1},{65,97},{97,65},{2,34}... | collective-permute-start | bytes 331784 | tf_op jit(solution)/shard_map/ppermute | solution.py:237
  69.3 5.2 %collective-permute-done.24 = f32[8,128]{1,0:T(8,128)S(1)} collective-permute-done((f32[8,128]{1,0:T(8,128)S(1)}, f32[8,128]{1,0:T(8,128)S(1)}, u32[]{:S(2)}, u32[]{:S(2)}) %collective-permute-start.24) | collective-permute-done | bytes 4128 | tf_op jit(solution)/shard_map/ppermute | solution.py:246
  75.5 3.0 %collective-permute-start.27 = (f32[8,128]{1,0:T(8,128)S(1)}, f32[8,128]{1,0:T(8,128)S(1)}, u32[]{:S(2)}, u32[]{:S(2)}) collective-permute-start(f32[8,128]{1,0:T(8,128)S(1)} %add.37), channel_id=1, source_target_pairs={{0,6},{2,4},{4,2},{6,0},{1,7},{3,5},{5,3},{7,1},{8,14},{10,12},{12... | collective-permute-start | bytes 12296 | tf_op jit(solution)/shard_map/ppermute | solution.py:237
  79.8 3.0 %collective-permute-start.19 = (bf16[2,3,144,128]{3,2,1,0:T(8,128)(2,1)S(1)}, bf16[2,3,144,128]{3,2,1,0:T(8,128)(2,1)S(1)}, u32[]{:S(2)}, u32[]{:S(2)}) collective-permute-start(bf16[2,3,144,128]{3,2,1,0:T(8,128)(2,1)S(1)} %get-tuple-element.86), channel_id=1, source_target_pairs={{0,224},{32,192},{64,160},{96,128},{128,96},{160,64},{192,32},{224... | collective-permute-start | bytes 663560 | tf_op jit(solution)/shard_map/ppermute | solution.py:246
  83.7 3.3 %collective-permute-start.30 = (f32[8,128]{1,0:T(8,128)S(1)}, f32[8,128]{1,0:T(8,128)S(1)}, u32[]{:S(2)}, u32[]{:S(2)}) collective-permute-start(f32[8,128]{1,0:T(8,128)S(1)} %add_add_fusion.1), channel_id=1, source_target_pairs={{0,24},{8,16},{16,8},{24,0},{1,25},{9,17},{17,9},{25,1},{2,26},{10... | collective-permute-start | bytes 12296 | tf_op jit(solution)/shard_map/ppermute | solution.py:237
  88.9 3.2 %collective-permute-done.29 = f32[8,128]{1,0:T(8,128)S(1)} collective-permute-done((f32[8,128]{1,0:T(8,128)S(1)}, f32[8,128]{1,0:T(8,128)S(1)}, u32[]{:S(2)}, u32[]{:S(2)}) %collective-permute-start.29) | collective-permute-done | bytes 4128 | tf_op jit(solution)/shard_map/ppermute | solution.py:237
  (56 shorter events, 15.2 us)
Async XLA Ops:
  1.7 13.3 %collective-permute-start.2 = (bf16[2,3,144,128]{3,2,1,0:T(8,128)(2,1)S(1)}, bf16[2,3,144,128]{3,2,1,0:T(8,128)(2,1)S(1)}, u32[]{:S(2)}, u32[]{:S(2)}) collective-permute-start(bf16[2,3,144,128]{3,2,1,0:T(8,128)(2,1)S(1)} %pad_maximum_fusion.q0.refs_6_.raw), channel_id=1, source_target_pairs={{0,96},{32,64},{64,32},{96,0},{1,97},{33,65},{65,33},{97,1},{2,98}... | collective-permute-start | bytes 663560 | tf_op jit(solution)/shard_map/ppermute | solution.py:237
  3.7 23.6 %copy-start.1 = (f32[2,128]{1,0:T(2,128)S(1)}, f32[2,128]{1,0:T(2,128)}, u32[]{:S(2)}) copy-start(f32[2,128]{1,0:T(2,128)} %gain_ref.2) | copy-start | bytes 3076
  3.7 15.1 %collective-permute-start = (bf16[2,3,144,128]{3,2,1,0:T(8,128)(2,1)S(1)}, bf16[2,3,144,128]{3,2,1,0:T(8,128)(2,1)S(1)}, u32[]{:S(2)}, u32[]{:S(2)}) collective-permute-start(bf16[2,3,144,128]{3,2,1,0:T(8,128)(2,1)S(1)} %pad_maximum_fusion.1.kv0.refs_4_.raw), channel_id=1, source_target_pairs={{0,224},{32,192},{64,160},{96,128},{128,96},{160,64},{192,32},{224... | collective-permute-start | bytes 663560 | tf_op jit(solution)/shard_map/ppermute | solution.py:246
  8.7 10.2 %collective-permute-start.6 = (bf16[2,3,144,128]{3,2,1,0:T(8,128)(2,1)S(1)}, bf16[2,3,144,128]{3,2,1,0:T(8,128)(2,1)S(1)}, u32[]{:S(2)}, u32[]{:S(2)}) collective-permute-start(bf16[2,3,144,128]{3,2,1,0:T(8,128)(2,1)S(1)} %pad_maximum_fusion.1.kv0.refs_4_.raw), channel_id=1, source_target_pairs={{16,0},{24,8},{0,16},{8,24},{17,1},{25,9},{1,17},{9,25},{18,2},{26... | collective-permute-start | bytes 663560 | tf_op jit(solution)/shard_map/ppermute | solution.py:233
  11.8 9.8 %collective-permute-start.5 = (bf16[2,3,144,128]{3,2,1,0:T(8,128)(2,1)S(1)}, bf16[2,3,144,128]{3,2,1,0:T(8,128)(2,1)S(1)}, u32[]{:S(2)}, u32[]{:S(2)}) collective-permute-start(bf16[2,3,144,128]{3,2,1,0:T(8,128)(2,1)S(1)} %pad_maximum_fusion.1.kv0.refs_4_.raw), channel_id=1, source_target_pairs={{24,0},{0,8},{8,16},{16,24},{25,1},{1,9},{9,17},{17,25},{26,2},{2,... | collective-permute-start | bytes 663560 | tf_op jit(solution)/shard_map/ppermute | solution.py:233
  12.4 9.3 %collective-permute-start.4 = (bf16[2,3,144,128]{3,2,1,0:T(8,128)(2,1)S(1)}, bf16[2,3,144,128]{3,2,1,0:T(8,128)(2,1)S(1)}, u32[]{:S(2)}, u32[]{:S(2)}) collective-permute-start(bf16[2,3,144,128]{3,2,1,0:T(8,128)(2,1)S(1)} %pad_maximum_fusion.1.kv0.refs_4_.raw), channel_id=1, source_target_pairs={{8,0},{16,8},{24,16},{0,24},{9,1},{17,9},{25,17},{1,25},{10,2},{18... | collective-permute-start | bytes 663560 | tf_op jit(solution)/shard_map/ppermute | solution.py:233
  15.0 12.0 %collective-permute-start.3 = (bf16[2,3,144,128]{3,2,1,0:T(8,128)(2,1)S(1)}, bf16[2,3,144,128]{3,2,1,0:T(8,128)(2,1)S(1)}, u32[]{:S(2)}, u32[]{:S(2)}) collective-permute-start(bf16[2,3,144,128]{3,2,1,0:T(8,128)(2,1)S(1)} %pad_maximum_fusion.q0.refs_6_.raw), channel_id=1, source_target_pairs={{0,64},{32,96},{64,0},{96,32},{1,65},{33,97},{65,1},{97,33},{2,66}... | collective-permute-start | bytes 663560 | tf_op jit(solution)/shard_map/ppermute | solution.py:237
  18.8 8.5 %collective-permute-start.1 = (bf16[2,3,144,128]{3,2,1,0:T(8,128)(2,1)S(1)}, bf16[2,3,144,128]{3,2,1,0:T(8,128)(2,1)S(1)}, u32[]{:S(2)}, u32[]{:S(2)}) collective-permute-start(bf16[2,3,144,128]{3,2,1,0:T(8,128)(2,1)S(1)} %pad_maximum_fusion.q0.refs_6_.raw), channel_id=1, source_target_pairs={{0,32},{32,0},{64,96},{96,64},{1,33},{33,1},{65,97},{97,65},{2,34}... | collective-permute-start | bytes 663560 | tf_op jit(solution)/shard_map/ppermute | solution.py:237
  21.7 9.9 %collective-permute-start.7 = (bf16[2,3,144,128]{3,2,1,0:T(8,128)(2,1)S(1)}, bf16[2,3,144,128]{3,2,1,0:T(8,128)(2,1)S(1)}, u32[]{:S(2)}, u32[]{:S(2)}) collective-permute-start(bf16[2,3,144,128]{3,2,1,0:T(8,128)(2,1)S(1)} %collective-permute-done.kv_a.refs_5_), channel_id=1, source_target_pairs={{16,0},{24,8},{0,16},{8,24},{17,1},{25,9},{1,17},{9,25},{18,2},{26... | collective-permute-start | bytes 663560 | tf_op jit(solution)/shard_map/ppermute | solution.py:233
  23.8 10.7 %collective-permute-start.9 = (bf16[2,3,144,128]{3,2,1,0:T(8,128)(2,1)S(1)}, bf16[2,3,144,128]{3,2,1,0:T(8,128)(2,1)S(1)}, u32[]{:S(2)}, u32[]{:S(2)}) collective-permute-start(bf16[2,3,144,128]{3,2,1,0:T(8,128)(2,1)S(1)} %collective-permute-done.kv_a.refs_5_), channel_id=1, source_target_pairs={{24,0},{0,8},{8,16},{16,24},{25,1},{1,9},{9,17},{17,25},{26,2},{2,... | collective-permute-start | bytes 663560 | tf_op jit(solution)/shard_map/ppermute | solution.py:233
  25.2 9.3 %collective-permute-start.8 = (bf16[2,3,144,128]{3,2,1,0:T(8,128)(2,1)S(1)}, bf16[2,3,144,128]{3,2,1,0:T(8,128)(2,1)S(1)}, u32[]{:S(2)}, u32[]{:S(2)}) collective-permute-start(bf16[2,3,144,128]{3,2,1,0:T(8,128)(2,1)S(1)} %collective-permute-done.kv_a.refs_5_), channel_id=1, source_target_pairs={{8,0},{16,8},{24,16},{0,24},{9,1},{17,9},{25,17},{1,25},{10,2},{18... | collective-permute-start | bytes 663560 | tf_op jit(solution)/shard_map/ppermute | solution.py:233
  35.7 5.5 %collective-permute-start.12 = (f32[16,576]{1,0:T(8,128)S(1)}, f32[16,576]{1,0:T(8,128)S(1)}, u32[]{:S(2)}, u32[]{:S(2)}) collective-permute-start(f32[16,576]{1,0:T(8,128)S(1)} %get-tuple-element.64.refs_0_), channel_id=1, source_target_pairs={{0,96},{32,64},{64,32},{96,0},{1,97},{33,65},{65,33},{97,1},{2,98}... | collective-permute-start | bytes 110600 | tf_op jit(solution)/shard_map/ppermute | solution.py:237
  36.8 5.1 %collective-permute-start.11 = (f32[16,576]{1,0:T(8,128)S(1)}, f32[16,576]{1,0:T(8,128)S(1)}, u32[]{:S(2)}, u32[]{:S(2)}) collective-permute-start(f32[16,576]{1,0:T(8,128)S(1)} %get-tuple-element.64.refs_0_), channel_id=1, source_target_pairs={{0,64},{32,96},{64,0},{96,32},{1,65},{33,97},{65,1},{97,33},{2,66}... | collective-permute-start | bytes 110600 | tf_op jit(solution)/shard_map/ppermute | solution.py:237
  39.2 4.0 %collective-permute-start.10 = (f32[16,576]{1,0:T(8,128)S(1)}, f32[16,576]{1,0:T(8,128)S(1)}, u32[]{:S(2)}, u32[]{:S(2)}) collective-permute-start(f32[16,576]{1,0:T(8,128)S(1)} %get-tuple-element.64.refs_0_), channel_id=1, source_target_pairs={{0,32},{32,0},{64,96},{96,64},{1,33},{33,1},{65,97},{97,65},{2,34}... | collective-permute-start | bytes 110600 | tf_op jit(solution)/shard_map/ppermute | solution.py:237
  45.3 19.9 %collective-permute-start.16 = (bf16[2,2,3,144,128]{4,3,2,1,0:T(8,128)(2,1)S(1)}, bf16[2,2,3,144,128]{4,3,2,1,0:T(8,128)(2,1)S(1)}, u32[]{:S(2)}, u32[]{:S(2)}) collective-permute-start(bf16[2,2,3,144,128]{4,3,2,1,0:T(8,128)(2,1)S(1)} %get-tuple-element.82), channel_id=1, source_target_pairs={{0,16},{8,24},{16,0},{24,8},{1,17},{9,25},{17,1},{25,9},{2,18},{10... | collective-permute-start | bytes 1327112 | tf_op jit(solution)/shard_map/ppermute | solution.py:241
  52.5 26.0 %collective-permute-start.18 = (bf16[2,2,3,144,128]{4,3,2,1,0:T(8,128)(2,1)S(1)}, bf16[2,2,3,144,128]{4,3,2,1,0:T(8,128)(2,1)S(1)}, u32[]{:S(2)}, u32[]{:S(2)}) collective-permute-start(bf16[2,2,3,144,128]{4,3,2,1,0:T(8,128)(2,1)S(1)} %get-tuple-element.84), channel_id=1, source_target_pairs={{0,24},{8,0},{16,8},{24,16},{1,25},{9,1},{17,9},{25,17},{2,26},{10... | collective-permute-start | bytes 1327112 | tf_op jit(solution)/shard_map/ppermute | solution.py:241
  54.6 24.5 %collective-permute-start.17 = (bf16[2,2,3,144,128]{4,3,2,1,0:T(8,128)(2,1)S(1)}, bf16[2,2,3,144,128]{4,3,2,1,0:T(8,128)(2,1)S(1)}, u32[]{:S(2)}, u32[]{:S(2)}) collective-permute-start(bf16[2,2,3,144,128]{4,3,2,1,0:T(8,128)(2,1)S(1)} %get-tuple-element.83), channel_id=1, source_target_pairs={{0,8},{8,16},{16,24},{24,0},{1,9},{9,17},{17,25},{25,1},{2,10},{10... | collective-permute-start | bytes 1327112 | tf_op jit(solution)/shard_map/ppermute | solution.py:241
  57.3 3.7 %collective-permute-start.22 = (f32[8,128]{1,0:T(8,128)S(1)}, f32[8,128]{1,0:T(8,128)S(1)}, u32[]{:S(2)}, u32[]{:S(2)}) collective-permute-start(f32[8,128]{1,0:T(8,128)S(1)} %get-tuple-element.90), channel_id=1, source_target_pairs={{0,96},{32,64},{64,32},{96,0},{1,97},{33,65},{65,33},{97,1},{2,98}... | collective-permute-start | bytes 12296 | tf_op jit(solution)/shard_map/ppermute | solution.py:237
  58.4 5.2 %collective-permute-start.21 = (f32[8,128]{1,0:T(8,128)S(1)}, f32[8,128]{1,0:T(8,128)S(1)}, u32[]{:S(2)}, u32[]{:S(2)}) collective-permute-start(f32[8,128]{1,0:T(8,128)S(1)} %get-tuple-element.90), channel_id=1, source_target_pairs={{0,64},{32,96},{64,0},{96,32},{1,65},{33,97},{65,1},{97,33},{2,66}... | collective-permute-start | bytes 12296 | tf_op jit(solution)/shard_map/ppermute | solution.py:237
  61.0 4.2 %collective-permute-start.20 = (f32[8,128]{1,0:T(8,128)S(1)}, f32[8,128]{1,0:T(8,128)S(1)}, u32[]{:S(2)}, u32[]{:S(2)}) collective-permute-start(f32[8,128]{1,0:T(8,128)S(1)} %get-tuple-element.90), channel_id=1, source_target_pairs={{0,32},{32,0},{64,96},{96,64},{1,33},{33,1},{65,97},{97,65},{2,34}... | collective-permute-start | bytes 12296 | tf_op jit(solution)/shard_map/ppermute | solution.py:237
  65.3 2.2 %collective-permute-start.23 = (f32[8,128]{1,0:T(8,128)S(1)}, f32[8,128]{1,0:T(8,128)S(1)}, u32[]{:S(2)}, u32[]{:S(2)}) collective-permute-start(f32[8,128]{1,0:T(8,128)S(1)} %add_add_fusion.2), channel_id=1, source_target_pairs={{0,1},{1,0},{2,3},{3,2},{4,5},{5,4},{6,7},{7,6},{8,9},{9,8},{10,11... | collective-permute-start | bytes 12296 | tf_op jit(solution)/shard_map/ppermute | solution.py:237
  65.4 10.2 %collective-permute-start.13 = (bf16[3,144,128]{2,1,0:T(8,128)(2,1)S(1)}, bf16[3,144,128]{2,1,0:T(8,128)(2,1)S(1)}, u32[]{:S(2)}, u32[]{:S(2)}) collective-permute-start(bf16[3,144,128]{2,1,0:T(8,128)(2,1)S(1)} %get-tuple-element.78), channel_id=1, source_target_pairs={{0,32},{32,0},{64,96},{96,64},{1,33},{33,1},{65,97},{97,65},{2,34}... | collective-permute-start | bytes 331784 | tf_op jit(solution)/shard_map/ppermute | solution.py:237
  67.5 7.0 %collective-permute-start.24 = (f32[8,128]{1,0:T(8,128)S(1)}, f32[8,128]{1,0:T(8,128)S(1)}, u32[]{:S(2)}, u32[]{:S(2)}) collective-permute-start(f32[8,128]{1,0:T(8,128)S(1)} %add.36), channel_id=1, source_target_pairs={{0,224},{32,192},{64,160},{96,128},{128,96},{160,64},{192,32},{224... | collective-permute-start | bytes 12296 | tf_op jit(solution)/shard_map/ppermute | solution.py:246
  68.7 11.1 %collective-permute-start.14 = (bf16[3,144,128]{2,1,0:T(8,128)(2,1)S(1)}, bf16[3,144,128]{2,1,0:T(8,128)(2,1)S(1)}, u32[]{:S(2)}, u32[]{:S(2)}) collective-permute-start(bf16[3,144,128]{2,1,0:T(8,128)(2,1)S(1)} %get-tuple-element.79), channel_id=1, source_target_pairs={{0,64},{32,96},{64,0},{96,32},{1,65},{33,97},{65,1},{97,33},{2,66}... | collective-permute-start | bytes 331784 | tf_op jit(solution)/shard_map/ppermute | solution.py:237
  74.5 8.3 %collective-permute-start.15 = (bf16[3,144,128]{2,1,0:T(8,128)(2,1)S(1)}, bf16[3,144,128]{2,1,0:T(8,128)(2,1)S(1)}, u32[]{:S(2)}, u32[]{:S(2)}) collective-permute-start(bf16[3,144,128]{2,1,0:T(8,128)(2,1)S(1)} %get-tuple-element.80), channel_id=1, source_target_pairs={{0,96},{32,64},{64,32},{96,0},{1,97},{33,65},{65,33},{97,1},{2,98}... | collective-permute-start | bytes 331784 | tf_op jit(solution)/shard_map/ppermute | solution.py:237
  75.5 7.3 %collective-permute-start.27 = (f32[8,128]{1,0:T(8,128)S(1)}, f32[8,128]{1,0:T(8,128)S(1)}, u32[]{:S(2)}, u32[]{:S(2)}) collective-permute-start(f32[8,128]{1,0:T(8,128)S(1)} %add.37), channel_id=1, source_target_pairs={{0,6},{2,4},{4,2},{6,0},{1,7},{3,5},{5,3},{7,1},{8,14},{10,12},{12... | collective-permute-start | bytes 12296 | tf_op jit(solution)/shard_map/ppermute | solution.py:237
  78.5 5.1 %collective-permute-start.26 = (f32[8,128]{1,0:T(8,128)S(1)}, f32[8,128]{1,0:T(8,128)S(1)}, u32[]{:S(2)}, u32[]{:S(2)}) collective-permute-start(f32[8,128]{1,0:T(8,128)S(1)} %add.37), channel_id=1, source_target_pairs={{0,4},{2,6},{4,0},{6,2},{1,5},{3,7},{5,1},{7,3},{8,12},{10,14},{12... | collective-permute-start | bytes 12296 | tf_op jit(solution)/shard_map/ppermute | solution.py:237
  79.2 4.5 %collective-permute-start.25 = (f32[8,128]{1,0:T(8,128)S(1)}, f32[8,128]{1,0:T(8,128)S(1)}, u32[]{:S(2)}, u32[]{:S(2)}) collective-permute-start(f32[8,128]{1,0:T(8,128)S(1)} %add.37), channel_id=1, source_target_pairs={{0,2},{2,0},{4,6},{6,4},{1,3},{3,1},{5,7},{7,5},{8,10},{10,8},{12,... | collective-permute-start | bytes 12296 | tf_op jit(solution)/shard_map/ppermute | solution.py:237
  79.8 12.3 %collective-permute-start.19 = (bf16[2,3,144,128]{3,2,1,0:T(8,128)(2,1)S(1)}, bf16[2,3,144,128]{3,2,1,0:T(8,128)(2,1)S(1)}, u32[]{:S(2)}, u32[]{:S(2)}) collective-permute-start(bf16[2,3,144,128]{3,2,1,0:T(8,128)(2,1)S(1)} %get-tuple-element.86), channel_id=1, source_target_pairs={{0,224},{32,192},{64,160},{96,128},{128,96},{160,64},{192,32},{224... | collective-permute-start | bytes 663560 | tf_op jit(solution)/shard_map/ppermute | solution.py:246
  83.7 5.2 %collective-permute-start.30 = (f32[8,128]{1,0:T(8,128)S(1)}, f32[8,128]{1,0:T(8,128)S(1)}, u32[]{:S(2)}, u32[]{:S(2)}) collective-permute-start(f32[8,128]{1,0:T(8,128)S(1)} %add_add_fusion.1), channel_id=1, source_target_pairs={{0,24},{8,16},{16,8},{24,0},{1,25},{9,17},{17,9},{25,1},{2,26},{10... | collective-permute-start | bytes 12296 | tf_op jit(solution)/shard_map/ppermute | solution.py:237
  87.0 5.1 %collective-permute-start.29 = (f32[8,128]{1,0:T(8,128)S(1)}, f32[8,128]{1,0:T(8,128)S(1)}, u32[]{:S(2)}, u32[]{:S(2)}) collective-permute-start(f32[8,128]{1,0:T(8,128)S(1)} %add_add_fusion.1), channel_id=1, source_target_pairs={{0,16},{8,24},{16,0},{24,8},{1,17},{9,25},{17,1},{25,9},{2,18},{10... | collective-permute-start | bytes 12296 | tf_op jit(solution)/shard_map/ppermute | solution.py:237
  87.0 5.1 %collective-permute-start.28 = (f32[8,128]{1,0:T(8,128)S(1)}, f32[8,128]{1,0:T(8,128)S(1)}, u32[]{:S(2)}, u32[]{:S(2)}) collective-permute-start(f32[8,128]{1,0:T(8,128)S(1)} %add_add_fusion.1), channel_id=1, source_target_pairs={{0,8},{8,0},{16,24},{24,16},{1,9},{9,1},{17,25},{25,17},{2,10},{10... | collective-permute-start | bytes 12296 | tf_op jit(solution)/shard_map/ppermute | solution.py:237
  (3 other events, 29.6 us)

commit v6 on v5

--- a/solution.py
+++ b/solution.py
@@ -310,7 +310,9 @@
         else:
             kv_got.append(give(got[0], "x", NX, k))
             carried = got[1:]
-    gains = summed(gains, "zq", NQ, kv_got[0])
+    gains = gains + swap(gains, "zq", NQ, 1)
+    gains, other, *_ = lax.optimization_barrier((gains, swap(gains, "zq", NQ, 2), kv_got[0]))
+    gains = gains + other
     messages = [swap(m, "zq", NQ, k) for k, m in enumerate(messages, 1)]
     gains = gains + swap(gains, "core", 2, 1)
     gains = gains + mirror(gains)
@@ -320,13 +322,18 @@
     got = mirror(send)
     gains = summed(gains, "y", 4, *messages)
     (q_out,) = kernel_call(q_out_kernel, [(part, BF16)], [dq_own, *messages, qd, q_gain])
-    gains = summed(after(gains, send), "x", NX, got)
-    k_out, v_out = kernel_call(
-        kv_out_kernel, [(part, BF16)] * 2, [keep, got, kv, k_gain]
-    )
+    k_out, v_out = kernel_call(kv_out_kernel, [(part, BF16)] * 2, [keep, got, kv, k_gain])
+    gains = after(gains, send)
+    terms = [gains] + [swap(gains, "x", NX, k) for k in range(1, NX)]
+    terms = lax.optimization_barrier((*terms, k_out))[:NX]
+
+    def gain_grad(rows):
+        a, b, c, d = [t[rows] for t in terms]
+        return (a + b) + (c + d)
+
 
     return (
-        heads_first(q_out), heads_first(k_out), heads_first(v_out), gains[0:2], gains[2:4],
+        heads_first(q_out), heads_first(k_out), heads_first(v_out), gain_grad(slice(0, 2)), gain_grad(slice(2, 4)),
     )
 
 

time: 93.7 us -> 92.2 us (0.984)
  starting transfers between devices: 51.2 us -> 46.1 us
  waiting for transfers between devices: 23.7 us -> 27.1 us
    ppermute x19 -> x18, starting transfers between devices: 25.4 us -> 20.3 us  [swap(): return lax.ppermute(a, axis, [(i, i ^ k) for i in range(n)])]
    ppermute x19 -> x18, waiting for transfers between devices: 10.2 us -> 13.4 us  [swap(): return lax.ppermute(a, axis, [(i, i ^ k) for i in range(n)])]
  transfers between devices with their start and end apart: 31 -> 30, of which waited for: 14 -> 15; matrix products, arithmetic and copies ran while one was open for 0% -> 0% of each run, Pallas kernels for 13% -> 14%
where the time goes in v6:
time: 92.2 us; the launch traced here: 91.9 us
  starting transfers between devices  46.1 us (50%)
  waiting for transfers between devices  27.1 us (29%)
  Pallas kernels  16.3 us (18%)
  other arithmetic  1.63 us (2%)
    ppermute x18, starting transfers between devices, swap(): return lax.ppermute(a, axis, [(i, i ^ k) for i in range(n)])  20.3 us
    pallas_call x10, Pallas kernels, kernel_call(): pl.pallas_call(kernel, out_shape=[jax.ShapeDtypeStruct(s, d) for s, d in...  16.3 us
    ppermute x18, waiting for transfers between devices, swap(): return lax.ppermute(a, axis, [(i, i ^ k) for i in range(n)])  13.4 us
    ppermute x6, starting transfers between devices, fetch(): return lax.ppermute(a, axis, [((i + k) % n, i) for i in range(n)])  11.6 us
    ppermute x3, starting transfers between devices, mirror(): return lax.ppermute(a, ('zk', 'zq'), [(i, n - 1 - i) for i in range(n)])  9.29 us
    ppermute x3, waiting for transfers between devices, mirror(): return lax.ppermute(a, ('zk', 'zq'), [(i, n - 1 - i) for i in range(n)])  7.55 us
    ppermute x6, waiting for transfers between devices, fetch(): return lax.ppermute(a, axis, [((i + k) % n, i) for i in range(n)])  6.11 us
    ppermute x3, starting transfers between devices, give(): return lax.ppermute(a, axis, [(i, (i + k) % n) for i in range(n)])  5.02 us
  transfers between devices with their start and end apart: 30, of which 15 were waited for; matrix products, arithmetic and copies ran while one was open for 0% of the time, Pallas kernels for 14%

profile of v6, /device:TPU:32, one launch (start us, length us, event | category | flops | bytes accessed | tf_op | source)
XLA Modules:
  0.0 91.9 jit_solution(2986878842837646105)
XLA Ops:
  1.7 2.0 %collective-permute-start.2 = (bf16[2,3,144,128]{3,2,1,0:T(8,128)(2,1)S(1)}, bf16[2,3,144,128]{3,2,1,0:T(8,128)(2,1)S(1)}, u32[]{:S(2)}, u32[]{:S(2)}) collective-permute-start(bf16[2,3,144,128]{3,2,1,0:T(8,128)(2,1)S(1)} %pad_maximum_fusion.q0.refs_6_.raw), channel_id=1, source_target_pairs={{0,96},{32,64},{64,32},{96,0},{1,97},{33,65},{65,33},{97,1},{2,98}... | collective-permute-start | bytes 663560 | tf_op jit(solution)/shard_map/ppermute | solution.py:237
  3.7 5.0 %collective-permute-start = (bf16[2,3,144,128]{3,2,1,0:T(8,128)(2,1)S(1)}, bf16[2,3,144,128]{3,2,1,0:T(8,128)(2,1)S(1)}, u32[]{:S(2)}, u32[]{:S(2)}) collective-permute-start(bf16[2,3,144,128]{3,2,1,0:T(8,128)(2,1)S(1)} %pad_maximum_fusion.1.kv0.refs_4_.raw), channel_id=1, source_target_pairs={{0,224},{32,192},{64,160},{96,128},{128,96},{160,64},{192,32},{224... | collective-permute-start | bytes 663560 | tf_op jit(solution)/shard_map/ppermute | solution.py:246
  8.7 3.0 %collective-permute-start.6 = (bf16[2,3,144,128]{3,2,1,0:T(8,128)(2,1)S(1)}, bf16[2,3,144,128]{3,2,1,0:T(8,128)(2,1)S(1)}, u32[]{:S(2)}, u32[]{:S(2)}) collective-permute-start(bf16[2,3,144,128]{3,2,1,0:T(8,128)(2,1)S(1)} %pad_maximum_fusion.1.kv0.refs_4_.raw), channel_id=1, source_target_pairs={{16,0},{24,8},{0,16},{8,24},{17,1},{25,9},{1,17},{9,25},{18,2},{26... | collective-permute-start | bytes 663560 | tf_op jit(solution)/shard_map/ppermute | solution.py:233
  12.4 2.6 %collective-permute-start.4 = (bf16[2,3,144,128]{3,2,1,0:T(8,128)(2,1)S(1)}, bf16[2,3,144,128]{3,2,1,0:T(8,128)(2,1)S(1)}, u32[]{:S(2)}, u32[]{:S(2)}) collective-permute-start(bf16[2,3,144,128]{3,2,1,0:T(8,128)(2,1)S(1)} %pad_maximum_fusion.1.kv0.refs_4_.raw), channel_id=1, source_target_pairs={{8,0},{16,8},{24,16},{0,24},{9,1},{17,9},{25,17},{1,25},{10,2},{18... | collective-permute-start | bytes 663560 | tf_op jit(solution)/shard_map/ppermute | solution.py:233
  15.0 1.5 %collective-permute-start.3 = (bf16[2,3,144,128]{3,2,1,0:T(8,128)(2,1)S(1)}, bf16[2,3,144,128]{3,2,1,0:T(8,128)(2,1)S(1)}, u32[]{:S(2)}, u32[]{:S(2)}) collective-permute-start(bf16[2,3,144,128]{3,2,1,0:T(8,128)(2,1)S(1)} %pad_maximum_fusion.q0.refs_6_.raw), channel_id=1, source_target_pairs={{0,64},{32,96},{64,0},{96,32},{1,65},{33,97},{65,1},{97,33},{2,66}... | collective-permute-start | bytes 663560 | tf_op jit(solution)/shard_map/ppermute | solution.py:237
  16.5 2.3 %collective-permute-done.kv_a.refs_5_ = bf16[2,3,144,128]{3,2,1,0:T(8,128)(2,1)S(1)} collective-permute-done((bf16[2,3,144,128]{3,2,1,0:T(8,128)(2,1)S(1)}, bf16[2,3,144,128]{3,2,1,0:T(8,128)(2,1)S(1)}, u32[]{:S(2)}, u32[]{:S(2)}) %collective-permute-start) | collective-permute-done | bytes 221216 | tf_op jit(solution)/shard_map/ppermute | solution.py:246
  18.9 2.7 %collective-permute-done.5.kv3.refs_4_ = bf16[2,3,144,128]{3,2,1,0:T(8,128)(2,1)S(1)} collective-permute-done((bf16[2,3,144,128]{3,2,1,0:T(8,128)(2,1)S(1)}, bf16[2,3,144,128]{3,2,1,0:T(8,128)(2,1)S(1)}, u32[]{:S(2)}, u32[]{:S(2)}) %collective-permute-start.5) | collective-permute-done | bytes 221216 | tf_op jit(solution)/shard_map/ppermute | solution.py:233
  21.7 2.1 %collective-permute-start.7 = (bf16[2,3,144,128]{3,2,1,0:T(8,128)(2,1)S(1)}, bf16[2,3,144,128]{3,2,1,0:T(8,128)(2,1)S(1)}, u32[]{:S(2)}, u32[]{:S(2)}) collective-permute-start(bf16[2,3,144,128]{3,2,1,0:T(8,128)(2,1)S(1)} %collective-permute-done.kv_a.refs_5_), channel_id=1, source_target_pairs={{16,0},{24,8},{0,16},{8,24},{17,1},{25,9},{1,17},{9,25},{18,2},{26... | collective-permute-start | bytes 663560 | tf_op jit(solution)/shard_map/ppermute | solution.py:233
  23.8 1.5 %collective-permute-start.9 = (bf16[2,3,144,128]{3,2,1,0:T(8,128)(2,1)S(1)}, bf16[2,3,144,128]{3,2,1,0:T(8,128)(2,1)S(1)}, u32[]{:S(2)}, u32[]{:S(2)}) collective-permute-start(bf16[2,3,144,128]{3,2,1,0:T(8,128)(2,1)S(1)} %collective-permute-done.kv_a.refs_5_), channel_id=1, source_target_pairs={{24,0},{0,8},{8,16},{16,24},{25,1},{1,9},{9,17},{17,25},{26,2},{2,... | collective-permute-start | bytes 663560 | tf_op jit(solution)/shard_map/ppermute | solution.py:233
  25.2 1.8 %collective-permute-start.8 = (bf16[2,3,144,128]{3,2,1,0:T(8,128)(2,1)S(1)}, bf16[2,3,144,128]{3,2,1,0:T(8,128)(2,1)S(1)}, u32[]{:S(2)}, u32[]{:S(2)}) collective-permute-start(bf16[2,3,144,128]{3,2,1,0:T(8,128)(2,1)S(1)} %collective-permute-done.kv_a.refs_5_), channel_id=1, source_target_pairs={{8,0},{16,8},{24,16},{0,24},{9,1},{17,9},{25,17},{1,25},{10,2},{18... | collective-permute-start | bytes 663560 | tf_op jit(solution)/shard_map/ppermute | solution.py:233
  27.2 2.7 %shard_map.101 = (f32[16,576]{1,0:T(8,128)S(1)}, bf16[3,576,128]{2,1,0:T(8,128)(2,1)S(1)}, bf16[3,576,128]{2,1,0:T(8,128)(2,1)S(1)}, bf16[3,576,128]{2,1,0:T(8,128)(2,1)S(1)}, bf16[3,576,128]{2,1,0:T(8,128)(2,1)S(1)}) custom-call(bf16[2,3,144,128]{3,2,1,0:T(8,128)(2,1)S(1)} %pad_maximum_fusion.q0.refs_6_.raw, ...), custom_call_target="tpu_custom_call" | custom-call | flops 509607936 | bytes 1771520 | tf_op jit(solution)/shard_map/pallas_call | solution.py:221
  29.9 1.6 %collective-permute-done.7.kv_b.refs_5_ = bf16[2,3,144,128]{3,2,1,0:T(8,128)(2,1)S(1)} collective-permute-done((bf16[2,3,144,128]{3,2,1,0:T(8,128)(2,1)S(1)}, bf16[2,3,144,128]{3,2,1,0:T(8,128)(2,1)S(1)}, u32[]{:S(2)}, u32[]{:S(2)}) %collective-permute-start.7) | collective-permute-done | bytes 221216 | tf_op jit(solution)/shard_map/ppermute | solution.py:233
  31.6 1.2 %shard_map.102 = (f32[16,576]{1,0:T(8,128)S(1)}, bf16[3,288,128]{2,1,0:T(8,128)(2,1)S(1)}, bf16[3,288,128]{2,1,0:T(8,128)(2,1)S(1)}) custom-call(f32[16,576]{1,0:T(8,128)S(1)} %get-tuple-element.57.before_ref, bf16[3,576,128]{2,1,0:T(8,128)(2,1)S(1)} %get-tuple-element.58.qn_ref.refs_6_.refs_10_, ...), custom_call_target="tpu_custom_call" | custom-call | flops 254803968 | bytes 1364992 | tf_op jit(solution)/shard_map/pallas_call | solution.py:221
  32.8 1.7 %collective-permute-done.9.kv_b.refs_5_ = bf16[2,3,144,128]{3,2,1,0:T(8,128)(2,1)S(1)} collective-permute-done((bf16[2,3,144,128]{3,2,1,0:T(8,128)(2,1)S(1)}, bf16[2,3,144,128]{3,2,1,0:T(8,128)(2,1)S(1)}, u32[]{:S(2)}, u32[]{:S(2)}) %collective-permute-start.9) | collective-permute-done | bytes 221216 | tf_op jit(solution)/shard_map/ppermute | solution.py:233
  36.8 2.4 %collective-permute-start.11 = (f32[16,576]{1,0:T(8,128)S(1)}, f32[16,576]{1,0:T(8,128)S(1)}, u32[]{:S(2)}, u32[]{:S(2)}) collective-permute-start(f32[16,576]{1,0:T(8,128)S(1)} %get-tuple-element.62.refs_0_), channel_id=1, source_target_pairs={{0,64},{32,96},{64,0},{96,32},{1,65},{33,97},{65,1},{97,33},{2,66}... | collective-permute-start | bytes 110600 | tf_op jit(solution)/shard_map/ppermute | solution.py:237
  39.3 2.0 %collective-permute-done.12.refs_3_ = f32[16,576]{1,0:T(8,128)S(1)} collective-permute-done((f32[16,576]{1,0:T(8,128)S(1)}, f32[16,576]{1,0:T(8,128)S(1)}, u32[]{:S(2)}, u32[]{:S(2)}) %collective-permute-start.12) | collective-permute-done | bytes 36896 | tf_op jit(solution)/shard_map/ppermute | solution.py:237
  42.0 1.2 %collective-permute-done.10.refs_1_ = f32[16,576]{1,0:T(8,128)S(1)} collective-permute-done((f32[16,576]{1,0:T(8,128)S(1)}, f32[16,576]{1,0:T(8,128)S(1)}, u32[]{:S(2)}, u32[]{:S(2)}) %collective-permute-start.10) | collective-permute-done | bytes 36896 | tf_op jit(solution)/shard_map/ppermute | solution.py:237
  43.2 2.1 %shard_map.104 = (bf16[2,2,3,144,128]{4,3,2,1,0:T(8,128)(2,1)S(1)}, f32[3,576,128]{2,1,0:T(8,128)S(1)}, f32[8,128]{1,0:T(8,128)S(1)}) custom-call(f32[16,576]{1,0:T(8,128)S(1)} %get-tuple-element.62.refs_0_, f32[16,576]{1,0:T(8,128)S(1)} %collective-permute-done.10.refs_1_, f32[16,576]{1,0:T(8,128)S(1)} %collective-permute-done.11.refs_2_, ...), custom_call_target="tpu_custom_call" | custom-call | flops 764411904 | bytes 2801664 | tf_op jit(solution)/shard_map/pallas_call | solution.py:221
  45.3 2.9 %collective-permute-start.16 = (bf16[2,2,3,144,128]{4,3,2,1,0:T(8,128)(2,1)S(1)}, bf16[2,2,3,144,128]{4,3,2,1,0:T(8,128)(2,1)S(1)}, u32[]{:S(2)}, u32[]{:S(2)}) collective-permute-start(bf16[2,2,3,144,128]{4,3,2,1,0:T(8,128)(2,1)S(1)} %get-tuple-element.80), channel_id=1, source_target_pairs={{0,16},{8,24},{16,0},{24,8},{1,17},{9,25},{17,1},{25,9},{2,18},{10... | collective-permute-start | bytes 1327112 | tf_op jit(solution)/shard_map/ppermute | solution.py:241
  48.2 2.1 %shard_map.105 = (bf16[2,2,3,144,128]{4,3,2,1,0:T(8,128)(2,1)S(1)}, f32[3,576,128]{2,1,0:T(8,128)S(1)}, f32[8,128]{1,0:T(8,128)S(1)}) custom-call(f32[16,576]{1,0:T(8,128)S(1)} %get-tuple-element.62.refs_0_, f32[16,576]{1,0:T(8,128)S(1)} %collective-permute-done.10.refs_1_, f32[16,576]{1,0:T(8,128)S(1)} %collective-permute-done.11.refs_2_, ...), custom_call_target="tpu_custom_call" | custom-call | flops 764411904 | bytes 3690496 | tf_op jit(solution)/shard_map/pallas_call | solution.py:221
  50.4 2.1 %shard_map.106 = (bf16[2,2,3,144,128]{4,3,2,1,0:T(8,128)(2,1)S(1)}, f32[3,576,128]{2,1,0:T(8,128)S(1)}, f32[8,128]{1,0:T(8,128)S(1)}) custom-call(f32[16,576]{1,0:T(8,128)S(1)} %get-tuple-element.62.refs_0_, f32[16,576]{1,0:T(8,128)S(1)} %collective-permute-done.10.refs_1_, f32[16,576]{1,0:T(8,128)S(1)} %collective-permute-done.11.refs_2_, ...), custom_call_target="tpu_custom_call" | custom-call | flops 764411904 | bytes 3690496 | tf_op jit(solution)/shard_map/pallas_call | solution.py:221
  52.5 2.1 %collective-permute-start.18 = (bf16[2,2,3,144,128]{4,3,2,1,0:T(8,128)(2,1)S(1)}, bf16[2,2,3,144,128]{4,3,2,1,0:T(8,128)(2,1)S(1)}, u32[]{:S(2)}, u32[]{:S(2)}) collective-permute-start(bf16[2,2,3,144,128]{4,3,2,1,0:T(8,128)(2,1)S(1)} %get-tuple-element.82), channel_id=1, source_target_pairs={{0,24},{8,0},{16,8},{24,16},{1,25},{9,1},{17,9},{25,17},{2,26},{10... | collective-permute-start | bytes 1327112 | tf_op jit(solution)/shard_map/ppermute | solution.py:241
  54.6 2.7 %shard_map.107 = (f32[2,2,3,144,128]{4,3,2,1,0:T(8,128)S(1)}, f32[3,144,128]{2,1,0:T(8,128)S(1)}, bf16[3,144,128]{2,1,0:T(8,128)(2,1)S(1)}, bf16[3,144,128]{2,1,...) custom-call(f32[16,576]{1,0:T(8,128)S(1)} %get-tuple-element.62.refs_0_, ...), custom_call_target="tpu_custom_call" | custom-call | flops 764411904 | bytes 4575232 | tf_op jit(solution)/shard_map/pallas_call | solution.py:221
  58.3 2.8 %collective-permute-done.20 = f32[8,128]{1,0:T(8,128)S(1)} collective-permute-done((f32[8,128]{1,0:T(8,128)S(1)}, f32[8,128]{1,0:T(8,128)S(1)}, u32[]{:S(2)}, u32[]{:S(2)}) %collective-permute-start.20) | collective-permute-done | bytes 4128 | tf_op jit(solution)/shard_map/ppermute | solution.py:237
  61.0 1.3 %collective-permute-start.21 = (f32[8,128]{1,0:T(8,128)S(1)}, f32[8,128]{1,0:T(8,128)S(1)}, u32[]{:S(2)}, u32[]{:S(2)}) collective-permute-start(f32[8,128]{1,0:T(8,128)S(1)} %add.39), channel_id=1, source_target_pairs={{0,64},{32,96},{64,0},{96,32},{1,65},{33,97},{65,1},{97,33},{2,66}... | collective-permute-start | bytes 12296 | tf_op jit(solution)/shard_map/ppermute | solution.py:237
  62.3 3.2 %collective-permute-done.21 = f32[8,128]{1,0:T(8,128)S(1)} collective-permute-done((f32[8,128]{1,0:T(8,128)S(1)}, f32[8,128]{1,0:T(8,128)S(1)}, u32[]{:S(2)}, u32[]{:S(2)}) %collective-permute-start.21) | collective-permute-done | bytes 4128 | tf_op jit(solution)/shard_map/ppermute | solution.py:237
  66.7 1.3 %collective-permute-start.23 = (f32[8,128]{1,0:T(8,128)S(1)}, f32[8,128]{1,0:T(8,128)S(1)}, u32[]{:S(2)}, u32[]{:S(2)}) collective-permute-start(f32[8,128]{1,0:T(8,128)S(1)} %add.41), channel_id=1, source_target_pairs={{0,224},{32,192},{64,160},{96,128},{128,96},{160,64},{192,32},{224... | collective-permute-start | bytes 12296 | tf_op jit(solution)/shard_map/ppermute | solution.py:246
  68.5 5.2 %collective-permute-done.23 = f32[8,128]{1,0:T(8,128)S(1)} collective-permute-done((f32[8,128]{1,0:T(8,128)S(1)}, f32[8,128]{1,0:T(8,128)S(1)}, u32[]{:S(2)}, u32[]{:S(2)}) %collective-permute-start.23) | collective-permute-done | bytes 4128 | tf_op jit(solution)/shard_map/ppermute | solution.py:246
  74.8 3.0 %collective-permute-start.26 = (f32[8,128]{1,0:T(8,128)S(1)}, f32[8,128]{1,0:T(8,128)S(1)}, u32[]{:S(2)}, u32[]{:S(2)}) collective-permute-start(f32[8,128]{1,0:T(8,128)S(1)} %add.42), channel_id=1, source_target_pairs={{0,6},{2,4},{4,2},{6,0},{1,7},{3,5},{5,3},{7,1},{8,14},{10,12},{12... | collective-permute-start | bytes 12296 | tf_op jit(solution)/shard_map/ppermute | solution.py:237
  79.1 3.0 %collective-permute-start.19 = (bf16[2,3,144,128]{3,2,1,0:T(8,128)(2,1)S(1)}, bf16[2,3,144,128]{3,2,1,0:T(8,128)(2,1)S(1)}, u32[]{:S(2)}, u32[]{:S(2)}) collective-permute-start(bf16[2,3,144,128]{3,2,1,0:T(8,128)(2,1)S(1)} %get-tuple-element.84), channel_id=1, source_target_pairs={{0,224},{32,192},{64,160},{96,128},{128,96},{160,64},{192,32},{224... | collective-permute-start | bytes 663560 | tf_op jit(solution)/shard_map/ppermute | solution.py:246
  82.9 3.3 %collective-permute-start.29 = (f32[8,128]{1,0:T(8,128)S(1)}, f32[8,128]{1,0:T(8,128)S(1)}, u32[]{:S(2)}, u32[]{:S(2)}) collective-permute-start(f32[8,128]{1,0:T(8,128)S(1)} %add_add_fusion), channel_id=1, source_target_pairs={{0,24},{8,16},{16,8},{24,0},{1,25},{9,17},{17,9},{25,1},{2,26},{10... | collective-permute-start | bytes 12296 | tf_op jit(solution)/shard_map/ppermute | solution.py:237
  89.1 2.3 %collective-permute-done.28 = f32[8,128]{1,0:T(8,128)S(1)} collective-permute-done((f32[8,128]{1,0:T(8,128)S(1)}, f32[8,128]{1,0:T(8,128)S(1)}, u32[]{:S(2)}, u32[]{:S(2)}) %collective-permute-start.28) | collective-permute-done | bytes 4128 | tf_op jit(solution)/shard_map/ppermute | solution.py:237
  (54 shorter events, 14.5 us)
Async XLA Ops:
  1.7 13.3 %collective-permute-start.2 = (bf16[2,3,144,128]{3,2,1,0:T(8,128)(2,1)S(1)}, bf16[2,3,144,128]{3,2,1,0:T(8,128)(2,1)S(1)}, u32[]{:S(2)}, u32[]{:S(2)}) collective-permute-start(bf16[2,3,144,128]{3,2,1,0:T(8,128)(2,1)S(1)} %pad_maximum_fusion.q0.refs_6_.raw), channel_id=1, source_target_pairs={{0,96},{32,64},{64,32},{96,0},{1,97},{33,65},{65,33},{97,1},{2,98}... | collective-permute-start | bytes 663560 | tf_op jit(solution)/shard_map/ppermute | solution.py:237
  3.7 23.6 %copy-start = (f32[2,128]{1,0:T(2,128)S(1)}, f32[2,128]{1,0:T(2,128)}, u32[]{:S(2)}) copy-start(f32[2,128]{1,0:T(2,128)} %gain_ref.3) | copy-start | bytes 3076
  3.7 23.6 %copy-start.1 = (f32[2,128]{1,0:T(2,128)S(1)}, f32[2,128]{1,0:T(2,128)}, u32[]{:S(2)}) copy-start(f32[2,128]{1,0:T(2,128)} %gain_ref.2) | copy-start | bytes 3076
  3.7 15.1 %collective-permute-start = (bf16[2,3,144,128]{3,2,1,0:T(8,128)(2,1)S(1)}, bf16[2,3,144,128]{3,2,1,0:T(8,128)(2,1)S(1)}, u32[]{:S(2)}, u32[]{:S(2)}) collective-permute-start(bf16[2,3,144,128]{3,2,1,0:T(8,128)(2,1)S(1)} %pad_maximum_fusion.1.kv0.refs_4_.raw), channel_id=1, source_target_pairs={{0,224},{32,192},{64,160},{96,128},{128,96},{160,64},{192,32},{224... | collective-permute-start | bytes 663560 | tf_op jit(solution)/shard_map/ppermute | solution.py:246
  8.7 10.2 %collective-permute-start.6 = (bf16[2,3,144,128]{3,2,1,0:T(8,128)(2,1)S(1)}, bf16[2,3,144,128]{3,2,1,0:T(8,128)(2,1)S(1)}, u32[]{:S(2)}, u32[]{:S(2)}) collective-permute-start(bf16[2,3,144,128]{3,2,1,0:T(8,128)(2,1)S(1)} %pad_maximum_fusion.1.kv0.refs_4_.raw), channel_id=1, source_target_pairs={{16,0},{24,8},{0,16},{8,24},{17,1},{25,9},{1,17},{9,25},{18,2},{26... | collective-permute-start | bytes 663560 | tf_op jit(solution)/shard_map/ppermute | solution.py:233
  11.8 9.8 %collective-permute-start.5 = (bf16[2,3,144,128]{3,2,1,0:T(8,128)(2,1)S(1)}, bf16[2,3,144,128]{3,2,1,0:T(8,128)(2,1)S(1)}, u32[]{:S(2)}, u32[]{:S(2)}) collective-permute-start(bf16[2,3,144,128]{3,2,1,0:T(8,128)(2,1)S(1)} %pad_maximum_fusion.1.kv0.refs_4_.raw), channel_id=1, source_target_pairs={{24,0},{0,8},{8,16},{16,24},{25,1},{1,9},{9,17},{17,25},{26,2},{2,... | collective-permute-start | bytes 663560 | tf_op jit(solution)/shard_map/ppermute | solution.py:233
  12.4 9.3 %collective-permute-start.4 = (bf16[2,3,144,128]{3,2,1,0:T(8,128)(2,1)S(1)}, bf16[2,3,144,128]{3,2,1,0:T(8,128)(2,1)S(1)}, u32[]{:S(2)}, u32[]{:S(2)}) collective-permute-start(bf16[2,3,144,128]{3,2,1,0:T(8,128)(2,1)S(1)} %pad_maximum_fusion.1.kv0.refs_4_.raw), channel_id=1, source_target_pairs={{8,0},{16,8},{24,16},{0,24},{9,1},{17,9},{25,17},{1,25},{10,2},{18... | collective-permute-start | bytes 663560 | tf_op jit(solution)/shard_map/ppermute | solution.py:233
  15.0 12.0 %collective-permute-start.3 = (bf16[2,3,144,128]{3,2,1,0:T(8,128)(2,1)S(1)}, bf16[2,3,144,128]{3,2,1,0:T(8,128)(2,1)S(1)}, u32[]{:S(2)}, u32[]{:S(2)}) collective-permute-start(bf16[2,3,144,128]{3,2,1,0:T(8,128)(2,1)S(1)} %pad_maximum_fusion.q0.refs_6_.raw), channel_id=1, source_target_pairs={{0,64},{32,96},{64,0},{96,32},{1,65},{33,97},{65,1},{97,33},{2,66}... | collective-permute-start | bytes 663560 | tf_op jit(solution)/shard_map/ppermute | solution.py:237
  18.8 8.5 %collective-permute-start.1 = (bf16[2,3,144,128]{3,2,1,0:T(8,128)(2,1)S(1)}, bf16[2,3,144,128]{3,2,1,0:T(8,128)(2,1)S(1)}, u32[]{:S(2)}, u32[]{:S(2)}) collective-permute-start(bf16[2,3,144,128]{3,2,1,0:T(8,128)(2,1)S(1)} %pad_maximum_fusion.q0.refs_6_.raw), channel_id=1, source_target_pairs={{0,32},{32,0},{64,96},{96,64},{1,33},{33,1},{65,97},{97,65},{2,34}... | collective-permute-start | bytes 663560 | tf_op jit(solution)/shard_map/ppermute | solution.py:237
  21.7 9.9 %collective-permute-start.7 = (bf16[2,3,144,128]{3,2,1,0:T(8,128)(2,1)S(1)}, bf16[2,3,144,128]{3,2,1,0:T(8,128)(2,1)S(1)}, u32[]{:S(2)}, u32[]{:S(2)}) collective-permute-start(bf16[2,3,144,128]{3,2,1,0:T(8,128)(2,1)S(1)} %collective-permute-done.kv_a.refs_5_), channel_id=1, source_target_pairs={{16,0},{24,8},{0,16},{8,24},{17,1},{25,9},{1,17},{9,25},{18,2},{26... | collective-permute-start | bytes 663560 | tf_op jit(solution)/shard_map/ppermute | solution.py:233
  23.8 10.7 %collective-permute-start.9 = (bf16[2,3,144,128]{3,2,1,0:T(8,128)(2,1)S(1)}, bf16[2,3,144,128]{3,2,1,0:T(8,128)(2,1)S(1)}, u32[]{:S(2)}, u32[]{:S(2)}) collective-permute-start(bf16[2,3,144,128]{3,2,1,0:T(8,128)(2,1)S(1)} %collective-permute-done.kv_a.refs_5_), channel_id=1, source_target_pairs={{24,0},{0,8},{8,16},{16,24},{25,1},{1,9},{9,17},{17,25},{26,2},{2,... | collective-permute-start | bytes 663560 | tf_op jit(solution)/shard_map/ppermute | solution.py:233
  25.2 9.3 %collective-permute-start.8 = (bf16[2,3,144,128]{3,2,1,0:T(8,128)(2,1)S(1)}, bf16[2,3,144,128]{3,2,1,0:T(8,128)(2,1)S(1)}, u32[]{:S(2)}, u32[]{:S(2)}) collective-permute-start(bf16[2,3,144,128]{3,2,1,0:T(8,128)(2,1)S(1)} %collective-permute-done.kv_a.refs_5_), channel_id=1, source_target_pairs={{8,0},{16,8},{24,16},{0,24},{9,1},{17,9},{25,17},{1,25},{10,2},{18... | collective-permute-start | bytes 663560 | tf_op jit(solution)/shard_map/ppermute | solution.py:233
  35.7 5.5 %collective-permute-start.12 = (f32[16,576]{1,0:T(8,128)S(1)}, f32[16,576]{1,0:T(8,128)S(1)}, u32[]{:S(2)}, u32[]{:S(2)}) collective-permute-start(f32[16,576]{1,0:T(8,128)S(1)} %get-tuple-element.62.refs_0_), channel_id=1, source_target_pairs={{0,96},{32,64},{64,32},{96,0},{1,97},{33,65},{65,33},{97,1},{2,98}... | collective-permute-start | bytes 110600 | tf_op jit(solution)/shard_map/ppermute | solution.py:237
  36.8 5.1 %collective-permute-start.11 = (f32[16,576]{1,0:T(8,128)S(1)}, f32[16,576]{1,0:T(8,128)S(1)}, u32[]{:S(2)}, u32[]{:S(2)}) collective-permute-start(f32[16,576]{1,0:T(8,128)S(1)} %get-tuple-element.62.refs_0_), channel_id=1, source_target_pairs={{0,64},{32,96},{64,0},{96,32},{1,65},{33,97},{65,1},{97,33},{2,66}... | collective-permute-start | bytes 110600 | tf_op jit(solution)/shard_map/ppermute | solution.py:237
  39.2 4.0 %collective-permute-start.10 = (f32[16,576]{1,0:T(8,128)S(1)}, f32[16,576]{1,0:T(8,128)S(1)}, u32[]{:S(2)}, u32[]{:S(2)}) collective-permute-start(f32[16,576]{1,0:T(8,128)S(1)} %get-tuple-element.62.refs_0_), channel_id=1, source_target_pairs={{0,32},{32,0},{64,96},{96,64},{1,33},{33,1},{65,97},{97,65},{2,34}... | collective-permute-start | bytes 110600 | tf_op jit(solution)/shard_map/ppermute | solution.py:237
  45.3 20.2 %collective-permute-start.16 = (bf16[2,2,3,144,128]{4,3,2,1,0:T(8,128)(2,1)S(1)}, bf16[2,2,3,144,128]{4,3,2,1,0:T(8,128)(2,1)S(1)}, u32[]{:S(2)}, u32[]{:S(2)}) collective-permute-start(bf16[2,2,3,144,128]{4,3,2,1,0:T(8,128)(2,1)S(1)} %get-tuple-element.80), channel_id=1, source_target_pairs={{0,16},{8,24},{16,0},{24,8},{1,17},{9,25},{17,1},{25,9},{2,18},{10... | collective-permute-start | bytes 1327112 | tf_op jit(solution)/shard_map/ppermute | solution.py:241
  52.5 25.3 %collective-permute-start.18 = (bf16[2,2,3,144,128]{4,3,2,1,0:T(8,128)(2,1)S(1)}, bf16[2,2,3,144,128]{4,3,2,1,0:T(8,128)(2,1)S(1)}, u32[]{:S(2)}, u32[]{:S(2)}) collective-permute-start(bf16[2,2,3,144,128]{4,3,2,1,0:T(8,128)(2,1)S(1)} %get-tuple-element.82), channel_id=1, source_target_pairs={{0,24},{8,0},{16,8},{24,16},{1,25},{9,1},{17,9},{25,17},{2,26},{10... | collective-permute-start | bytes 1327112 | tf_op jit(solution)/shard_map/ppermute | solution.py:241
  54.6 23.8 %collective-permute-start.17 = (bf16[2,2,3,144,128]{4,3,2,1,0:T(8,128)(2,1)S(1)}, bf16[2,2,3,144,128]{4,3,2,1,0:T(8,128)(2,1)S(1)}, u32[]{:S(2)}, u32[]{:S(2)}) collective-permute-start(bf16[2,2,3,144,128]{4,3,2,1,0:T(8,128)(2,1)S(1)} %get-tuple-element.81), channel_id=1, source_target_pairs={{0,8},{8,16},{16,24},{24,0},{1,9},{9,17},{17,25},{25,1},{2,10},{10... | collective-permute-start | bytes 1327112 | tf_op jit(solution)/shard_map/ppermute | solution.py:241
  57.3 3.7 %collective-permute-start.20 = (f32[8,128]{1,0:T(8,128)S(1)}, f32[8,128]{1,0:T(8,128)S(1)}, u32[]{:S(2)}, u32[]{:S(2)}) collective-permute-start(f32[8,128]{1,0:T(8,128)S(1)} %get-tuple-element.87), channel_id=1, source_target_pairs={{0,32},{32,0},{64,96},{96,64},{1,33},{33,1},{65,97},{97,65},{2,34}... | collective-permute-start | bytes 12296 | tf_op jit(solution)/shard_map/ppermute | solution.py:237
  61.0 4.5 %collective-permute-start.21 = (f32[8,128]{1,0:T(8,128)S(1)}, f32[8,128]{1,0:T(8,128)S(1)}, u32[]{:S(2)}, u32[]{:S(2)}) collective-permute-start(f32[8,128]{1,0:T(8,128)S(1)} %add.39), channel_id=1, source_target_pairs={{0,64},{32,96},{64,0},{96,32},{1,65},{33,97},{65,1},{97,33},{2,66}... | collective-permute-start | bytes 12296 | tf_op jit(solution)/shard_map/ppermute | solution.py:237
  65.5 1.2 %collective-permute-start.22 = (f32[8,128]{1,0:T(8,128)S(1)}, f32[8,128]{1,0:T(8,128)S(1)}, u32[]{:S(2)}, u32[]{:S(2)}) collective-permute-start(f32[8,128]{1,0:T(8,128)S(1)} %add.40), channel_id=1, source_target_pairs={{0,1},{1,0},{2,3},{3,2},{4,5},{5,4},{6,7},{7,6},{8,9},{9,8},{10,11... | collective-permute-start | bytes 12296 | tf_op jit(solution)/shard_map/ppermute | solution.py:237
  65.5 9.2 %collective-permute-start.13 = (bf16[3,144,128]{2,1,0:T(8,128)(2,1)S(1)}, bf16[3,144,128]{2,1,0:T(8,128)(2,1)S(1)}, u32[]{:S(2)}, u32[]{:S(2)}) collective-permute-start(bf16[3,144,128]{2,1,0:T(8,128)(2,1)S(1)} %get-tuple-element.76), channel_id=1, source_target_pairs={{0,32},{32,0},{64,96},{96,64},{1,33},{33,1},{65,97},{97,65},{2,34}... | collective-permute-start | bytes 331784 | tf_op jit(solution)/shard_map/ppermute | solution.py:237
  66.7 7.0 %collective-permute-start.23 = (f32[8,128]{1,0:T(8,128)S(1)}, f32[8,128]{1,0:T(8,128)S(1)}, u32[]{:S(2)}, u32[]{:S(2)}) collective-permute-start(f32[8,128]{1,0:T(8,128)S(1)} %add.41), channel_id=1, source_target_pairs={{0,224},{32,192},{64,160},{96,128},{128,96},{160,64},{192,32},{224... | collective-permute-start | bytes 12296 | tf_op jit(solution)/shard_map/ppermute | solution.py:246
  68.0 11.1 %collective-permute-start.14 = (bf16[3,144,128]{2,1,0:T(8,128)(2,1)S(1)}, bf16[3,144,128]{2,1,0:T(8,128)(2,1)S(1)}, u32[]{:S(2)}, u32[]{:S(2)}) collective-permute-start(bf16[3,144,128]{2,1,0:T(8,128)(2,1)S(1)} %get-tuple-element.77), channel_id=1, source_target_pairs={{0,64},{32,96},{64,0},{96,32},{1,65},{33,97},{65,1},{97,33},{2,66}... | collective-permute-start | bytes 331784 | tf_op jit(solution)/shard_map/ppermute | solution.py:237
  73.7 8.3 %collective-permute-start.15 = (bf16[3,144,128]{2,1,0:T(8,128)(2,1)S(1)}, bf16[3,144,128]{2,1,0:T(8,128)(2,1)S(1)}, u32[]{:S(2)}, u32[]{:S(2)}) collective-permute-start(bf16[3,144,128]{2,1,0:T(8,128)(2,1)S(1)} %get-tuple-element.78), channel_id=1, source_target_pairs={{0,96},{32,64},{64,32},{96,0},{1,97},{33,65},{65,33},{97,1},{2,98}... | collective-permute-start | bytes 331784 | tf_op jit(solution)/shard_map/ppermute | solution.py:237
  74.8 7.3 %collective-permute-start.26 = (f32[8,128]{1,0:T(8,128)S(1)}, f32[8,128]{1,0:T(8,128)S(1)}, u32[]{:S(2)}, u32[]{:S(2)}) collective-permute-start(f32[8,128]{1,0:T(8,128)S(1)} %add.42), channel_id=1, source_target_pairs={{0,6},{2,4},{4,2},{6,0},{1,7},{3,5},{5,3},{7,1},{8,14},{10,12},{12... | collective-permute-start | bytes 12296 | tf_op jit(solution)/shard_map/ppermute | solution.py:237
  77.8 5.1 %collective-permute-start.25 = (f32[8,128]{1,0:T(8,128)S(1)}, f32[8,128]{1,0:T(8,128)S(1)}, u32[]{:S(2)}, u32[]{:S(2)}) collective-permute-start(f32[8,128]{1,0:T(8,128)S(1)} %add.42), channel_id=1, source_target_pairs={{0,4},{2,6},{4,0},{6,2},{1,5},{3,7},{5,1},{7,3},{8,12},{10,14},{12... | collective-permute-start | bytes 12296 | tf_op jit(solution)/shard_map/ppermute | solution.py:237
  78.4 4.5 %collective-permute-start.24 = (f32[8,128]{1,0:T(8,128)S(1)}, f32[8,128]{1,0:T(8,128)S(1)}, u32[]{:S(2)}, u32[]{:S(2)}) collective-permute-start(f32[8,128]{1,0:T(8,128)S(1)} %add.42), channel_id=1, source_target_pairs={{0,2},{2,0},{4,6},{6,4},{1,3},{3,1},{5,7},{7,5},{8,10},{10,8},{12,... | collective-permute-start | bytes 12296 | tf_op jit(solution)/shard_map/ppermute | solution.py:237
  79.1 9.1 %collective-permute-start.19 = (bf16[2,3,144,128]{3,2,1,0:T(8,128)(2,1)S(1)}, bf16[2,3,144,128]{3,2,1,0:T(8,128)(2,1)S(1)}, u32[]{:S(2)}, u32[]{:S(2)}) collective-permute-start(bf16[2,3,144,128]{3,2,1,0:T(8,128)(2,1)S(1)} %get-tuple-element.84), channel_id=1, source_target_pairs={{0,224},{32,192},{64,160},{96,128},{128,96},{160,64},{192,32},{224... | collective-permute-start | bytes 663560 | tf_op jit(solution)/shard_map/ppermute | solution.py:246
  82.9 6.2 %collective-permute-start.29 = (f32[8,128]{1,0:T(8,128)S(1)}, f32[8,128]{1,0:T(8,128)S(1)}, u32[]{:S(2)}, u32[]{:S(2)}) collective-permute-start(f32[8,128]{1,0:T(8,128)S(1)} %add_add_fusion), channel_id=1, source_target_pairs={{0,24},{8,16},{16,8},{24,0},{1,25},{9,17},{17,9},{25,1},{2,26},{10... | collective-permute-start | bytes 12296 | tf_op jit(solution)/shard_map/ppermute | solution.py:237
  86.2 5.1 %collective-permute-start.28 = (f32[8,128]{1,0:T(8,128)S(1)}, f32[8,128]{1,0:T(8,128)S(1)}, u32[]{:S(2)}, u32[]{:S(2)}) collective-permute-start(f32[8,128]{1,0:T(8,128)S(1)} %add_add_fusion), channel_id=1, source_target_pairs={{0,16},{8,24},{16,0},{24,8},{1,17},{9,25},{17,1},{25,9},{2,18},{10... | collective-permute-start | bytes 12296 | tf_op jit(solution)/shard_map/ppermute | solution.py:237
  86.2 5.1 %collective-permute-start.27 = (f32[8,128]{1,0:T(8,128)S(1)}, f32[8,128]{1,0:T(8,128)S(1)}, u32[]{:S(2)}, u32[]{:S(2)}) collective-permute-start(f32[8,128]{1,0:T(8,128)S(1)} %add_add_fusion), channel_id=1, source_target_pairs={{0,8},{8,0},{16,24},{24,16},{1,9},{9,1},{17,25},{25,17},{2,10},{10... | collective-permute-start | bytes 12296 | tf_op jit(solution)/shard_map/ppermute | solution.py:237
  (2 other events, 6.1 us)
